TPU v7x, 32 devices: a whole 2x2x4 slice. The times are simulated.
32 devices in a mesh: rep: 4 (over x, core), shard: 8 (over z, y).
Axes of the slice: x: 2, y: 2, z: 4, core: 2. Of those that a mesh axis runs over, the one named last changes fastest.
Arguments:
- tokens: bfloat16 [32768, 1024], P(('rep', 'shard')), may hold values from -6 to 6
- resets: int32 [32768], P(('rep', 'shard')), may hold values 0 or 1
- norm_gain: bfloat16 [1024], P('shard'), may hold values from 0.5 to 1.5
- in_weight: bfloat16 [1024, 4384], P('shard'), may hold values from -0.1875 to 0.1875
- conv_weight: bfloat16 [4, 2304], P(None, 'shard'), may hold values from -3 to 3
- conv_bias: bfloat16 [2304], P('shard'), may hold values from -0.5 to 0.5
- step_bias: bfloat16 [32], P('shard'), may hold values from -7 to -3
- decay_log: bfloat16 [32], P('shard'), may hold values from 0 to 2.5
- skip_gain: bfloat16 [32], P('shard'), may hold values from 0.5 to 1.5
- gate_gain: bfloat16 [2048], P('shard'), may hold values from 0.5 to 1.5
- out_weight: bfloat16 [2048, 1024], P('shard'), may hold values from -0.125 to 0.125
- cotangent: bfloat16 [32768, 1024], P(('rep', 'shard')), may hold values from -6 to 6
Outputs:
- output: bfloat16 [32768, 1024], P(('rep', 'shard'))
- input_grad: bfloat16 [32768, 1024], P(('rep', 'shard'))
- norm_gain_grad: float32 [1024], P('shard')
- in_weight_grad: float32 [1024, 4384], P('shard')
- conv_weight_grad: float32 [4, 2304], P(None, 'shard')
- conv_bias_grad: float32 [2304], P('shard')
- step_bias_grad: float32 [32], P('shard')
- decay_log_grad: float32 [32], P('shard')
- skip_gain_grad: float32 [32], P('shard')
- gate_gain_grad: float32 [2048], P('shard')
- out_weight_grad: float32 [2048, 1024], P('shard')
Inputs may be any that keep to these rules, and one draw needn't show every extreme that they name: resets[t] = 1 starts a new document at position t of its sequence.
All inputs are finite; a program needn't handle non-finite values. No bound on the sum of `resets` on one device may be relied on, other than what follows from the above.
Results may differ from a plain program's by a relative error of at most 0.0082.
Values may be sent and summed in bfloat16 or wider, within the bound.
No kernel may reach another device: no remote copies, remote signals or barrier semaphores. Data moves between devices by JAX's collectives and lax.ppermute only.
A program may use at most 256 MiB of HBM per device.

v0:
```python
from functools import partial

import jax
import jax.numpy as jnp
from jax import lax
from jax.sharding import PartitionSpec as P

SPAN = 256


EPS = 1e-05


def causal_conv(inputs, segment, conv_weight, conv_bias):
    taps = conv_weight.shape[0]
    length = inputs.shape[0]
    total = conv_bias[None, :] + jnp.zeros_like(inputs)
    for offset in range(taps):
        behind = taps - 1 - offset
        moved = jnp.pad(inputs, ((behind, 0), (0, 0)))[:length]
        moved_seg = jnp.pad(segment, (behind, 0), constant_values=-1)[:length]
        same_doc = (moved_seg == segment).astype(jnp.float32)
        total = total + conv_weight[offset][None, :] * moved * same_doc[:, None]
    return total


def span_scan(x_all, b_all, c_all, rate_all, step_all, segment):
    length, head_count, head_width = x_all.shape
    block_count = length // SPAN
    state_width = b_all.shape[1]
    x_blocks = x_all.reshape(block_count, SPAN, head_count, head_width)
    b_blocks = b_all.reshape(block_count, SPAN, state_width)
    c_blocks = c_all.reshape(block_count, SPAN, state_width)
    rate_heads = jnp.swapaxes(rate_all.reshape(block_count, SPAN, head_count), 1, 2)
    step_heads = jnp.swapaxes(step_all.reshape(block_count, SPAN, head_count), 1, 2)
    seg_blocks = segment.reshape(block_count, SPAN)
    cumulative = jnp.cumsum(rate_heads, axis=2)
    row_index = lax.broadcasted_iota(jnp.int32, (SPAN, SPAN), 0)
    col_index = lax.broadcasted_iota(jnp.int32, (SPAN, SPAN), 1)
    linked = (
        (row_index >= col_index)[None, :, :] & (seg_blocks[:, :, None] == seg_blocks[:, None, :])
    )[:, None, :, :]
    spread = cumulative[:, :, :, None] - cumulative[:, :, None, :]
    decay_mask = jnp.where(linked, jnp.exp(jnp.where(linked, spread, 0.0)), 0.0)
    intersection = jnp.einsum("btn,bsn->bts", c_blocks, b_blocks, precision=lax.Precision.HIGHEST)
    weights = intersection[:, None, :, :] * decay_mask * step_heads[:, :, None, :]
    inside = jnp.einsum("bhts,bshp->bthp", weights, x_blocks, precision=lax.Precision.HIGHEST)
    last_segs = seg_blocks[:, -1]
    prev_last = jnp.concatenate([jnp.full((1,), -1, jnp.int32), last_segs[:-1]])
    carried = (seg_blocks == prev_last[:, None]).astype(jnp.float32)
    entry_scale = jnp.exp(cumulative) * carried[:, None, :]
    closing = (seg_blocks == last_segs[:, None]).astype(jnp.float32)
    to_end = jnp.exp(cumulative[:, :, -1:] - cumulative) * closing[:, None, :] * step_heads
    keep_all = jnp.exp(cumulative[:, :, -1]) * (last_segs == prev_last).astype(jnp.float32)[:, None]
    weighted_x = x_blocks * jnp.swapaxes(to_end, 1, 2)[:, :, :, None]
    added = jnp.einsum("bshp,bsn->bhpn", weighted_x, b_blocks, precision=lax.Precision.HIGHEST)
    state = jnp.zeros((head_count, head_width, state_width), jnp.float32)
    entering = []
    for block in range(block_count):
        entering.append(state)
        state = state * keep_all[block][:, None, None] + added[block]
    entering = jnp.stack(entering)
    from_state = jnp.einsum("btn,bhpn->bthp", c_blocks, entering, precision=lax.Precision.HIGHEST)
    from_state = from_state * jnp.swapaxes(entry_scale, 1, 2)[:, :, :, None]
    return (inside + from_state).reshape(length, head_count, head_width)


def mixer(projected, conv_weight, conv_bias, step_bias, decay_log, skip_gain, gate_gain, segment):
    inner_width = gate_gain.shape[0]
    mixed_width = conv_bias.shape[0]
    state_width = (mixed_width - inner_width) // 2
    head_count = step_bias.shape[0]
    length = projected.shape[0]
    gate_part = projected[:, :inner_width]
    conv_in = projected[:, inner_width : inner_width + mixed_width]
    step_raw = projected[:, inner_width + mixed_width :]
    convolved = jax.nn.silu(causal_conv(conv_in, segment, conv_weight, conv_bias))
    values_x = convolved[:, :inner_width].reshape(length, head_count, inner_width // head_count)
    input_b = convolved[:, inner_width : inner_width + state_width]
    output_c = convolved[:, inner_width + state_width :]
    step_size = jax.nn.softplus(step_raw + step_bias[None, :])
    rates = -jnp.exp(decay_log)[None, :] * step_size
    scanned = span_scan(values_x, input_b, output_c, rates, step_size, segment)
    scanned = scanned + skip_gain[None, :, None] * values_x
    gated = scanned.reshape(length, inner_width) * jax.nn.silu(gate_part)
    return (
        gated
        * lax.rsqrt(jnp.mean(gated * gated, axis=-1, keepdims=True) + EPS)
        * gate_gain[None, :]
    )


def on_device(
    tokens,
    resets,
    norm_gain,
    in_weight,
    conv_weight,
    conv_bias,
    step_bias,
    decay_log,
    skip_gain,
    gate_gain,
    out_weight,
    cotangent,
):
    gathered = (
        lax.all_gather(norm_gain, "shard", axis=0, tiled=True),
        lax.all_gather(in_weight, "shard", axis=0, tiled=True),
        lax.all_gather(conv_weight, "shard", axis=1, tiled=True),
        lax.all_gather(conv_bias, "shard", axis=0, tiled=True),
        lax.all_gather(step_bias, "shard", axis=0, tiled=True),
        lax.all_gather(decay_log, "shard", axis=0, tiled=True),
        lax.all_gather(skip_gain, "shard", axis=0, tiled=True),
        lax.all_gather(gate_gain, "shard", axis=0, tiled=True),
        lax.all_gather(out_weight, "shard", axis=0, tiled=True),
    )
    (
        full_norm,
        full_in,
        full_conv,
        full_bias,
        full_step,
        full_decay,
        full_skip,
        full_gate,
        full_out,
    ) = gathered
    segment = jnp.cumsum(resets)
    inputs = tokens.astype(jnp.float32)
    inv_rms = lax.rsqrt(jnp.mean(inputs * inputs, axis=-1, keepdims=True) + EPS)
    gain_f = full_norm.astype(jnp.float32)[None, :]
    normed = (inputs * inv_rms * gain_f).astype(jnp.bfloat16)
    projected = jnp.dot(normed, full_in, preferred_element_type=jnp.float32)
    small = tuple(
        (
            value.astype(jnp.float32)
            for value in (full_conv, full_bias, full_step, full_decay, full_skip, full_gate)
        )
    )
    mixed_f, pull_mixer = jax.vjp(partial(mixer, segment=segment), projected, *small)
    mixed_out = mixed_f.astype(jnp.bfloat16)
    branch = jnp.dot(mixed_out, full_out, preferred_element_type=jnp.float32)
    output = (inputs + branch).astype(jnp.bfloat16)
    back_in, back_out = (
        lax.all_gather(in_weight, "shard", axis=0, tiled=True),
        lax.all_gather(out_weight, "shard", axis=0, tiled=True),
    )
    out_grad = lax.dot_general(
        mixed_out, cotangent, (((0,), (0,)), ((), ())), preferred_element_type=jnp.float32
    )
    mixed_grad = lax.dot_general(
        cotangent, back_out, (((1,), (1,)), ((), ())), preferred_element_type=jnp.float32
    )
    pulled = pull_mixer(mixed_grad)
    proj_grad = pulled[0].astype(jnp.bfloat16)
    conv_grad, bias_grad, step_grad, decay_grad, skip_grad, gate_grad = pulled[1:]
    in_grad = lax.dot_general(
        normed, proj_grad, (((0,), (0,)), ((), ())), preferred_element_type=jnp.float32
    )
    normed_grad = lax.dot_general(
        proj_grad, back_in, (((1,), (1,)), ((), ())), preferred_element_type=jnp.float32
    )
    scaled = normed_grad * gain_f
    norm_grad = jnp.sum(normed_grad * inputs * inv_rms, axis=0)
    cube = inv_rms * inv_rms * inv_rms
    input_grad = (
        cotangent.astype(jnp.float32)
        + inv_rms * scaled
        - inputs * cube * jnp.mean(scaled * inputs, axis=-1, keepdims=True)
    )
    shares = (
        lax.psum_scatter(norm_grad, "shard", scatter_dimension=0, tiled=True),
        lax.psum_scatter(in_grad, "shard", scatter_dimension=0, tiled=True),
        lax.psum_scatter(conv_grad, "shard", scatter_dimension=1, tiled=True),
        lax.psum_scatter(bias_grad, "shard", scatter_dimension=0, tiled=True),
        lax.psum_scatter(step_grad, "shard", scatter_dimension=0, tiled=True),
        lax.psum_scatter(decay_grad, "shard", scatter_dimension=0, tiled=True),
        lax.psum_scatter(skip_grad, "shard", scatter_dimension=0, tiled=True),
        lax.psum_scatter(gate_grad, "shard", scatter_dimension=0, tiled=True),
        lax.psum_scatter(out_grad, "shard", scatter_dimension=0, tiled=True),
    )
    totals = lax.psum(
        (
            shares[0],
            shares[1],
            shares[2],
            shares[3],
            shares[4],
            shares[5],
            shares[6],
            shares[7],
            shares[8],
        ),
        "rep",
    )
    return (
        output,
        input_grad.astype(jnp.bfloat16),
        totals[0],
        totals[1],
        totals[2],
        totals[3],
        totals[4],
        totals[5],
        totals[6],
        totals[7],
        totals[8],
    )


def solution(mesh):
    placed = (
        P(("rep", "shard"), None),
        P(("rep", "shard")),
        P("shard"),
        P("shard", None),
        P(None, "shard"),
        P("shard"),
        P("shard"),
        P("shard"),
        P("shard"),
        P("shard"),
        P("shard", None),
        P(("rep", "shard"), None),
    )
    return jax.shard_map(
        on_device,
        mesh=mesh,
        in_specs=placed,
        out_specs=(
            P(("rep", "shard"), None),
            P(("rep", "shard"), None),
            P("shard"),
            P("shard", None),
            P(None, "shard"),
            P("shard"),
            P("shard"),
            P("shard"),
            P("shard"),
            P("shard"),
            P("shard", None),
        ),
        check_vma=False,
    )
```

profile of v0, /device:TPU:0, one launch (start us, length us, event | category | flops | bytes accessed | tf_op | source)
XLA Modules:
  0.0 1103.3 jit_solution(10867402310653550901)
XLA Ops:
  13.9 22.4 %all-gather.1 = bf16[8,1,128]{2,1,0:T(2,128)(2,1)S(1)} all-gather(bf16[1,1,128]{2,1,0:T(2,128)(2,1)} %bitcast.273), channel_id=1, replica_groups=mesh['rep'=4,'shard'=8] {'shard'}, dimensions={0}, use_global_device_ids=true | all-gather | bytes 2304 | tf_op jit(solution)/shard_map/all_gather | solution.py:108
  42.4 18.2 %all-reduce.40 = (bf16[2304]{0:T(1024)(128)(2,1)S(1)}, bf16[32]{0:T(256)(128)(2,1)S(1)}, bf16[32]{0:T(256)(128)(2,1)S(1)}, bf16[32]{0:T(256)(128)(2,1)S(1)}) all-reduce(bf16[2304]{0:T(1024)(128)(2,1)S(1)} %dynamic-update-slice, bf16[32]{0:T(256)(128)(2,1)S(1)} %dynamic-update-slice.2, ...), channel_id=1, replica_groups=mesh['rep'=4,'shard'=8] {'shard'}, use_global_device_ids=true, to_apply=%add.27 | all-reduce | flops 2400 | bytes 9600
  60.7 18.4 %all-gather.2 = bf16[8,1,256]{2,1,0:T(2,128)(2,1)S(1)} all-gather(bf16[1,1,256]{2,1,0:T(2,128)(2,1)S(1)} %reshape.388), channel_id=1, replica_groups=mesh['rep'=4,'shard'=8] {'shard'}, dimensions={0}, use_global_device_ids=true | all-gather | bytes 4608 | tf_op jit(solution)/shard_map/all_gather | solution.py:115
  79.4 36.0 %all-gather = bf16[8,288,4]{1,2,0:T(4,128)(2,1)S(1)} all-gather(bf16[1,288,4]{1,2,0:T(4,128)(2,1)} %bitcast.269), channel_id=1, replica_groups=mesh['rep'=4,'shard'=8] {'shard'}, dimensions={0}, use_global_device_ids=true | all-gather | bytes 20736 | tf_op jit(solution)/shard_map/all_gather | solution.py:110
  116.9 29.7 %all-gather.6.cloned.1.call-done = bf16[1024,4384]{0,1:T(8,128)(2,1)} async-done(((bf16[128,4384]{0,1:T(8,128)(2,1)}), bf16[1024,4384]{0,1:T(8,128)(2,1)}) %all-gather.6.cloned.1.call-update) | async-done | bytes 8978448 | tf_op jit(solution)/shard_map/all_gather | solution.py:109
  146.6 13.2 %fusion.88 = f32[1024,4384]{0,1:T(8,128)S(1)} fusion(bf16[1024,4384]{0,1:T(8,128)(2,1)} %all-gather.6.cloned.1.call-done, bf16[1024,1024]{1,0:T(8,128)(2,1)} %param.12, f32[1024]{0:T(1024)S(1)} %bitcast.263, f32[1024]{0:T(1024)S(1)} %get-tuple-element.79), kind=kOutput, calls=%fused_computation.131 | convolution fusion | flops 9198108672 | bytes 29040640 | tf_op jit(solution)/shard_map/dot_general | solution.py:134
  172.0 22.2 %fusion.26 = (f32[1024,2304]{0,1:T(8,128)S(1)}, f32[1024,2304]{0,1:T(8,128)}) fusion(f32[1024,2304]{0,1:T(8,128)} %slice.135, f32[2304]{0:T(1024)S(1)} %get-tuple-element.28, f32[1024]{0:T(1024)S(1)} %get-tuple-element.86, f32[2304]{0:T(1024)S(1)} %get-tuple-element.29, f32[1024]{0:T(1024)S(1)} %get-tuple-element.85, f32[2304]{0:T(1024)S(1)} %get-tuple-element.30, ...), kind=kLoop, calls=%fused_computation.43 | loop fusion | flops 35389440 | bytes 28369920 | tf_op jit(solution)/shard_map/jvp(jit(silu))/mul | solution.py:77
  239.3 40.7 %bitcast_add_fusion.1 = f32[4,256,32,64]{1,3,2,0:T(8,128)} fusion(f32[4,256,32,64]{1,3,2,0:T(8,128)S(1)} %fusion.73, f32[4,256,32]{1,2,0:T(8,128)S(1)} %get-tuple-element.76, f32[4,32,256]{2,1,0:T(8,128)S(1)} %bitcast.256, f32[4,32,256]{2,1,0:T(8,128)S(1)} %copy_bitcast_fusion, f32[4,256,256]{2,1,0:T(8,128)S(1)} %fusion.129, ...), kind=kOutput, calls=%fused_computation.60 | convolution fusion | flops 6488588288 | bytes 26869760 | tf_op jit(solution)/shard_map/jvp(bhts,bshp->bthp)/dot_general | solution.py:47
  280.1 14.0 %copy.359 = f32[4,256,32,64]{1,0,3,2:T(4,128)} copy(f32[4,256,32,64]{1,3,2,0:T(8,128)} %bitcast_add_fusion.1) | data formatting | bytes 16777216 | tf_op jit(solution)/shard_map/jvp()/add | solution.py:65
  332.2 18.4 %multiply_reduce_fusion.7 = (f32[2048]{0:T(1024)}, f32[1024,2048]{0,1:T(8,128)}, f32[1024,2048]{0,1:T(8,128)}) fusion(f32[1024,2304]{0,1:T(8,128)} %copy-done, f32[1024,4384]{0,1:T(8,128)} %copy-done.4, f32[1024,2048]{0,1:T(8,128)} %get-tuple-element.58, f32[1024]{0:T(1024)S(1)} %multiply_multiply_fusion.4, f32[1024]{0:T(1024)S(1)} %fusion.112, ...), kind=kLoop, calls=%fused_computation.62 | loop fusion | flops 44038144 | bytes 58753024 | tf_op jit(solution)/shard_map/transpose(jvp())/reduce_sum | solution.py:84
  361.3 18.0 %fusion.79 = f32[4,256,128]{2,1,0:T(8,128)} fusion(f32[1,32,64,128]{3,2,1,0:T(8,128)S(1)} %get-tuple-element.59, f32[1,32,64,128]{3,2,1,0:T(8,128)S(1)} %copy-done.21, f32[1,32,64,128]{3,2,1,0:T(8,128)} %copy-done.22, f32[4]{0:T(128)S(1)} %pad.134.clone, f32[4,256,32,64]{1,0,3,2:T(4,128)} %reshape.358, f32[4,256,32]{1,2,0:T(8,128)S(1)} %get-tuple-element.76), kind=kOutput, calls=%fused_computation.112 | convolution fusion | flops 3226468352 | bytes 12189712 | tf_op jit(solution)/shard_map/transpose(jvp(btn,bhpn->bthp))/dot_general | solution.py:63
  379.2 59.0 %fusion.8 = (f32[4,32,256]{2,1,0:T(8,128)}, f32[4,32,256]{2,1,0:T(8,128)}, f32[4,32,256]{2,1,0:T(8,128)}, f32[4,256,256]{2,1,0:T(8,128)S(1)}) fusion(f32[4,32,256]{2,1,0:T(8,128)S(1)} %bitcast.257, f32[4,32,256]{2,1,0:T(8,128)S(1)} %copy_bitcast_fusion, f32[4,256,256]{2,1,0:T(8,128)S(1)} %copy-done.30, pred[4,256,256]{2,1,0:T(8,128)(4,1)S(1)} %copy-done.39, ...), kind=kOutput, calls=%fused_computation.11 | convolution fusion | flops 6567919616 | bytes 19791872 | tf_op jit(solution)/shard_map/transpose(jvp(bhts,bshp->bthp))/dot_general | solution.py:47
  470.2 32.3 %bitcast_add_fusion = f32[4,256,32,64]{1,3,2,0:T(8,128)} fusion(f32[4,256,32,64]{1,3,2,0:T(8,128)S(1)} %get-tuple-element.94, f32[4,256,32]{1,2,0:T(8,128)S(1)} %copy-done.33, f32[4,32,256]{2,1,0:T(8,128)S(1)} %bitcast.258, f32[4,32,256]{2,1,0:T(8,128)S(1)} %copy-done.37, f32[4,256,256]{2,1,0:T(8,128)S(1)} %copy-done.31, ...), kind=kOutput, calls=%fused_computation.56 | convolution fusion | flops 6488588288 | bytes 26869760 | tf_op jit(solution)/shard_map/transpose(jvp(bhts,bshp->bthp))/dot_general | solution.py:47
  502.5 14.1 %copy.381 = f32[4,256,32,64]{1,0,3,2:T(4,128)} copy(f32[4,256,32,64]{1,3,2,0:T(8,128)} %bitcast_add_fusion) | data formatting | bytes 16777216 | tf_op jit(solution)/shard_map/transpose(jvp(bhts,bshp->bthp))/add_any | solution.py:47
  525.7 13.6 %fusion.76 = f32[4,256,128]{2,1,0:T(8,128)S(1)} fusion(f32[1,32,64,128]{3,2,1,0:T(8,128)S(1)} %get-tuple-element.55, f32[1,32,64,128]{3,2,1,0:T(8,128)S(1)} %copy-done.24, f32[1,32,64,128]{3,2,1,0:T(8,128)S(1)} %copy-done.26, f32[4,256,32,64]{1,0,3,2:T(4,128)S(1)} %bitcast.234, f32[4,256,32]{1,2,0:T(8,128)S(1)} %copy-done.34), kind=kOutput, calls=%fused_computation.111 | convolution fusion | flops 3225419776 | bytes 12189696 | tf_op jit(solution)/shard_map/transpose(jvp(bshp,bsn->bhpn))/dot_general | solution.py:56
  572.5 26.9 %multiply_reduce_fusion.4 = (f32[2304]{0:T(1024)S(1)}, f32[2304]{0:T(1024)S(1)}, f32[2304]{0:T(1024)S(1)}, f32[2304]{0:T(1024)S(1)}, f32[2304]{0:T(1024)S(1)}, /*index=5*/f32[1024,2304]{0,1:T(8,128)}) fusion(f32[1024,2304]{0,1:T(8,128)} %slice.135, f32[1024]{0:T(1024)S(1)} %copy-done.66, f32[1024]{0:T(1024)S(1)} %copy-done.64, f32[1024]{0:T(1024)S(1)} %copy-done.62, ...), kind=kLoop, calls=%fused_computation.40 | loop fusion | flops 54252288 | bytes 47244288 | tf_op jit(solution)/shard_map/transpose(jvp())/reduce_sum | solution.py:23
  599.4 13.7 %multiply_multiply_fusion = (f32[1024,2304]{0,1:T(8,128)S(1)}, f32[1024,2304]{0,1:T(8,128)}, f32[1024,2304]{0,1:T(8,128)}) fusion(f32[1024,2304]{0,1:T(8,128)} %get-tuple-element.54, f32[1024]{0:T(1024)S(1)} %copy-done.62, f32[2304]{0:T(1024)S(1)} %copy-done.52, f32[1024]{0:T(1024)S(1)} %copy-done.64, f32[2304]{0:T(1024)S(1)} %copy-done.56, ...), kind=kLoop, calls=%fused_computation.51 | loop fusion | flops 14155776 | bytes 37788672 | tf_op jit(solution)/shard_map/transpose(jvp())/mul | solution.py:23
  613.1 15.1 %fusion.23 = f32[1024,2304]{0,1:T(8,128)} fusion(f32[1024,2304]{0,1:T(8,128)} %get-tuple-element.69, f32[1024,2304]{0,1:T(8,128)} %get-tuple-element.68, f32[1024,2304]{0,1:T(8,128)S(1)} %get-tuple-element.67, f32[1024,2304]{0,1:T(8,128)S(1)} %copy-done.1, f32[2304]{0:T(1024)S(1)} %copy-done.50), kind=kLoop, calls=%fused_computation.35 | loop fusion | flops 9437184 | bytes 47195136 | tf_op jit(solution)/shard_map/transpose(jvp())/add_any | solution.py:20
  628.2 21.9 %fusion.86 = f32[1024,4384]{0,1:T(8,128)} fusion(bf16[1024,1024]{1,0:T(8,128)(2,1)S(1)} %copy-done.7, f32[1024]{0:T(1024)S(1)} %bitcast.264, f32[1024]{0:T(1024)S(1)} %copy-done.76, f32[1024,2048]{0,1:T(8,128)} %get-tuple-element.66, f32[1024,2304]{0,1:T(8,128)} %fusion.23, f32[1024,32]{0,1:T(8,128)S(1)} %get-tuple-element.53), kind=kOutput, calls=%fused_computation.130 | convolution fusion | flops 9211576320 | bytes 38019072 | tf_op jit(solution)/shard_map/dot_general | solution.py:158
  654.3 19.2 %fusion.58 = (f32[1024]{0:T(1024)S(1)}, f32[1024]{0:T(1024)S(1)}, f32[1024,1024]{1,0:T(8,128)}) fusion(bf16[1024,1024]{1,0:T(8,128)(2,1)S(1)} %copy-done.7, f32[1024]{0:T(1024)S(1)} %copy-done.76, f32[1024]{0:T(1024)S(1)} %bitcast.265, bf16[1024,4384]{0,1:T(8,128)(2,1)} %all-gather.6.cloned.1.call-done, f32[1024,2048]{0,1:T(8,128)} %get-tuple-element.66, ...), kind=kOutput, calls=%fused_computation.97 | convolution fusion | flops 9214720000 | bytes 33243136 | tf_op jit(solution)/shard_map/dot_general | solution.py:161
  673.8 36.6 %all-reduce.37 = (f32[1024]{0:T(1024)S(1)}, f32[2304]{0:T(1024)S(1)}, f32[32]{0:T(128)S(1)}, f32[32]{0:T(128)S(1)}, f32[32]{0:T(128)S(1)}, /*index=5*/f32[2048]{0:T(1024)S(1)}) all-reduce(f32[1024]{0:T(1024)S(1)} %get-tuple-element.24, f32[2304]{0:T(1024)S(1)} %get-tuple-element.20, ...), channel_id=2, replica_groups=mesh['rep'=4,'shard'=8] {'shard'}, use_global_device_ids=true, to_apply=%region_21.22.clone | all-reduce | flops 5472 | bytes 43776
  710.9 239.8 %reduce-scatter.6.cloned.1.call-done = f32[128,4384]{0,1:T(8,128)} async-done(((f32[1024,4384]{0,1:T(8,128)}), f32[128,4384]{0,1:T(8,128)}) %reduce-scatter.6.cloned.1.call-update) | async-done | bytes 2244624 | tf_op jit(solution)/shard_map/reduce_scatter | solution.py:174
  964.8 53.3 %reduce-scatter.10.cloned.1.call-done = f32[288,4]{1,0:T(8,128)} async-done(((f32[2304,4]{1,0:T(8,128)}), f32[288,4]{1,0:T(8,128)}) %reduce-scatter.10.cloned.1.call-update) | async-done | bytes 4624
  1030.3 60.5 %all-reduce.43.cloned.1.call-done = (f32[128,4384]{0,1:T(8,128)}, f32[256,1024]{1,0:T(8,128)}) async-done(((f32[128,4384]{0,1:T(8,128)}, f32[256,1024]{1,0:T(8,128)}), (f32[128,4384]{0,1:T(8,128)}, f32[256,1024]{1,0:T(8,128)})) %all-reduce.43.cloned.1.call-update) | async-done | bytes 3293200 | tf_op jit(solution)/shard_map/psum | solution.py:183
  (353 shorter events, 226.3 us)
Async XLA Ops:
  7.2 139.4 %all-gather.6.cloned.1.call-start = ((), (), s32[]{:S(2)}) async-start(), calls=%async_computation.3 | async-start | bytes 10100736 | tf_op jit(solution)/shard_map/all_gather | solution.py:109
  7.9 312.8 %all-gather.8.cloned.1.call-start = ((), (), s32[]{:S(2)}) async-start(), calls=%async_computation.4 | async-start | bytes 4718592 | tf_op jit(solution)/shard_map/all_gather | solution.py:116
  8.7 702.2 %reduce-scatter.8.cloned.1.call-start = ((), (), s32[]{:S(2)}) async-start(), calls=%async_computation.6 | async-start | bytes 9437184 | tf_op jit(solution)/shard_map/reduce_scatter | solution.py:181
  36.3 123.5 %copy-start.77 = (f32[8,1,128]{2,1,0:T(1,128)}, f32[8,1,128]{2,1,0:T(1,128)S(1)}, u32[]{:S(2)}) copy-start(f32[8,1,128]{2,1,0:T(1,128)S(1)} %convert_element_type.96) | copy-start | bytes 12292
  39.0 120.8 %copy-start.75 = (f32[1024]{0:T(1024)}, f32[1024]{0:T(1024)S(1)}, u32[]{:S(2)}) copy-start(f32[1024]{0:T(1024)S(1)} %get-tuple-element.79) | copy-start | bytes 12292
  60.6 104.2 %copy-start.90 = (f32[32]{0:T(128)}, f32[32]{0:T(128)S(1)}, u32[]{:S(2)}) copy-start(f32[32]{0:T(128)S(1)} %convert_element_type.85) | copy-start | bytes 388
  60.7 104.2 %copy-start.92 = (f32[32]{0:T(128)}, f32[32]{0:T(128)S(1)}, u32[]{:S(2)}) copy-start(f32[32]{0:T(128)S(1)} %fusion.113) | copy-start | bytes 388
  79.1 253.1 %copy-start.72 = (f32[8,1,256]{2,1,0:T(1,128)}, f32[8,1,256]{2,1,0:T(1,128)S(1)}, u32[]{:S(2)}) copy-start(f32[8,1,256]{2,1,0:T(1,128)S(1)} %convert_element_type.97) | copy-start | bytes 24580
  79.2 92.7 %copy-start.61 = (f32[1024]{0:T(1024)}, f32[1024]{0:T(1024)S(1)}, u32[]{:S(2)}) copy-start(f32[1024]{0:T(1024)S(1)} %get-tuple-element.84) | copy-start | bytes 12292
  79.2 92.7 %copy-start.63 = (f32[1024]{0:T(1024)}, f32[1024]{0:T(1024)S(1)}, u32[]{:S(2)}) copy-start(f32[1024]{0:T(1024)S(1)} %get-tuple-element.85) | copy-start | bytes 12292
  79.2 92.8 %copy-start.65 = (f32[1024]{0:T(1024)}, f32[1024]{0:T(1024)S(1)}, u32[]{:S(2)}) copy-start(f32[1024]{0:T(1024)S(1)} %get-tuple-element.86) | copy-start | bytes 12292
  79.4 252.8 %copy-start.42 = (f32[2048]{0:T(1024)}, f32[2048]{0:T(1024)S(1)}, u32[]{:S(2)}) copy-start(f32[2048]{0:T(1024)S(1)} %mul.610) | copy-start | bytes 24580
  116.9 77.5 %copy-start.86 = (f32[4]{0:T(128)}, f32[4]{0:T(128)S(1)}, u32[]{:S(2)}) copy-start(f32[4]{0:T(128)S(1)} %convert_reduce_fusion) | copy-start | bytes 52
  116.9 96.1 %copy-start.67 = (f32[4,256]{1,0:T(4,128)}, f32[4,256]{1,0:T(4,128)S(1)}, u32[]{:S(2)}) copy-start(f32[4,256]{1,0:T(4,128)S(1)} %get-tuple-element.81) | copy-start | bytes 12292
  116.9 96.1 %copy-start.69 = (f32[4,256]{1,0:T(4,128)}, f32[4,256]{1,0:T(4,128)S(1)}, u32[]{:S(2)}) copy-start(f32[4,256]{1,0:T(4,128)S(1)} %get-tuple-element.80) | copy-start | bytes 12292
  171.8 207.4 %copy-start.36 = (f32[4,32,256]{2,1,0:T(8,128)}, f32[4,32,256]{2,1,0:T(8,128)S(1)}, u32[]{:S(2)}) copy-start(f32[4,32,256]{2,1,0:T(8,128)S(1)} %copy_bitcast_fusion) | copy-start | bytes 393220
  200.5 178.8 %copy-start.44 = (f32[4,4,8,256]{3,2,0,1:T(8,128)}, f32[4,4,8,256]{3,2,0,1:T(8,128)S(1)}, u32[]{:S(2)}) copy-start(f32[4,4,8,256]{3,2,0,1:T(8,128)S(1)} %copy.482) | copy-start | bytes 393220
  379.2 59.0 %copy-start.11 = (f32[4,256,128,1]{2,1,3,0:T(8,128)S(1)}, f32[4,256,128,1]{2,1,3,0:T(8,128)}, u32[]{:S(2)}) copy-start(f32[4,256,128,1]{2,1,3,0:T(8,128)} %copy-done.10) | copy-start | bytes 1572868
  447.4 503.2 %reduce-scatter.6.cloned.1.call-start = ((), (), s32[]{:S(2)}) async-start(), calls=%async_computation.5 | async-start | bytes 20201472 | tf_op jit(solution)/shard_map/reduce_scatter | solution.py:174
  650.1 368.0 %reduce-scatter.10.cloned.1.call-start = ((), (), s32[]{:S(2)}) async-start(), calls=%async_computation.7 | async-start | bytes 1327104
  654.3 296.4 %copy-start.74 = (f32[1024]{0:T(1024)S(1)}, f32[1024]{0:T(1024)}, u32[]{:S(2)}) copy-start(f32[1024]{0:T(1024)} %get-tuple-element.78) | copy-start | bytes 12292
  673.5 281.9 %copy-start.73 = (f32[8,1,256]{2,1,0:T(1,128)S(1)}, f32[8,1,256]{2,1,0:T(1,128)}, u32[]{:S(2)}) copy-start(f32[8,1,256]{2,1,0:T(1,128)} %copy-done.72) | copy-start | bytes 24580
  673.5 281.9 %copy-start.80 = (f32[1024]{0:T(1024)S(1)}, f32[1024]{0:T(1024)}, u32[]{:S(2)}) copy-start(f32[1024]{0:T(1024)} %copy-done.79) | copy-start | bytes 12292
  673.5 417.3 %all-reduce.43.cloned.1.call-start = ((), (), s32[]{:S(2)}) async-start(), calls=%async_computation.8 | async-start | bytes 6586368 | tf_op jit(solution)/shard_map/psum | solution.py:183
  (88 other events, 1493.1 us)
Sparse Core Ops, SparseCore 0:
  10.1 136.5 all-gather.5
  148.7 71.6 all-gather.7
  447.5 147.2 reduce-scatter.7
  650.2 300.3 reduce-scatter.5
  954.8 63.2 reduce-scatter.9
  1020.6 70.2 all-reduce.42
where the time goes:
time: 1110 us; the launch traced here: 1100 us
  waiting for transfers between devices  385 us (35%)
  matrix products  295 us (27%)
  other arithmetic  156 us (14%)
  blocking collectives  143 us (13%)
  local copies, waits for them, and re-layouts  105 us (9%)
  between operations  19.8 us (2%)
    reduce_scatter x1, waiting for transfers between devices, on_device(): lax.psum_scatter(in_grad, 'shard', scatter_dimension=0, tiled=True)  240 us
    dot_general x3, matrix products, span_scan(): jnp.einsum('bhts,bshp->bthp', weights, x_blocks, precision=lax.Precision....  132 us
    psum x1, waiting for transfers between devices, on_device(): lax.psum((shares[0], shares[1], shares[2], shares[3], shares[4], shares[5...  60.5 us
    unnamed x2, blocking collectives  54.8 us
    unnamed x7, waiting for transfers between devices  54.7 us
    unnamed x235, local copies, waits for them, and re-layouts  40.1 us
    dot_general x3, matrix products, span_scan(): jnp.einsum('bshp,bsn->bhpn', weighted_x, b_blocks, precision=lax.Precisio...  39.3 us
    all_gather x1, blocking collectives, on_device(): lax.all_gather(conv_weight, 'shard', axis=1, tiled=True)  36 us
  transfers between devices with their start and end apart: 6, of which 4 were waited for; matrix products, arithmetic and copies ran while one was open for 37% of the time, Pallas kernels for 0%

commit v1 on v0

v1 whole, which is shorter than its diff:
```python
from functools import partial

import jax
import jax.numpy as jnp
import numpy as np
from jax import lax
from jax.experimental import pallas as pl
from jax.experimental.pallas import tpu as pltpu
from jax.sharding import PartitionSpec as P

EPS = 1e-05
SPAN = 128
LANES = 128
WIDTH = 64
BF = jnp.bfloat16
F32 = jnp.float32
HIGH = lax.Precision.HIGHEST


def mm(a, b):
    return jnp.dot(a, b, preferred_element_type=F32)


def mm_nt(a, b):
    return lax.dot_general(a, b, (((1,), (1,)), ((), ())), preferred_element_type=F32)


def split_lanes(v):
    lane = lax.broadcasted_iota(jnp.int32, v.shape, 1)
    high = v.astype(BF).astype(F32)
    return jnp.where(lane < 32, high, v - high).astype(BF)


def halves(v):
    high = v.astype(BF)
    return high, (v - high.astype(F32)).astype(BF)


def block_diag(v):
    lane = lax.broadcasted_iota(jnp.int32, v.shape, 1)
    zero = jnp.zeros_like(v)
    return jnp.concatenate([jnp.where(lane < WIDTH, v, zero), jnp.where(lane >= WIDTH, v, zero)], axis=0)


def softplus(v):
    return jnp.maximum(v, 0.0) + jnp.log1p(jnp.exp(-jnp.abs(v)))


def head_values(raw, col, hp_ref, ee_ref, a3_ref, at_ref, dtx_ref, esx_ref, tex_ref, keepx_ref):
    span = raw.shape[0]
    shifted = raw + hp_ref[0:1, :]
    dt = softplus(shifted)
    rates = hp_ref[1:2, :] * dt
    row = lax.broadcasted_iota(jnp.int32, (span, span), 0)
    column = lax.broadcasted_iota(jnp.int32, (span, span), 1)
    tri = jnp.where(row >= column, 1.0, 0.0).astype(F32)
    total = jnp.dot(tri, rates, precision=HIGH, preferred_element_type=F32)
    at_ref[...] = total.T
    for head in range(a3_ref.shape[0]):
        a3_ref[head] = jnp.broadcast_to(total[:, head : head + 1], a3_ref.shape[1:])
    last = total[span - 1 : span, :]
    ee = ee_ref[...]
    dtx_ref[...] = mm(split_lanes(dt), ee)
    esx_ref[...] = mm(split_lanes(jnp.exp(total) * col[:, 7:8]), ee)
    tex_ref[...] = mm(split_lanes(jnp.exp(last - total) * col[:, 8:9]), ee)
    keepx_ref[...] = mm(split_lanes(jnp.broadcast_to(jnp.exp(last) * col[0:1, 9:10], (8, LANES))), ee)
    return shifted, rates


def pair_decay(pair, a3_ref, at_ref):
    column = jnp.concatenate([a3_ref[2 * pair], a3_ref[2 * pair + 1]], axis=1)
    row = jnp.concatenate([at_ref[pl.ds(2 * pair, 1), :], at_ref[pl.ds(2 * pair + 1, 1), :]], axis=1)
    return column, row


def fwd_kernel(
    inner,
    xbc_ref, col_ref, row_ref, cw_ref, hp_ref, skip_ref, ee_ref,
    y_ref, pre_ref, sin_ref,
    buf, state, a3_ref, at_ref, dtx_ref, esx_ref, tex_ref, keepx_ref, g2_ref,
):
    span = y_ref.shape[0]
    mixed = pre_ref.shape[1]
    step = pl.program_id(0)

    @pl.when(step == 0)
    def _():
        buf[0:8, :] = jnp.zeros((8, mixed), F32)
        state[...] = jnp.zeros_like(state)

    @pl.when(step > 0)
    def _():
        buf[0:8, :] = buf[span : span + 8, :]

    buf[8 : 8 + span, :] = xbc_ref[:, :mixed]
    col = col_ref[...]
    head_values(
        xbc_ref[:, mixed : mixed + LANES], col, hp_ref, ee_ref, a3_ref, at_ref, dtx_ref, esx_ref, tex_ref, keepx_ref
    )
    same = [None] + [jnp.broadcast_to(col[:, k : k + 1], (span, LANES)) for k in (1, 2, 3)]

    def conv(lanes):
        total = cw_ref[4:5, lanes] + cw_ref[3:4, lanes] * buf[8 : 8 + span, lanes]
        for k in (1, 2, 3):
            total = total + cw_ref[3 - k : 4 - k, lanes] * (buf[8 - k : 8 - k + span, lanes] * same[k])
        pre_ref[:, lanes] = total
        return total * jax.nn.sigmoid(total)

    b_f = conv(slice(inner, inner + LANES))
    c_b = conv(slice(inner + LANES, inner + 2 * LANES)).astype(BF)
    b_b = b_f.astype(BF)
    b_t = b_f.T.astype(BF)
    t_index = lax.broadcasted_iota(jnp.int32, (span, span), 0)
    s_index = lax.broadcasted_iota(jnp.int32, (span, span), 1)
    linked = (t_index >= s_index) & (col[:, 0:1] == row_ref[0:1, :])
    inter = jnp.where(linked, mm_nt(c_b, b_b), 0.0)
    g2_ref[...] = jnp.concatenate([inter, inter], axis=1)

    def pair_step(pair, carry):
        lanes = pl.ds(pl.multiple_of(pair * LANES, LANES), LANES)
        x = conv(lanes)
        xd = x * dtx_ref[:, lanes]
        column, row = pair_decay(pair, a3_ref, at_ref)
        decay = jnp.exp(jnp.minimum(column - row, 0.0))
        inside = mm((g2_ref[...] * decay).astype(BF), block_diag(xd.astype(BF)))
        held = state[:, lanes]
        held_b = held.astype(BF)
        sin_ref[:, lanes] = held_b
        y_ref[:, lanes] = inside + mm(c_b, held_b) * esx_ref[:, lanes] + skip_ref[0:1, lanes] * x
        state[:, lanes] = held * keepx_ref[0:1, lanes] + mm(b_t, (xd * tex_ref[:, lanes]).astype(BF))
        return carry

    lax.fori_loop(0, inner // LANES, pair_step, 0, unroll=2)


def bwd_kernel(
    inner,
    xbc_ref, pre_ref, y_ref, gy_ref, sin_ref, col_ref, row_ref, cw_ref, hp_ref, skip_ref, ee_ref, rt_ref,
    gp_ref, cwg_ref, hpg_ref, skg_ref,
    grad, halo, gstate, a3_ref, at_ref, dtx_ref, esx_ref, tex_ref, keepx_ref, gt2_ref, ggt_ref, gb_ref, gc_ref, acc_ref, kv_ref,
):
    span = y_ref.shape[0]
    mixed = pre_ref.shape[1]
    step = pl.program_id(0)

    @pl.when(step == 0)
    def _():
        halo[...] = jnp.zeros_like(halo)
        gstate[...] = jnp.zeros_like(gstate)
        cwg_ref[...] = jnp.zeros_like(cwg_ref)
        hpg_ref[...] = jnp.zeros_like(hpg_ref)
        skg_ref[...] = jnp.zeros_like(skg_ref)

    col = col_ref[...]
    shifted, rates = head_values(
        xbc_ref[:, mixed : mixed + LANES], col, hp_ref, ee_ref, a3_ref, at_ref, dtx_ref, esx_ref, tex_ref, keepx_ref
    )
    ahead = [None] + [jnp.broadcast_to(col[:, 3 + k : 4 + k], (span, LANES)) for k in (1, 2, 3)]

    def conv_back(lanes, g):
        grad[0:span, lanes] = g
        grad[span : span + 8, lanes] = halo[:, lanes]
        halo[:, lanes] = g[0:8, :]
        xin = xbc_ref[:, lanes]
        back = cw_ref[3:4, lanes] * g
        cwg_ref[3:4, lanes] += jnp.sum(xin * g, axis=0, keepdims=True)
        cwg_ref[4:5, lanes] += jnp.sum(g, axis=0, keepdims=True)
        for k in (1, 2, 3):
            moved = grad[k : k + span, lanes] * ahead[k]
            back = back + cw_ref[3 - k : 4 - k, lanes] * moved
            cwg_ref[3 - k : 4 - k, lanes] += jnp.sum(xin * moved, axis=0, keepdims=True)
        gp_ref[:, lanes] = back.astype(BF)

    def act(lanes):
        pre = pre_ref[:, lanes]
        sig = jax.nn.sigmoid(pre)
        return pre * sig, sig * (1.0 + pre * (1.0 - sig))

    b_lanes, c_lanes = slice(inner, inner + LANES), slice(inner + LANES, inner + 2 * LANES)
    b_f, b_slope = act(b_lanes)
    c_f, c_slope = act(c_lanes)
    b_b, c_b = b_f.astype(BF), c_f.astype(BF)
    c_t = c_f.T.astype(BF)
    s_index = lax.broadcasted_iota(jnp.int32, (span, span), 0)
    t_index = lax.broadcasted_iota(jnp.int32, (span, span), 1)
    linked = (t_index >= s_index) & (col[:, 0:1] == row_ref[0:1, :])
    inter = jnp.where(linked, mm_nt(b_b, c_b), 0.0)
    gt2_ref[...] = jnp.concatenate([inter, inter], axis=1)
    ggt_ref[...] = jnp.zeros_like(ggt_ref)
    gb_ref[...] = jnp.zeros_like(gb_ref)
    gc_ref[...] = jnp.zeros_like(gc_ref)
    acc_ref[...] = jnp.zeros_like(acc_ref)

    def pair_step(pair, carry):
        lanes = pl.ds(pl.multiple_of(pair * LANES, LANES), LANES)
        x, slope = act(lanes)
        dtx, tex = dtx_ref[:, lanes], tex_ref[:, lanes]
        xd = x * dtx
        xd_b = xd.astype(BF)
        gy_b = gy_ref[:, lanes]
        gy = gy_b.astype(F32)
        diag = block_diag(gy_b)
        column, row = pair_decay(pair, a3_ref, at_ref)
        decay = jnp.exp(jnp.minimum(row - column, 0.0))
        linked_g = mm_nt(xd_b, diag) * decay
        ggt_ref[...] += linked_g[:, :span] + linked_g[:, span:]
        gx_in = mm((gt2_ref[...] * decay).astype(BF), diag)
        gs = gstate[:, lanes]
        gs_b = gs.astype(BF)
        gx_state = tex * mm(b_b, gs_b)
        gxd = gx_in + gx_state
        from_state = xd * gx_state
        skip = skip_ref[0:1, lanes]
        drift = gy * (y_ref[:, lanes] - skip * x) - xd_b.astype(F32) * gx_in - from_state
        parts = [halves(v) for v in (drift, from_state, x * gxd)]
        stacked = jnp.concatenate([jnp.concatenate(part, axis=1) for part in parts], axis=0)
        rt = rt_ref[lanes, :]
        acc_ref[...] += mm(stacked, jnp.concatenate([rt, rt], axis=0))
        skg_ref[0:1, lanes] += jnp.sum(gy * x, axis=0, keepdims=True)
        held_b = sin_ref[:, lanes]
        keepx = keepx_ref[0:1, lanes]
        kv_ref[0:1, lanes] = keepx * jnp.sum(held_b.astype(F32) * gs, axis=0, keepdims=True)
        scaled = (esx_ref[:, lanes] * gy).astype(BF)
        gc_ref[...] += mm_nt(scaled, held_b)
        gb_ref[...] += mm_nt((xd * tex).astype(BF), gs_b)
        gstate[:, lanes] = keepx * gs + mm(c_t, scaled)
        conv_back(lanes, (dtx * gxd + skip * gy) * slope)
        return carry

    kv_ref[...] = jnp.zeros_like(kv_ref)
    lax.fori_loop(0, inner // LANES, pair_step, 0, unroll=2)
    g_inter = jnp.where(linked, ggt_ref[...], 0.0)
    conv_back(b_lanes, (gb_ref[...] + mm(g_inter.astype(BF), c_b)) * b_slope)
    conv_back(c_lanes, (gc_ref[...] + mm(g_inter.T.astype(BF), b_b)) * c_slope)
    kv_high, kv_low = halves(kv_ref[...])
    rt = rt_ref[...]
    kept = mm(kv_high, rt) + mm(kv_low, rt)
    at_end = jnp.sum(acc_ref[span : 2 * span, :], axis=0, keepdims=True) + kept[0:1, :]
    tri = jnp.where(t_index >= s_index, 1.0, 0.0).astype(F32)
    g_rate = jnp.dot(tri, acc_ref[0:span, :], precision=HIGH, preferred_element_type=F32) + at_end
    g_raw = (acc_ref[2 * span : 3 * span, :] + hp_ref[1:2, :] * g_rate) * jax.nn.sigmoid(shifted)
    gp_ref[:, mixed : mixed + LANES] = g_raw.astype(BF)
    hpg_ref[0:1, :] += jnp.sum(g_raw, axis=0, keepdims=True)
    hpg_ref[1:2, :] += jnp.sum(rates * g_rate, axis=0, keepdims=True)


def gate_kernel(y_ref, z_ref, gm_ref, gain_ref, out_ref, gy_ref, gz_ref, gg_ref):
    rows, inner = y_ref.shape

    @pl.when(pl.program_id(0) == 0)
    def _():
        gg_ref[...] = jnp.zeros_like(gg_ref)

    pieces = [slice(k, k + LANES) for k in range(0, inner, LANES)]
    square = jnp.zeros((rows, LANES), F32)
    cross = jnp.zeros((rows, LANES), F32)
    for lanes in pieces:
        z = z_ref[:, lanes]
        gated = y_ref[:, lanes] * (z * jax.nn.sigmoid(z))
        square = square + gated * gated
        cross = cross + gated * (gm_ref[:, lanes] * gain_ref[0:1, lanes])
    inv = lax.rsqrt(jnp.sum(square, axis=1, keepdims=True) / inner + EPS)
    pull = inv * inv * inv * (jnp.sum(cross, axis=1, keepdims=True) / inner)
    for lanes in pieces:
        z, y, gm = z_ref[:, lanes], y_ref[:, lanes], gm_ref[:, lanes]
        sig = jax.nn.sigmoid(z)
        silu = z * sig
        gated = y * silu
        gain = gain_ref[0:1, lanes]
        unit = gated * inv
        out_ref[:, lanes] = (unit * gain).astype(BF)
        gg_ref[0:1, lanes] += jnp.sum(gm * unit, axis=0, keepdims=True)
        g_gated = inv * (gm * gain) - gated * pull
        gy_ref[:, lanes] = (g_gated * silu).astype(BF)
        gz_ref[:, lanes] = (g_gated * y * (sig * (1.0 + z * (1.0 - sig)))).astype(BF)


def full(shape):
    return pl.BlockSpec(shape, lambda i: (0,) * len(shape))


def onehots(inner):
    heads = inner // WIDTH
    owner = np.arange(inner) // WIDTH
    spread = np.zeros((LANES, inner), np.float32)
    spread[owner, np.arange(inner)] = 1
    spread[32 + owner, np.arange(inner)] = 1
    collect = np.zeros((inner, LANES), np.float32)
    collect[np.arange(inner), owner] = 1
    return jnp.asarray(spread, BF), jnp.asarray(collect, BF)


PARAMS = pltpu.CompilerParams(dimension_semantics=("arbitrary",), vmem_limit_bytes=52 * 2**20)


def common_scratch(inner):
    heads = inner // WIDTH
    return [
        pltpu.VMEM((heads, SPAN, LANES), F32),
        pltpu.VMEM((LANES, SPAN), F32),
        pltpu.VMEM((SPAN, inner), F32),
        pltpu.VMEM((SPAN, inner), F32),
        pltpu.VMEM((SPAN, inner), F32),
        pltpu.VMEM((8, inner), F32),
        pltpu.VMEM((SPAN, 2 * SPAN), F32),
    ]


def scan_forward(xbc, col, row, cw, hp, skip):
    length, mixed, inner = xbc.shape[0], cw.shape[1], skip.shape[1]
    spread, _ = onehots(inner)
    blocks = length // SPAN
    return pl.pallas_call(
        partial(fwd_kernel, inner),
        grid=(blocks,),
        in_specs=[
            pl.BlockSpec((SPAN, mixed + LANES), lambda i: (i, 0)),
            pl.BlockSpec((SPAN, 16), lambda i: (i, 0)),
            pl.BlockSpec((8, SPAN), lambda i: (0, i)),
            full((8, mixed)), full((8, LANES)), full((8, inner)), full((LANES, inner)),
        ],
        out_specs=[
            pl.BlockSpec((SPAN, inner), lambda i: (i, 0)),
            pl.BlockSpec((SPAN, mixed), lambda i: (i, 0)),
            pl.BlockSpec((LANES, inner), lambda i: (i, 0)),
        ],
        out_shape=[
            jax.ShapeDtypeStruct((length, inner), F32),
            jax.ShapeDtypeStruct((length, mixed), F32),
            jax.ShapeDtypeStruct((blocks * LANES, inner), BF),
        ],
        scratch_shapes=[pltpu.VMEM((SPAN + 8, mixed), F32), pltpu.VMEM((LANES, inner), F32)] + common_scratch(inner),
        compiler_params=PARAMS,
        cost_estimate=pl.CostEstimate(flops=6 * 10**9, bytes_accessed=3 * 10**7, transcendentals=10**7),
        name="scan_forward",
    )(xbc, col, row, cw, hp, skip, spread)


def scan_backward(xbc, pre, y, gy, sin, col, row, cw, hp, skip):
    length, mixed, inner = xbc.shape[0], cw.shape[1], skip.shape[1]
    spread, collect = onehots(inner)
    blocks = length // SPAN
    rev = lambda i: (blocks - 1 - i, 0)
    return pl.pallas_call(
        partial(bwd_kernel, inner),
        grid=(blocks,),
        in_specs=[
            pl.BlockSpec((SPAN, mixed + LANES), rev),
            pl.BlockSpec((SPAN, mixed), rev),
            pl.BlockSpec((SPAN, inner), rev),
            pl.BlockSpec((SPAN, inner), rev),
            pl.BlockSpec((LANES, inner), rev),
            pl.BlockSpec((SPAN, 16), rev),
            pl.BlockSpec((8, SPAN), lambda i: (0, blocks - 1 - i)),
            full((8, mixed)), full((8, LANES)), full((8, inner)), full((LANES, inner)), full((inner, LANES)),
        ],
        out_specs=[
            pl.BlockSpec((SPAN, mixed + LANES), rev),
            full((8, mixed)), full((8, LANES)), full((8, inner)),
        ],
        out_shape=[
            jax.ShapeDtypeStruct((length, mixed + LANES), BF),
            jax.ShapeDtypeStruct((8, mixed), F32),
            jax.ShapeDtypeStruct((8, LANES), F32),
            jax.ShapeDtypeStruct((8, inner), F32),
        ],
        scratch_shapes=[
            pltpu.VMEM((SPAN + 8, mixed), F32), pltpu.VMEM((8, mixed), F32), pltpu.VMEM((LANES, inner), F32),
        ] + common_scratch(inner) + [
            pltpu.VMEM((SPAN, SPAN), F32), pltpu.VMEM((SPAN, LANES), F32), pltpu.VMEM((SPAN, LANES), F32),
            pltpu.VMEM((3 * SPAN, LANES), F32), pltpu.VMEM((8, inner), F32),
        ],
        compiler_params=PARAMS,
        cost_estimate=pl.CostEstimate(flops=2 * 10**10, bytes_accessed=5 * 10**7, transcendentals=10**7),
        name="scan_backward",
    )(xbc, pre, y, gy, sin, col, row, cw, hp, skip, spread, collect)


def gate(y, z, gm, gain):
    length, inner = y.shape
    rows = 128
    block = lambda: pl.BlockSpec((rows, inner), lambda i: (i, 0))
    return pl.pallas_call(
        gate_kernel,
        grid=(length // rows,),
        in_specs=[block(), block(), block(), full((8, inner))],
        out_specs=[block(), block(), block(), full((8, inner))],
        out_shape=[jax.ShapeDtypeStruct((length, inner), BF)] * 3 + [jax.ShapeDtypeStruct((8, inner), F32)],
        compiler_params=PARAMS,
        cost_estimate=pl.CostEstimate(flops=10**8, bytes_accessed=4 * 10**7, transcendentals=4 * 10**6),
        name="gate",
    )(y, z, gm, gain)


def document_info(resets):
    length = resets.shape[0]
    segment = jnp.cumsum(resets).astype(jnp.int32)
    back = [jnp.pad(segment, (k, 0), constant_values=-1)[:length] == segment for k in (1, 2, 3)]
    ahead = [jnp.pad(segment, (0, k), constant_values=-1)[k:] == segment for k in (1, 2, 3)]
    last = segment.reshape(-1, SPAN)[:, -1]
    before = jnp.concatenate([jnp.full((1,), -1, jnp.int32), last[:-1]])
    last, before = jnp.repeat(last, SPAN), jnp.repeat(before, SPAN)
    columns = [segment] + back + ahead + [segment == before, segment == last, last == before]
    columns = columns + [jnp.zeros_like(segment)] * (16 - len(columns))
    col = jnp.stack([c.astype(F32) for c in columns], axis=1)
    row = jnp.broadcast_to(segment.astype(F32)[None, :], (8, length))
    return col, row


def rows8(*rows):
    width = rows[0].shape[-1]
    rows = [r.reshape(-1, width).astype(F32) for r in rows]
    have = sum(r.shape[0] for r in rows)
    return jnp.concatenate(rows + [jnp.zeros((8 - have, width), F32)], axis=0)


def pairs(size, flip):
    return [(i, i ^ flip) for i in range(size)]


def other_core(value, reps):
    return lax.ppermute(value, "rep", pairs(reps, 1))


def swap_halves(own, core, reps, axis):
    other = other_core(own, reps)
    first = core == 0
    return jnp.stack([jnp.where(first, own, other), jnp.where(first, other, own)], axis=axis)


def half_of(value, core, axis):
    pick = lambda k: lax.dynamic_index_in_dim(value, k, axis, keepdims=False)
    return pick(core), pick(1 - core)


def sum_cores(value, core, reps):
    mine, theirs = half_of(value, core, 1)
    return (mine.astype(F32) + other_core(theirs, reps).astype(F32)).astype(BF)


def sum_reps(value, reps):
    flip = 2
    while flip < reps:
        value = (value.astype(F32) + lax.ppermute(value, "rep", pairs(reps, flip)).astype(F32)).astype(BF)
        flip *= 2
    return value


def sum_all(value, reps, shards):
    for axis, size in (("rep", reps), ("shard", shards)):
        flip = 1
        while flip < size:
            value = value + lax.ppermute(value, axis, pairs(size, flip))
            flip *= 2
    return value


def on_device(reps, shards, *args):
    (tokens, resets, norm_gain, in_weight, conv_weight, conv_bias, step_bias, decay_log, skip_gain, gate_gain,
     out_weight, cotangent) = args
    rows, proj = in_weight.shape
    width = tokens.shape[1]
    inner = shards * gate_gain.shape[0]
    mixed = shards * conv_bias.shape[0]
    heads = shards * step_bias.shape[0]
    half = rows // 2
    core = lax.axis_index("rep") % 2
    member = lax.axis_index("shard")

    small_parts = (norm_gain, conv_weight, conv_bias, step_bias, decay_log, skip_gain, gate_gain)
    small = jnp.concatenate([v.reshape(-1) for v in small_parts])
    small = jnp.pad(small, (0, half * LANES - small.shape[0])).reshape(half, LANES)
    dt_in = in_weight[:, inner + mixed :]
    x_in = jnp.concatenate([in_weight[:, inner : inner + mixed]] + [dt_in] * (LANES // heads), axis=1)
    x_own = lax.dynamic_slice_in_dim(x_in, core * half, half, 0)
    x_all = lax.all_gather(jnp.concatenate([x_own, small], axis=1), "shard", axis=0)
    x_width = mixed + LANES
    w_x = swap_halves(x_all[:, :, :x_width], core, reps, 1).reshape(width, x_width)
    small_all = x_all[:, :, x_width:].reshape(shards, -1).astype(F32)
    z_own = lax.dynamic_slice_in_dim(in_weight[:, :inner], core * half, half, 0)
    out_own = lax.dynamic_slice_in_dim(out_weight, core * 2 * half, 2 * half, 0).reshape(half, inner)
    zo_all = lax.all_gather(jnp.concatenate([z_own, out_own], axis=0), "shard", axis=0)
    zo = swap_halves(zo_all, core, reps, 1)
    w_z = zo[:, :, :half].reshape(width, inner)
    w_out = zo[:, :, half:].reshape(inner, width)

    full_small, at = [], 0
    for part in small_parts:
        piece = small_all[:, at : at + part.size]
        at += part.size
        if part.ndim == 2:
            piece = jnp.moveaxis(piece.reshape(shards, part.shape[0], part.shape[1]), 0, 1).reshape(part.shape[0], -1)
        else:
            piece = piece.reshape(-1)
        full_small.append(piece)
    gain, cw, cb, sb, dl, sk, gg = full_small
    repeat = LANES // heads
    cw8 = rows8(cw, cb)
    hp8 = rows8(jnp.tile(sb, repeat), jnp.tile(-jnp.exp(dl), repeat))
    sk8 = rows8(jnp.repeat(sk, WIDTH))
    gg8 = rows8(gg)

    col, row = document_info(resets)
    inputs = tokens.astype(F32)
    inv_rms = lax.rsqrt(jnp.mean(inputs * inputs, axis=-1, keepdims=True) + EPS)
    normed = (inputs * inv_rms * gain[None, :]).astype(BF)
    xbc = mm(normed, w_x)
    y, pre, sin = scan_forward(xbc, col, row, cw8, hp8, sk8)
    z = mm(normed, w_z)
    g_mixed = mm_nt(cotangent, w_out)
    mixed_out, gy, gz, gg_grad = gate(y, z, g_mixed, gg8)

    def grad_of(left, right):
        return lax.dot_general(left, right, (((0,), (0,)), ((), ())), preferred_element_type=F32).astype(BF)

    out_grad = grad_of(mixed_out, cotangent).reshape(shards, 2, half, inner)
    z_grad = grad_of(normed, gz).reshape(shards, 2, half, inner)
    zo_sum = sum_cores(jnp.concatenate([z_grad, out_grad], axis=2), core, reps)
    zo_own = lax.psum_scatter(zo_sum, "shard", scatter_dimension=0)
    gp, cwg, hpg, skg = scan_backward(xbc, pre, y, gy, sin, col, row, cw8, hp8, sk8)
    x_grad = grad_of(normed, gp).reshape(shards, 2, half, x_width)
    x_own = lax.psum_scatter(sum_cores(x_grad, core, reps), "shard", scatter_dimension=0)
    output = (inputs + mm(mixed_out, w_out)).astype(BF)

    g_normed = mm_nt(gz, w_z) + mm_nt(gp, w_x)
    scaled = g_normed * gain[None, :]
    unit = inputs * inv_rms
    gain_grad = jnp.sum(g_normed * unit, axis=0)
    back = cotangent.astype(F32) + inv_rms * (scaled - unit * jnp.mean(scaled * unit, axis=-1, keepdims=True))
    input_grad = back.astype(BF)

    grads = (cwg[:4], cwg[4], hpg[0, :heads], hpg[1, :heads], skg[0].reshape(heads, WIDTH).sum(axis=1), gg_grad[0])
    split = lambda v: jnp.moveaxis(v.reshape(v.shape[:-1] + (shards, -1)), -2, 0).reshape(shards, -1)
    totals = sum_all(jnp.concatenate([split(v) for v in (gain_grad,) + grads], axis=1), reps, shards)
    own = lax.dynamic_index_in_dim(totals, member, 0, keepdims=False)
    small_grads, at = [], 0
    for part in small_parts:
        small_grads.append(own[at : at + part.size].reshape(part.shape))
        at += part.size

    both = jnp.concatenate([zo_own[:half], zo_own[half:], x_own], axis=1)
    both = swap_halves(sum_reps(both, reps), core, reps, 0).astype(F32)
    z_part = both[:, :, :inner].reshape(rows, inner)
    out_part = both[:, :, inner : 2 * inner].reshape(out_weight.shape)
    x_part = both[:, :, 2 * inner : 2 * inner + mixed + heads].reshape(rows, mixed + heads)
    in_grad = jnp.concatenate([z_part, x_part], axis=1)
    return (output, input_grad, small_grads[0], in_grad, *small_grads[1:], out_part)


def solution(mesh):
    by_token, by_shard = P(("rep", "shard"), None), P("shard")
    in_specs = (
        by_token, P(("rep", "shard")), by_shard, P("shard", None), P(None, "shard"), by_shard, by_shard, by_shard,
        by_shard, by_shard, P("shard", None), by_token,
    )
    out_specs = (
        by_token, by_token, by_shard, P("shard", None), P(None, "shard"), by_shard, by_shard, by_shard, by_shard,
        by_shard, P("shard", None),
    )
    return jax.shard_map(
        partial(on_device, mesh.shape["rep"], mesh.shape["shard"]),
        mesh=mesh,
        in_specs=in_specs,
        out_specs=out_specs,
        check_vma=False,
    )
```

time: 1110 us -> 499 us (0.45)
  matrix products: 295 us -> 74.7 us
  waiting for transfers between devices: 385 us -> 191 us
  blocking collectives: 143 us -> 0 us
  Pallas kernels: 0 us -> 135 us
  other arithmetic: 156 us -> 27.8 us
  local copies, waits for them, and re-layouts: 105 us -> 39.3 us
    dot_general x18 -> x9, matrix products: 295 us -> 74.7 us  [the longest x3 27.4 us: mm(): return jnp.dot(a, b, preferred_element_type=F32)]
    reduce_scatter x2, waiting for transfers between devices: 240 us -> 47.2 us  [the longest x1 47.2 us: on_device(): lax.psum_scatter(sum_cores(x_grad, core, reps), 'shard', scatter_dimensio...]
    pallas_call x0 -> x3, Pallas kernels: none -> 135 us  [the longest x1 75.8 us: scan_backward(): pl.pallas_call(partial(bwd_kernel, inner), grid=(blocks,), in_specs=[pl.B...]
    all_gather x2, waiting for transfers between devices: 29.7 us -> 123 us  [the longest x1 68.1 us: on_device(): lax.all_gather(jnp.concatenate([z_own, out_own], axis=0), 'shard', axis=0)]
    all_gather x3 -> x0, blocking collectives: 76.9 us -> none  [the longest x1 36 us: on_device(): lax.all_gather(conv_weight, 'shard', axis=1, tiled=True)]
    reduce_sum x8 -> x1, other arithmetic: 69.3 us -> 0.12 us  [on_device(): skg[0].reshape(heads, WIDTH).sum(axis=1)]
    psum x1 -> x0, waiting for transfers between devices: 60.5 us -> none  [on_device(): lax.psum((shares[0], shares[1], shares[2], shares[3], shares[4], shares[5...]
    unnamed x2 -> x0, blocking collectives: 54.8 us -> none
  transfers between devices with their start and end apart: 6 -> 15, of which waited for: 4 -> 9; matrix products, arithmetic and copies ran while one was open for 37% -> 14% of each run, Pallas kernels for 0% -> 24%
where the time goes in v1:
time: 499 us; the launch traced here: 489 us
  waiting for transfers between devices  191 us (38%)
  Pallas kernels  135 us (27%)
  matrix products  74.7 us (15%)
  local copies, waits for them, and re-layouts  39.3 us (8%)
  other arithmetic  27.8 us (6%)
  between operations  14.7 us (3%)
  starting transfers between devices  7.5 us (2%)
    pallas_call x1, Pallas kernels, scan_backward(): pl.pallas_call(partial(bwd_kernel, inner), grid=(blocks,), in_specs=[pl.B...  75.8 us
    all_gather x1, waiting for transfers between devices, on_device(): lax.all_gather(jnp.concatenate([z_own, out_own], axis=0), 'shard', axis=0)  68.1 us
    all_gather x1, waiting for transfers between devices, on_device(): lax.all_gather(jnp.concatenate([x_own, small], axis=1), 'shard', axis=0)  54.6 us
    reduce_scatter x1, waiting for transfers between devices, on_device(): lax.psum_scatter(sum_cores(x_grad, core, reps), 'shard', scatter_dimensio...  47.2 us
    pallas_call x1, Pallas kernels, scan_forward(): pl.pallas_call(partial(fwd_kernel, inner), grid=(blocks,), in_specs=[pl.B...  40.5 us
    dot_general x3, matrix products, mm(): return jnp.dot(a, b, preferred_element_type=F32)  27.4 us
    dot_general x3, matrix products, grad_of(): lax.dot_general(left, right, (((0,), (0,)), ((), ())), preferred_element_...  24.4 us
    dot_general x3, matrix products, mm_nt(): lax.dot_general(a, b, (((1,), (1,)), ((), ())), preferred_element_type=F32)  22.9 us
  transfers between devices with their start and end apart: 15, of which 9 were waited for; matrix products, arithmetic and copies ran while one was open for 14% of the time, Pallas kernels for 24%

profile of v1, /device:TPU:0, one launch (start us, length us, event | category | flops | bytes accessed | tf_op | source)
XLA Modules:
  0.0 489.2 jit_solution(7483262547606735527)
XLA Ops:
  10.3 4.1 concatenate.41
  18.5 54.6 %all-gather.5.cloned.1.call-done = bf16[512,2560]{1,0:T(8,128)(2,1)} async-done(((bf16[64,2560]{1,0:T(8,128)(2,1)}), bf16[512,2560]{1,0:T(8,128)(2,1)}) %all-gather.5.cloned.1.call-update) | async-done | bytes 2621456 | tf_op jit(solution)/shard_map/all_gather | solution.py:476
  79.7 68.1 %all-gather.7.cloned.1.call-done = bf16[1024,2048]{1,0:T(8,128)(2,1)} async-done(((bf16[128,2048]{1,0:T(8,128)(2,1)}), bf16[1024,2048]{1,0:T(8,128)(2,1)}) %all-gather.7.cloned.1.call-update) | async-done | bytes 4194320 | tf_op jit(solution)/shard_map/all_gather | solution.py:482
  151.9 8.6 %fusion.38.xbc_ref = f32[1024,2432]{1,0:T(8,128)} fusion(bf16[1024,2432]{1,0:T(8,128)(2,1)S(1)} %bitcast.108, bf16[1024,1024]{1,0:T(8,128)(2,1)S(1)} %copy-done.6, f32[1024]{0:T(1024)S(1)} %slice_bitcast_fusion.3, f32[1024]{0:T(1024)S(1)} %add_rsqrt_fusion), kind=kOutput, calls=%fused_computation.111 | convolution fusion | flops 5104467968 | bytes 17047552 | tf_op jit(solution)/shard_map/dot_general | solution.py:21
  160.4 40.5 %scan_forward.1 = (f32[1024,2048]{1,0:T(8,128)}, f32[1024,2304]{1,0:T(8,128)}, bf16[1024,2048]{1,0:T(8,128)(2,1)}) custom-call(f32[1024,2432]{1,0:T(8,128)} %fusion.38.xbc_ref, f32[1024,16]{1,0:T(8,128)S(1)} %copy.58.col_ref, f32[8,1024]{1,0:T(8,128)S(1)} %broadcast_in_dim.28.row_ref, f32[8,2304]{1,0:T(8,128)S(1)} %maximum_maximum_fusion.cw_ref, ...), custom_call_target="tpu_custom_call" | custom-call | flops 6000000000 | bytes 30000000 | tf_op jit(solution)/shard_map/scan_forward/pallas_call | solution.py:313
  201.6 3.9 pad_maximum_fusion.1
  205.5 7.2 %reshape.263 = bf16[2048,1024]{1,0:T(8,128)(2,1)} reshape(bf16[8,2,64,2048]{3,2,1,0:T(8,128)(2,1)} %get-tuple-element.61) | data formatting | bytes 8388608 | tf_op jit(solution)/shard_map/reshape | solution.py:485
  212.7 9.3 %fusion.36.z_ref = f32[1024,2048]{1,0:T(8,128)} fusion(bf16[1024,2048]{1,0:T(8,128)(2,1)} %bitcast.116, bf16[1024,1024]{1,0:T(8,128)(2,1)S(1)} %copy-done.6, f32[1024]{0:T(1024)S(1)} %slice_bitcast_fusion.3, f32[1024]{0:T(1024)S(1)} %add_rsqrt_fusion), kind=kOutput, calls=%fused_computation.110 | convolution fusion | flops 4299161600 | bytes 14688256 | tf_op jit(solution)/shard_map/dot_general | solution.py:21
  222.0 6.7 %convolution_bitcast_fusion.gm_ref = f32[1024,2048]{1,0:T(8,128)} fusion(bf16[2048,1024]{1,0:T(8,128)(2,1)S(1)} %copy-done.11, bf16[1024,1024]{1,0:T(8,128)(2,1)S(1)} %copy-done.14), kind=kOutput, calls=%fused_computation.19 | convolution fusion | flops 4294967296 | bytes 14680064 | tf_op jit(solution)/shard_map/dot_general | solution.py:25
  228.7 18.2 %gate.1 = (bf16[1024,2048]{1,0:T(8,128)(2,1)}, bf16[1024,2048]{1,0:T(8,128)(2,1)}, bf16[1024,2048]{1,0:T(8,128)(2,1)}, f32[8,2048]{1,0:T(8,128)S(1)}) custom-call(f32[1024,2048]{1,0:T(8,128)} %get-tuple-element.22.y_ref, f32[1024,2048]{1,0:T(8,128)} %fusion.36.z_ref, f32[1024,2048]{1,0:T(8,128)} %convolution_bitcast_fusion.gm_ref, ...), custom_call_target="tpu_custom_call" | custom-call | flops 100000000 | bytes 40000000 | tf_op jit(solution)/shard_map/gate/pallas_call | solution.py:383
  246.9 8.3 %convolution_convert_fusion.1 = bf16[2048,1024]{1,0:T(8,128)(2,1)} fusion(bf16[1024,2048]{1,0:T(8,128)(2,1)} %get-tuple-element.23, bf16[1024,1024]{1,0:T(8,128)(2,1)S(1)} %copy-done.14), kind=kOutput, calls=%fused_computation.37 | convolution fusion | flops 4297064448 | bytes 10485760 | tf_op jit(solution)/shard_map/dot_general | solution.py:514
  255.2 7.3 %reshape.269 = bf16[8,2,64,2048]{3,2,1,0:T(8,128)(2,1)} reshape(bf16[2048,1024]{1,0:T(8,128)(2,1)} %convolution_convert_fusion.1) | data formatting | bytes 8388608 | tf_op jit(solution)/shard_map/reshape | solution.py:516
  262.5 7.5 %convolution_convert_fusion.2 = bf16[1024,2048]{1,0:T(8,128)(2,1)S(1)} fusion(bf16[1024,2048]{1,0:T(8,128)(2,1)} %get-tuple-element.24, bf16[1024,1024]{1,0:T(8,128)(2,1)S(1)} %copy-done.6, f32[1024]{0:T(1024)S(1)} %slice_bitcast_fusion.3, f32[1024]{0:T(1024)S(1)} %add_rsqrt_fusion), kind=kOutput, calls=%fused_computation.38 | convolution fusion | flops 4301258752 | bytes 10493952 | tf_op jit(solution)/shard_map/dot_general | solution.py:514
  273.8 7.1 %collective-permute-done.7 = bf16[8,128,2048]{2,1,0:T(8,128)(2,1)} collective-permute-done((bf16[8,128,2048]{2,1,0:T(8,128)(2,1)}, bf16[8,128,2048]{2,1,0:T(8,128)(2,1)}, u32[]{:S(2)}, u32[]{:S(2)}) %collective-permute-start.7) | collective-permute-done | bytes 4194336 | tf_op jit(solution)/shard_map/ppermute | solution.py:422
  280.9 5.7 %fusion = bf16[8,128,2048]{2,1,0:T(8,128)(2,1)} fusion(bf16[8,128,2048]{2,1,0:T(8,128)(2,1)} %collective-permute-done.7, s32[]{:T(128)S(6)} %select_n.75, bf16[8,2,64,2048]{3,2,1,0:T(8,128)(2,1)} %bitcast.104, bf16[8,2,64,2048]{3,2,1,0:T(8,128)(2,1)} %reshape.269), kind=kLoop, calls=%fused_computation.7 | loop fusion | flops 16777216 | bytes 16777220 | tf_op jit(solution)/shard_map/convert_element_type | solution.py:438
  287.6 75.8 %scan_backward.1 = (bf16[1024,2432]{1,0:T(8,128)(2,1)}, f32[8,2304]{1,0:T(8,128)S(1)}, f32[8,128]{1,0:T(8,128)S(1)}, f32[8,2048]{1,0:T(8,128)S(1)}) custom-call(f32[1024,2432]{1,0:T(8,128)} %fusion.38.xbc_ref, f32[1024,2304]{1,0:T(8,128)} %get-tuple-element.25.pre_ref, f32[1024,2048]{1,0:T(8,128)} %get-tuple-element.22.y_ref, ...), custom_call_target="tpu_custom_call" | custom-call | flops 20000000000 | bytes 50000000 | tf_op jit(solution)/shard_map/scan_backward/pallas_call | solution.py:344
  363.4 8.6 %convolution_convert_fusion = bf16[1024,2432]{1,0:T(8,128)(2,1)S(1)} fusion(bf16[1024,2432]{1,0:T(8,128)(2,1)} %get-tuple-element.28, bf16[1024,1024]{1,0:T(8,128)(2,1)S(1)} %copy-done.7, f32[1024]{0:T(1024)S(1)} %slice_bitcast_fusion.3, f32[1024]{0:T(1024)S(1)} %add_rsqrt_fusion), kind=kOutput, calls=%fused_computation.15 | convolution fusion | flops 5106958336 | bytes 12066816 | tf_op jit(solution)/shard_map/dot_general | solution.py:514
  372.7 4.4 collective-permute-done.8
  380.0 9.1 %fusion.41 = f32[1024,1024]{1,0:T(8,128)S(1)} fusion(bf16[1024,2432]{1,0:T(8,128)(2,1)} %get-tuple-element.28, bf16[1024,2432]{1,0:T(8,128)(2,1)} %bitcast.109), kind=kOutput, calls=%fused_computation.113 | convolution fusion | flops 5100273664 | bytes 14155776 | tf_op jit(solution)/shard_map/dot_general | solution.py:25
  389.2 7.0 %fusion.12 = (f32[1024]{0:T(1024)S(1)}, f32[1024]{0:T(1024)S(1)}, f32[1024,1024]{1,0:T(8,128)}) fusion(bf16[1024,1024]{1,0:T(8,128)(2,1)S(1)} %copy-done.8, f32[1024]{0:T(1024)S(1)} %add_rsqrt_fusion, f32[1024]{0:T(1024)S(1)} %slice_bitcast_fusion.3, f32[1024,1024]{1,0:T(8,128)S(1)} %fusion.41, bf16[1024,2048]{1,0:T(8,128)(2,1)S(1)} %copy-done.18, ...), kind=kOutput, calls=%fused_computation.26 | convolution fusion | flops 4303353856 | bytes 18890752 | tf_op jit(solution)/shard_map/dot_general | solution.py:25
  400.2 47.2 %reduce-scatter.5.cloned.1.call-done = bf16[1,64,2432]{2,1,0:T(8,128)(2,1)} async-done(((bf16[8,64,2432]{2,1,0:T(8,128)(2,1)}), bf16[1,64,2432]{2,1,0:T(8,128)(2,1)}) %reduce-scatter.5.cloned.1.call-update) | async-done | bytes 311312 | tf_op jit(solution)/shard_map/reduce_scatter | solution.py:522
  450.0 9.5 %fusion.14 = bf16[1024,1024]{1,0:T(8,128)(2,1)} fusion(bf16[1024,1024]{1,0:T(8,128)(2,1)S(1)} %copy-done.8, bf16[1024,2048]{1,0:T(8,128)(2,1)} %get-tuple-element.23, bf16[2048,1024]{1,0:T(8,128)(2,1)} %reshape.263), kind=kOutput, calls=%fused_computation.28 | convolution fusion | flops 4298113024 | bytes 12582912 | tf_op jit(solution)/shard_map/dot_general | solution.py:21
  460.2 3.6 collective-permute-done.4
  469.6 3.7 collective-permute-done.6
  (175 shorter events, 48.3 us)
Async XLA Ops:
  7.2 65.9 %all-gather.5.cloned.1.call-start = ((), (), s32[]{:S(2)}) async-start(), calls=%async_computation.4 | async-start | bytes 2949120 | tf_op jit(solution)/shard_map/all_gather | solution.py:476
  15.6 132.2 %all-gather.7.cloned.1.call-start = ((), (), s32[]{:S(2)}) async-start(), calls=%async_computation.5 | async-start | bytes 4718592 | tf_op jit(solution)/shard_map/all_gather | solution.py:482
  16.1 60.9 %copy-start.6 = (bf16[1024,1024]{1,0:T(8,128)(2,1)S(1)}, bf16[1024,1024]{1,0:T(8,128)(2,1)}, u32[]{:S(2)}) copy-start(bf16[1024,1024]{1,0:T(8,128)(2,1)} %param.15) | copy-start | bytes 6291460
  17.1 382.0 %reduce-scatter.3.cloned.1.call-start = ((), (), s32[]{:S(2)}) async-start(), calls=%async_computation.2 | async-start | bytes 4718592 | tf_op jit(solution)/shard_map/reduce_scatter | solution.py:519
  76.5 71.4 %collective-permute-start = (bf16[8,64,2432]{2,1,0:T(8,128)(2,1)}, bf16[8,64,2432]{2,1,0:T(8,128)(2,1)}, u32[]{:S(2)}, u32[]{:S(2)}) collective-permute-start(bf16[8,64,2432]{2,1,0:T(8,128)(2,1)} %slice.210), channel_id=1, source_target_pairs={{0,8},{8,0},{16,24},{24,16},{1,9},{9,1},{17,25},{25,17},{2,10},{10... | collective-permute-start | bytes 7471112 | tf_op jit(solution)/shard_map/ppermute | solution.py:422
  147.8 53.1 %collective-permute-start.1 = (bf16[8,128,2048]{2,1,0:T(8,128)(2,1)}, bf16[8,128,2048]{2,1,0:T(8,128)(2,1)S(1)}, u32[]{:S(2)}, u32[]{:S(2)}) collective-permute-start(bf16[8,128,2048]{2,1,0:T(8,128)(2,1)} %bitcast.113), channel_id=1, source_target_pairs={{0,8},{8,0},{16,24},{24,16},{1,9},{9,1},{17,25},{25,17},{2,10},{10... | collective-permute-start | bytes 12582920 | tf_op jit(solution)/shard_map/ppermute | solution.py:422
  160.4 40.5 %copy-start.10 = (bf16[1024,2048]{1,0:T(8,128)(2,1)S(1)}, bf16[1024,2048]{1,0:T(8,128)(2,1)}, u32[]{:S(2)}) copy-start(bf16[1024,2048]{1,0:T(8,128)(2,1)} %all-gather.7.cloned.1.call-done) | copy-start | bytes 12582916
  212.7 9.3 %copy-start.11 = (bf16[2048,1024]{1,0:T(8,128)(2,1)S(1)}, bf16[2048,1024]{1,0:T(8,128)(2,1)}, u32[]{:S(2)}) copy-start(bf16[2048,1024]{1,0:T(8,128)(2,1)} %reshape.263) | copy-start | bytes 12582916
  212.7 9.3 %copy-start.14 = (bf16[1024,1024]{1,0:T(8,128)(2,1)S(1)}, bf16[1024,1024]{1,0:T(8,128)(2,1)}, u32[]{:S(2)}) copy-start(bf16[1024,1024]{1,0:T(8,128)(2,1)} %param.26) | copy-start | bytes 6291460
  273.2 7.6 %collective-permute-start.7 = (bf16[8,128,2048]{2,1,0:T(8,128)(2,1)}, bf16[8,128,2048]{2,1,0:T(8,128)(2,1)}, u32[]{:S(2)}, u32[]{:S(2)}) collective-permute-start(bf16[8,128,2048]{2,1,0:T(8,128)(2,1)} %fusion.17), channel_id=1, source_target_pairs={{0,8},{8,0},{16,24},{24,16},{1,9},{9,1},{17,25},{25,17},{2,10},{10... | collective-permute-start | bytes 12582920 | tf_op jit(solution)/shard_map/ppermute | solution.py:422
  286.6 160.8 %reduce-scatter.5.cloned.1.call-start = ((), (), s32[]{:S(2)}) async-start(), calls=%async_computation.3 | async-start | bytes 2801664 | tf_op jit(solution)/shard_map/reduce_scatter | solution.py:522
  287.6 75.8 %copy-start.7 = (bf16[1024,1024]{1,0:T(8,128)(2,1)S(1)}, bf16[1024,1024]{1,0:T(8,128)(2,1)}, u32[]{:S(2)}) copy-start(bf16[1024,1024]{1,0:T(8,128)(2,1)} %param.15) | copy-start | bytes 6291460
  372.3 4.8 collective-permute-start.8
  380.0 9.2 %copy-start.13 = (bf16[8,2,64,2048]{3,2,1,0:T(8,128)(2,1)S(1)}, bf16[8,2,64,2048]{3,2,1,0:T(8,128)(2,1)}, u32[]{:S(2)}) copy-start(bf16[8,2,64,2048]{3,2,1,0:T(8,128)(2,1)} %get-tuple-element.62) | copy-start | bytes 12582916
  380.0 9.2 %copy-start.18 = (bf16[1024,2048]{1,0:T(8,128)(2,1)S(1)}, bf16[1024,2048]{1,0:T(8,128)(2,1)}, u32[]{:S(2)}) copy-start(bf16[1024,2048]{1,0:T(8,128)(2,1)} %get-tuple-element.24) | copy-start | bytes 12582916
  396.3 1.3 collective-permute-start.2
  397.6 61.9 %collective-permute-start.3 = (f32[8,1836]{1,0:T(8,128)S(1)}, f32[8,1836]{1,0:T(8,128)S(1)}, u32[]{:S(2)}, u32[]{:S(2)}) collective-permute-start(f32[8,1836]{1,0:T(8,128)S(1)} %add.100), channel_id=1, source_target_pairs={{0,16},{8,24},{16,0},{24,8},{1,17},{9,25},{17,1},{25,9},{2,18},{10... | collective-permute-start | bytes 176264 | tf_op jit(solution)/shard_map/ppermute | solution.py:453
  448.4 16.4 %copy-start.12 = (f32[1024,1024]{1,0:T(8,128)S(1)}, f32[1024,1024]{1,0:T(8,128)}, u32[]{:S(2)}) copy-start(f32[1024,1024]{1,0:T(8,128)} %get-tuple-element.87) | copy-start | bytes 12582916
  448.4 16.4 %copy-start.15 = (bf16[1024,1024]{1,0:T(8,128)(2,1)S(1)}, bf16[1024,1024]{1,0:T(8,128)(2,1)}, u32[]{:S(2)}) copy-start(bf16[1024,1024]{1,0:T(8,128)(2,1)} %param.26) | copy-start | bytes 6291460
  448.4 20.9 %collective-permute-start.9 = (bf16[64,6528]{1,0:T(8,128)(2,1)S(1)}, bf16[64,6528]{1,0:T(8,128)(2,1)S(1)}, u32[]{:S(2)}, u32[]{:S(2)}) collective-permute-start(bf16[64,6528]{1,0:T(8,128)(2,1)S(1)} %pad_maximum_fusion.3), channel_id=1, source_target_pairs={{0,16},{8,24},{16,0},{24,8},{1,17},{9,25},{17,1},{25,9},{2,18},{10... | collective-permute-start | bytes 2506760 | tf_op jit(solution)/shard_map/ppermute | solution.py:444
  459.5 4.3 collective-permute-start.4
  463.8 4.3 collective-permute-start.5
  468.1 5.2 %collective-permute-start.6 = (f32[8,1836]{1,0:T(8,128)S(1)}, f32[8,1836]{1,0:T(8,128)S(1)}, u32[]{:S(2)}, u32[]{:S(2)}) collective-permute-start(f32[8,1836]{1,0:T(8,128)S(1)} %add.103), channel_id=1, source_target_pairs={{0,4},{1,5},{2,6},{3,7},{4,0},{5,1},{6,2},{7,3},{8,12},{9,13},{10,... | collective-permute-start | bytes 176264 | tf_op jit(solution)/shard_map/ppermute | solution.py:453
  469.6 6.8 %collective-permute-start.10 = (bf16[64,6528]{1,0:T(8,128)(2,1)S(1)}, bf16[64,6528]{1,0:T(8,128)(2,1)S(1)}, u32[]{:S(2)}, u32[]{:S(2)}) collective-permute-start(bf16[64,6528]{1,0:T(8,128)(2,1)S(1)} %add_convert_fusion), channel_id=1, source_target_pairs={{0,8},{8,0},{16,24},{24,16},{1,9},{9,1},{17,25},{25,17},{2,10},{10... | collective-permute-start | bytes 2506760 | tf_op jit(solution)/shard_map/ppermute | solution.py:422
  (11 other events, 67.4 us)
Sparse Core Ops, SparseCore 0:
  15.7 57.3 all-gather.4
  75.8 71.9 all-gather.6
  286.7 86.1 reduce-scatter.2
  379.3 68.0 reduce-scatter.4

commit v2 on v1

--- a/solution.py
+++ b/solution.py
@@ -46,9 +46,20 @@
     return jnp.maximum(v, 0.0) + jnp.log1p(jnp.exp(-jnp.abs(v)))
 
 
-def head_values(raw, col, hp_ref, ee_ref, a3_ref, at_ref, dtx_ref, esx_ref, tex_ref, keepx_ref):
+def sigmoid(v):
+    return 0.5 * jnp.tanh(0.5 * v) + 0.5
+
+
+def repeat_heads(raw):
+    lane = lax.broadcasted_iota(jnp.int32, raw.shape, 1)
+    once = jnp.where(lane < 32, raw, 0.0)
+    twice = once + pltpu.roll(once, 32, 1)
+    return twice + pltpu.roll(twice, 64, 1)
+
+
+def head_values(raw, col, hp_ref, ee_ref, at_ref, dtx_ref, esx_ref, tex_ref, keepx_ref):
     span = raw.shape[0]
-    shifted = raw + hp_ref[0:1, :]
+    shifted = repeat_heads(raw) + hp_ref[0:1, :]
     dt = softplus(shifted)
     rates = hp_ref[1:2, :] * dt
     row = lax.broadcasted_iota(jnp.int32, (span, span), 0)
@@ -56,20 +67,20 @@
     tri = jnp.where(row >= column, 1.0, 0.0).astype(F32)
     total = jnp.dot(tri, rates, precision=HIGH, preferred_element_type=F32)
     at_ref[...] = total.T
-    for head in range(a3_ref.shape[0]):
-        a3_ref[head] = jnp.broadcast_to(total[:, head : head + 1], a3_ref.shape[1:])
     last = total[span - 1 : span, :]
     ee = ee_ref[...]
     dtx_ref[...] = mm(split_lanes(dt), ee)
     esx_ref[...] = mm(split_lanes(jnp.exp(total) * col[:, 7:8]), ee)
     tex_ref[...] = mm(split_lanes(jnp.exp(last - total) * col[:, 8:9]), ee)
     keepx_ref[...] = mm(split_lanes(jnp.broadcast_to(jnp.exp(last) * col[0:1, 9:10], (8, LANES))), ee)
-    return shifted, rates
-
-
-def pair_decay(pair, a3_ref, at_ref):
-    column = jnp.concatenate([a3_ref[2 * pair], a3_ref[2 * pair + 1]], axis=1)
-    row = jnp.concatenate([at_ref[pl.ds(2 * pair, 1), :], at_ref[pl.ds(2 * pair + 1, 1), :]], axis=1)
+    return shifted, rates, total
+
+
+def pair_decay(pair, total, at_ref):
+    span = total.shape[0]
+    heads = (2 * pair, 2 * pair + 1)
+    column = jnp.concatenate([jnp.broadcast_to(total[:, h : h + 1], (span, span)) for h in heads], axis=1)
+    row = jnp.concatenate([at_ref[h : h + 1, :] for h in heads], axis=1)
     return column, row
 
 
@@ -77,7 +88,7 @@
     inner,
     xbc_ref, col_ref, row_ref, cw_ref, hp_ref, skip_ref, ee_ref,
     y_ref, pre_ref, sin_ref,
-    buf, state, a3_ref, at_ref, dtx_ref, esx_ref, tex_ref, keepx_ref, g2_ref,
+    buf, state, at_ref, dtx_ref, esx_ref, tex_ref, keepx_ref, g2_ref,
 ):
     span = y_ref.shape[0]
     mixed = pre_ref.shape[1]
@@ -94,17 +105,17 @@
 
     buf[8 : 8 + span, :] = xbc_ref[:, :mixed]
     col = col_ref[...]
-    head_values(
-        xbc_ref[:, mixed : mixed + LANES], col, hp_ref, ee_ref, a3_ref, at_ref, dtx_ref, esx_ref, tex_ref, keepx_ref
+    _, _, total = head_values(
+        xbc_ref[:, mixed : mixed + LANES], col, hp_ref, ee_ref, at_ref, dtx_ref, esx_ref, tex_ref, keepx_ref
     )
     same = [None] + [jnp.broadcast_to(col[:, k : k + 1], (span, LANES)) for k in (1, 2, 3)]
 
     def conv(lanes):
-        total = cw_ref[4:5, lanes] + cw_ref[3:4, lanes] * buf[8 : 8 + span, lanes]
+        pre = cw_ref[4:5, lanes] + cw_ref[3:4, lanes] * buf[8 : 8 + span, lanes]
         for k in (1, 2, 3):
-            total = total + cw_ref[3 - k : 4 - k, lanes] * (buf[8 - k : 8 - k + span, lanes] * same[k])
-        pre_ref[:, lanes] = total
-        return total * jax.nn.sigmoid(total)
+            pre = pre + cw_ref[3 - k : 4 - k, lanes] * (buf[8 - k : 8 - k + span, lanes] * same[k])
+        pre_ref[:, lanes] = pre
+        return pre * sigmoid(pre)
 
     b_f = conv(slice(inner, inner + LANES))
     c_b = conv(slice(inner + LANES, inner + 2 * LANES)).astype(BF)
@@ -116,11 +127,11 @@
     inter = jnp.where(linked, mm_nt(c_b, b_b), 0.0)
     g2_ref[...] = jnp.concatenate([inter, inter], axis=1)
 
-    def pair_step(pair, carry):
-        lanes = pl.ds(pl.multiple_of(pair * LANES, LANES), LANES)
+    def pair_step(pair):
+        lanes = slice(pair * LANES, (pair + 1) * LANES)
         x = conv(lanes)
         xd = x * dtx_ref[:, lanes]
-        column, row = pair_decay(pair, a3_ref, at_ref)
+        column, row = pair_decay(pair, total, at_ref)
         decay = jnp.exp(jnp.minimum(column - row, 0.0))
         inside = mm((g2_ref[...] * decay).astype(BF), block_diag(xd.astype(BF)))
         held = state[:, lanes]
@@ -128,16 +139,16 @@
         sin_ref[:, lanes] = held_b
         y_ref[:, lanes] = inside + mm(c_b, held_b) * esx_ref[:, lanes] + skip_ref[0:1, lanes] * x
         state[:, lanes] = held * keepx_ref[0:1, lanes] + mm(b_t, (xd * tex_ref[:, lanes]).astype(BF))
-        return carry
-
-    lax.fori_loop(0, inner // LANES, pair_step, 0, unroll=2)
+
+    for pair in range(inner // LANES):
+        pair_step(pair)
 
 
 def bwd_kernel(
     inner,
     xbc_ref, pre_ref, y_ref, gy_ref, sin_ref, col_ref, row_ref, cw_ref, hp_ref, skip_ref, ee_ref, rt_ref,
     gp_ref, cwg_ref, hpg_ref, skg_ref,
-    grad, halo, gstate, a3_ref, at_ref, dtx_ref, esx_ref, tex_ref, keepx_ref, gt2_ref, ggt_ref, gb_ref, gc_ref, acc_ref, kv_ref,
+    grad, halo, gstate, at_ref, dtx_ref, esx_ref, tex_ref, keepx_ref, gt2_ref, ggt_ref, gb_ref, gc_ref, acc_ref, kv_ref,
 ):
     span = y_ref.shape[0]
     mixed = pre_ref.shape[1]
@@ -152,8 +163,8 @@
         skg_ref[...] = jnp.zeros_like(skg_ref)
 
     col = col_ref[...]
-    shifted, rates = head_values(
-        xbc_ref[:, mixed : mixed + LANES], col, hp_ref, ee_ref, a3_ref, at_ref, dtx_ref, esx_ref, tex_ref, keepx_ref
+    shifted, rates, total = head_values(
+        xbc_ref[:, mixed : mixed + LANES], col, hp_ref, ee_ref, at_ref, dtx_ref, esx_ref, tex_ref, keepx_ref
     )
     ahead = [None] + [jnp.broadcast_to(col[:, 3 + k : 4 + k], (span, LANES)) for k in (1, 2, 3)]
 
@@ -173,7 +184,7 @@
 
     def act(lanes):
         pre = pre_ref[:, lanes]
-        sig = jax.nn.sigmoid(pre)
+        sig = sigmoid(pre)
         return pre * sig, sig * (1.0 + pre * (1.0 - sig))
 
     b_lanes, c_lanes = slice(inner, inner + LANES), slice(inner + LANES, inner + 2 * LANES)
@@ -191,8 +202,8 @@
     gc_ref[...] = jnp.zeros_like(gc_ref)
     acc_ref[...] = jnp.zeros_like(acc_ref)
 
-    def pair_step(pair, carry):
-        lanes = pl.ds(pl.multiple_of(pair * LANES, LANES), LANES)
+    def pair_step(pair):
+        lanes = slice(pair * LANES, (pair + 1) * LANES)
         x, slope = act(lanes)
         dtx, tex = dtx_ref[:, lanes], tex_ref[:, lanes]
         xd = x * dtx
@@ -200,7 +211,7 @@
         gy_b = gy_ref[:, lanes]
         gy = gy_b.astype(F32)
         diag = block_diag(gy_b)
-        column, row = pair_decay(pair, a3_ref, at_ref)
+        column, row = pair_decay(pair, total, at_ref)
         decay = jnp.exp(jnp.minimum(row - column, 0.0))
         linked_g = mm_nt(xd_b, diag) * decay
         ggt_ref[...] += linked_g[:, :span] + linked_g[:, span:]
@@ -225,10 +236,10 @@
         gb_ref[...] += mm_nt((xd * tex).astype(BF), gs_b)
         gstate[:, lanes] = keepx * gs + mm(c_t, scaled)
         conv_back(lanes, (dtx * gxd + skip * gy) * slope)
-        return carry
 
     kv_ref[...] = jnp.zeros_like(kv_ref)
-    lax.fori_loop(0, inner // LANES, pair_step, 0, unroll=2)
+    for pair in range(inner // LANES):
+        pair_step(pair)
     g_inter = jnp.where(linked, ggt_ref[...], 0.0)
     conv_back(b_lanes, (gb_ref[...] + mm(g_inter.astype(BF), c_b)) * b_slope)
     conv_back(c_lanes, (gc_ref[...] + mm(g_inter.T.astype(BF), b_b)) * c_slope)
@@ -238,7 +249,7 @@
     at_end = jnp.sum(acc_ref[span : 2 * span, :], axis=0, keepdims=True) + kept[0:1, :]
     tri = jnp.where(t_index >= s_index, 1.0, 0.0).astype(F32)
     g_rate = jnp.dot(tri, acc_ref[0:span, :], precision=HIGH, preferred_element_type=F32) + at_end
-    g_raw = (acc_ref[2 * span : 3 * span, :] + hp_ref[1:2, :] * g_rate) * jax.nn.sigmoid(shifted)
+    g_raw = (acc_ref[2 * span : 3 * span, :] + hp_ref[1:2, :] * g_rate) * sigmoid(shifted)
     gp_ref[:, mixed : mixed + LANES] = g_raw.astype(BF)
     hpg_ref[0:1, :] += jnp.sum(g_raw, axis=0, keepdims=True)
     hpg_ref[1:2, :] += jnp.sum(rates * g_rate, axis=0, keepdims=True)
@@ -256,14 +267,14 @@
     cross = jnp.zeros((rows, LANES), F32)
     for lanes in pieces:
         z = z_ref[:, lanes]
-        gated = y_ref[:, lanes] * (z * jax.nn.sigmoid(z))
+        gated = y_ref[:, lanes] * (z * sigmoid(z))
         square = square + gated * gated
         cross = cross + gated * (gm_ref[:, lanes] * gain_ref[0:1, lanes])
     inv = lax.rsqrt(jnp.sum(square, axis=1, keepdims=True) / inner + EPS)
     pull = inv * inv * inv * (jnp.sum(cross, axis=1, keepdims=True) / inner)
     for lanes in pieces:
         z, y, gm = z_ref[:, lanes], y_ref[:, lanes], gm_ref[:, lanes]
-        sig = jax.nn.sigmoid(z)
+        sig = sigmoid(z)
         silu = z * sig
         gated = y * silu
         gain = gain_ref[0:1, lanes]
@@ -294,9 +305,7 @@
 
 
 def common_scratch(inner):
-    heads = inner // WIDTH
     return [
-        pltpu.VMEM((heads, SPAN, LANES), F32),
         pltpu.VMEM((LANES, SPAN), F32),
         pltpu.VMEM((SPAN, inner), F32),
         pltpu.VMEM((SPAN, inner), F32),
@@ -455,10 +464,60 @@
     return value
 
 
+def add(*values):
+    return sum(v.astype(F32) for v in values).astype(BF)
+
+
+def gather_shards(value, shards):
+    if shards != 8:
+        return lax.all_gather(value, "shard", axis=0), value
+    member = lax.axis_index("shard")
+    z, y = member // 2, member % 2
+    got = [(0, value)]
+    for k in (1, 3, 2):
+        moves = [(i, (i + 2 * k) % 8) for i in range(8)]
+        got.append((k, lax.ppermute(value, "shard", moves)))
+    out = jnp.zeros((4, 2) + value.shape, value.dtype)
+    zero = (0,) * value.ndim
+    for k, block in got:
+        across = lax.ppermute(block, "shard", pairs(8, 1))
+        at = (z - k) % 4
+        out = lax.dynamic_update_slice(out, block[None, None], (at, y) + zero)
+        out = lax.dynamic_update_slice(out, across[None, None], (at, 1 - y) + zero)
+    return out.reshape((8,) + value.shape), got[1][1]
+
+
+ORDER = ((3, 2, 1, 0), (3, 2, 0, 1), (0, 1, 3, 2), (0, 1, 2, 3))
+
+
+def scatter_shards(value, shards):
+    if shards != 8:
+        return lax.psum_scatter(value, "shard", scatter_dimension=0)
+    member = lax.axis_index("shard")
+    z, y = member // 2, member % 2
+    order = lax.dynamic_index_in_dim(jnp.asarray(ORDER, jnp.int32), z, 0, keepdims=False)
+
+    def entry(i, side):
+        return lax.dynamic_index_in_dim(value, 2 * order[i] + side, 0, keepdims=False)
+
+    def move(block, steps):
+        return lax.ppermute(block, "shard", [(2 * a + s, 2 * b + s) for a, b in steps for s in (0, 1)])
+
+    across = [lax.ppermute(entry(i, 1 - y), "shard", pairs(8, 1)) for i in range(4)]
+    line = [add(entry(i, y), across[i]) for i in range(4)]
+    first = move(line[0], ((0, 1), (3, 2)))
+    second = jnp.where((z == 0) | (z == 3), line[1], add(line[0], first))
+    up = move(second, ((0, 1), (1, 2)))
+    down = move(second, ((3, 2), (2, 1)))
+    up = move(add(jnp.where(z == 1, line[1], line[2]), up), ((0, 1), (1, 2), (2, 3)))
+    down = move(add(jnp.where(z == 2, line[1], line[2]), down), ((3, 2), (2, 1), (1, 0)))
+    return add(line[3], up, down)
+
+
 def on_device(reps, shards, *args):
     (tokens, resets, norm_gain, in_weight, conv_weight, conv_bias, step_bias, decay_log, skip_gain, gate_gain,
      out_weight, cotangent) = args
-    rows, proj = in_weight.shape
+    rows = in_weight.shape[0]
     width = tokens.shape[1]
     inner = shards * gate_gain.shape[0]
     mixed = shards * conv_bias.shape[0]
@@ -466,23 +525,21 @@
     half = rows // 2
     core = lax.axis_index("rep") % 2
     member = lax.axis_index("shard")
+    barrier = lax.optimization_barrier
 
     small_parts = (norm_gain, conv_weight, conv_bias, step_bias, decay_log, skip_gain, gate_gain)
     small = jnp.concatenate([v.reshape(-1) for v in small_parts])
-    small = jnp.pad(small, (0, half * LANES - small.shape[0])).reshape(half, LANES)
-    dt_in = in_weight[:, inner + mixed :]
-    x_in = jnp.concatenate([in_weight[:, inner : inner + mixed]] + [dt_in] * (LANES // heads), axis=1)
-    x_own = lax.dynamic_slice_in_dim(x_in, core * half, half, 0)
-    x_all = lax.all_gather(jnp.concatenate([x_own, small], axis=1), "shard", axis=0)
-    x_width = mixed + LANES
-    w_x = swap_halves(x_all[:, :, :x_width], core, reps, 1).reshape(width, x_width)
-    small_all = x_all[:, :, x_width:].reshape(shards, -1).astype(F32)
-    z_own = lax.dynamic_slice_in_dim(in_weight[:, :inner], core * half, half, 0)
-    out_own = lax.dynamic_slice_in_dim(out_weight, core * 2 * half, 2 * half, 0).reshape(half, inner)
-    zo_all = lax.all_gather(jnp.concatenate([z_own, out_own], axis=0), "shard", axis=0)
-    zo = swap_halves(zo_all, core, reps, 1)
-    w_z = zo[:, :, :half].reshape(width, inner)
-    w_out = zo[:, :, half:].reshape(inner, width)
+    spare = LANES - heads
+    small = jnp.pad(small, (0, half * spare - small.shape[0])).reshape(half, spare)
+    small = jnp.pad(small, ((0, 0), (mixed + heads, 0)))
+    own_rows = lax.dynamic_slice_in_dim(in_weight, core * half, half, 0)
+    x_all, arrived = gather_shards(jnp.pad(own_rows[:, inner:], ((0, 0), (0, spare))) + small, shards)
+    w_x = swap_halves(x_all, core, reps, 1).reshape(width, mixed + LANES)
+    small_all = x_all[:, :, mixed + heads :].reshape(shards, -1).astype(F32)
+    out_own = lax.dynamic_slice_in_dim(out_weight, core * 2 * half, 2 * half, 0)
+    zo_own = jnp.concatenate([own_rows[:, :width], own_rows[:, width:inner], out_own], axis=0)
+    zo_own, _ = barrier((zo_own, arrived))
+    zo_all = lax.all_gather(zo_own, "shard", axis=0)
 
     full_small, at = [], 0
     for part in small_parts:
@@ -506,6 +563,10 @@
     normed = (inputs * inv_rms * gain[None, :]).astype(BF)
     xbc = mm(normed, w_x)
     y, pre, sin = scan_forward(xbc, col, row, cw8, hp8, sk8)
+    zo_all, y = barrier((zo_all, y))
+    zo = swap_halves(zo_all, core, reps, 1)
+    w_z = jnp.concatenate([zo[:, :, :half].reshape(width, width), zo[:, :, half : 2 * half].reshape(width, width)], axis=1)
+    w_out = zo[:, :, 2 * half :].reshape(inner, width)
     z = mm(normed, w_z)
     g_mixed = mm_nt(cotangent, w_out)
     mixed_out, gy, gz, gg_grad = gate(y, z, g_mixed, gg8)
@@ -513,13 +574,17 @@
     def grad_of(left, right):
         return lax.dot_general(left, right, (((0,), (0,)), ((), ())), preferred_element_type=F32).astype(BF)
 
-    out_grad = grad_of(mixed_out, cotangent).reshape(shards, 2, half, inner)
-    z_grad = grad_of(normed, gz).reshape(shards, 2, half, inner)
-    zo_sum = sum_cores(jnp.concatenate([z_grad, out_grad], axis=2), core, reps)
+    out_grad = sum_cores(grad_of(mixed_out, cotangent).reshape(shards, 2, 2 * half, width), core, reps)
+    z_grads = [
+        sum_cores(grad_of(normed, gz[:, k : k + width]).reshape(shards, 2, half, width), core, reps)
+        for k in (0, width)
+    ]
+    zo_sum, gy = barrier((jnp.concatenate(z_grads + [out_grad], axis=1), gy))
     zo_own = lax.psum_scatter(zo_sum, "shard", scatter_dimension=0)
     gp, cwg, hpg, skg = scan_backward(xbc, pre, y, gy, sin, col, row, cw8, hp8, sk8)
-    x_grad = grad_of(normed, gp).reshape(shards, 2, half, x_width)
-    x_own = lax.psum_scatter(sum_cores(x_grad, core, reps), "shard", scatter_dimension=0)
+    x_grad = grad_of(normed, gp).reshape(shards, 2, half, mixed + LANES)
+    zo_own, x_grad = barrier((zo_own, x_grad))
+    x_own = scatter_shards(sum_cores(x_grad, core, reps), shards)
     output = (inputs + mm(mixed_out, w_out)).astype(BF)
 
     g_normed = mm_nt(gz, w_z) + mm_nt(gp, w_x)
@@ -538,12 +603,17 @@
         small_grads.append(own[at : at + part.size].reshape(part.shape))
         at += part.size
 
-    both = jnp.concatenate([zo_own[:half], zo_own[half:], x_own], axis=1)
-    both = swap_halves(sum_reps(both, reps), core, reps, 0).astype(F32)
-    z_part = both[:, :, :inner].reshape(rows, inner)
-    out_part = both[:, :, inner : 2 * inner].reshape(out_weight.shape)
-    x_part = both[:, :, 2 * inner : 2 * inner + mixed + heads].reshape(rows, mixed + heads)
-    in_grad = jnp.concatenate([z_part, x_part], axis=1)
+    zo_own = swap_halves(sum_reps(zo_own, reps), core, reps, 0).astype(F32)
+    x_own = swap_halves(sum_reps(x_own, reps), core, reps, 0).astype(F32)
+    out_part = zo_own[:, 2 * half :].reshape(out_weight.shape)
+    in_grad = jnp.concatenate(
+        [
+            zo_own[:, :half].reshape(rows, width),
+            zo_own[:, half : 2 * half].reshape(rows, width),
+            x_own.reshape(rows, -1)[:, : mixed + heads],
+        ],
+        axis=1,
+    )
     return (output, input_grad, small_grads[0], in_grad, *small_grads[1:], out_part)
 
 

time: 499 us -> 381 us (0.76)
  waiting for transfers between devices: 191 us -> 91.9 us
  Pallas kernels: 135 us -> 95.1 us
  starting transfers between devices: 7.5 us -> 35.2 us
  matrix products: 74.7 us -> 66.5 us
    all_gather x2 -> x1, waiting for transfers between devices: 123 us -> 10.3 us  [on_device(): zo_all = lax.all_gather(zo_own, 'shard', axis=0)]
    reduce_scatter x1 -> x0, waiting for transfers between devices: 47.2 us -> none  [on_device(): lax.psum_scatter(sum_cores(x_grad, core, reps), 'shard', scatter_dimensio...]
    ppermute x0 -> x16, waiting for transfers between devices: none -> 39.9 us  [the longest x3 18 us: gather_shards(): got.append((k, lax.ppermute(value, 'shard', moves)))]
    ppermute x0 -> x16, starting transfers between devices: none -> 28.9 us  [the longest x5 15.8 us: move(): lax.ppermute(block, 'shard', [(2 * a + s, 2 * b + s) for a, b in steps fo...]
    pallas_call x1, Pallas kernels: 75.8 us -> 51.9 us  [scan_backward(): pl.pallas_call(partial(bwd_kernel, inner), grid=(blocks,), in_specs=[pl.B...]
    reduce_scatter x1, waiting for transfers between devices: 0.01 us -> 22.2 us  [on_device(): zo_own = lax.psum_scatter(zo_sum, 'shard', scatter_dimension=0)]
    reshape x5 -> x1, local copies, waits for them, and re-layouts: 16.9 us -> 0.09 us  [on_device(): jnp.pad(small, (0, half * spare - small.shape[0])).reshape(half, spare)]
    pallas_call x1, Pallas kernels: 40.5 us -> 24.3 us  [scan_forward(): pl.pallas_call(partial(fwd_kernel, inner), grid=(blocks,), in_specs=[pl.B...]
  transfers between devices with their start and end apart: 15 -> 33, of which waited for: 9 -> 18; matrix products, arithmetic and copies ran while one was open for 14% -> 21% of each run, Pallas kernels for 24% -> 20%
where the time goes in v2:
time: 381 us; the launch traced here: 376 us
  Pallas kernels  95.1 us (25%)
  waiting for transfers between devices  91.9 us (24%)
  matrix products  66.5 us (17%)
  local copies, waits for them, and re-layouts  37.7 us (10%)
  starting transfers between devices  35.2 us (9%)
  other arithmetic  31.6 us (8%)
  between operations  17.9 us (5%)
    pallas_call x1, Pallas kernels, scan_backward(): pl.pallas_call(partial(bwd_kernel, inner), grid=(blocks,), in_specs=[pl.B...  51.9 us
    pallas_call x1, Pallas kernels, scan_forward(): pl.pallas_call(partial(fwd_kernel, inner), grid=(blocks,), in_specs=[pl.B...  24.3 us
    dot_general x3, matrix products, mm_nt(): lax.dot_general(a, b, (((1,), (1,)), ((), ())), preferred_element_type=F32)  22.9 us
    dot_general x4, matrix products, grad_of(): lax.dot_general(left, right, (((0,), (0,)), ((), ())), preferred_element_...  22.2 us
    reduce_scatter x1, waiting for transfers between devices, on_device(): zo_own = lax.psum_scatter(zo_sum, 'shard', scatter_dimension=0)  22.2 us
    dot_general x3, matrix products, mm(): return jnp.dot(a, b, preferred_element_type=F32)  21.4 us
    pallas_call x1, Pallas kernels, gate(): pl.pallas_call(gate_kernel, grid=(length // rows,), in_specs=[block(), bl...  18.9 us
    ppermute x3, waiting for transfers between devices, gather_shards(): got.append((k, lax.ppermute(value, 'shard', moves)))  18 us
  transfers between devices with their start and end apart: 33, of which 18 were waited for; matrix products, arithmetic and copies ran while one was open for 21% of the time, Pallas kernels for 20%

profile of v2, /device:TPU:0, one launch (start us, length us, event | category | flops | bytes accessed | tf_op | source)
XLA Modules:
  0.0 376.0 jit_solution(2708114520555888985)
XLA Ops:
  9.7 4.1 %concatenate.34 = bf16[1836]{0:T(1024)(128)(2,1)S(1)} concatenate(bf16[128]{0:T(256)(128)(2,1)} %param.18, bf16[1152]{0:T(1024)(128)(2,1)S(1)} %reshape.289, bf16[288]{0:T(512)(128)(2,1)} %param.21, bf16[4]{0:T(256)(128)(2,1)} %param.22, bf16[4]{0:T(256)(128)(2,1)} %param.23, bf16[4]{0:T(256)(128)(2,1)} %param.24, bf16[256]{0:T(256)(128)(2,1)} %param.25), dimensions={0} | concatenate | bytes 7344 | tf_op jit(solution)/shard_map/concatenate | solution.py:531
  30.7 4.2 %collective-permute-done.3 = bf16[64,2432]{1,0:T(8,128)(2,1)} collective-permute-done((bf16[64,2432]{1,0:T(8,128)(2,1)}, bf16[64,2432]{1,0:T(8,128)(2,1)}, u32[]{:S(2)}, u32[]{:S(2)}) %collective-permute-start.3) | collective-permute-done | bytes 311328 | tf_op jit(solution)/shard_map/ppermute | solution.py:479
  35.5 13.4 %collective-permute-done.5 = bf16[64,2432]{1,0:T(8,128)(2,1)} collective-permute-done((bf16[64,2432]{1,0:T(8,128)(2,1)}, bf16[64,2432]{1,0:T(8,128)(2,1)}, u32[]{:S(2)}, u32[]{:S(2)}) %collective-permute-start.5) | collective-permute-done | bytes 311328 | tf_op jit(solution)/shard_map/ppermute | solution.py:479
  53.6 10.4 %collective-permute-done.6 = bf16[64,2432]{1,0:T(8,128)(2,1)S(1)} collective-permute-done((bf16[64,2432]{1,0:T(8,128)(2,1)}, bf16[64,2432]{1,0:T(8,128)(2,1)S(1)}, u32[]{:S(2)}, u32[]{:S(2)}) %collective-permute-start.6) | collective-permute-done | bytes 311328 | tf_op jit(solution)/shard_map/ppermute | solution.py:483
  73.0 8.8 %fusion.55.xbc_ref = f32[1024,2432]{1,0:T(8,128)} fusion(bf16[1024,2432]{1,0:T(8,128)(2,1)S(1)} %bitcast.156, bf16[1024,1024]{1,0:T(8,128)(2,1)S(1)} %copy-done.4, f32[1024]{0:T(1024)S(1)} %slice_bitcast_fusion.1, f32[1024]{0:T(1024)S(1)} %add_rsqrt_fusion), kind=kOutput, calls=%fused_computation.144 | convolution fusion | flops 5104467968 | bytes 17047552 | tf_op jit(solution)/shard_map/dot_general | solution.py:21
  81.8 24.3 %scan_forward.1 = (f32[1024,2048]{1,0:T(8,128)}, f32[1024,2304]{1,0:T(8,128)}, bf16[1024,2048]{1,0:T(8,128)(2,1)}) custom-call(f32[1024,2432]{1,0:T(8,128)} %fusion.55.xbc_ref, f32[1024,16]{1,0:T(8,128)S(1)} %copy.58.col_ref, f32[8,1024]{1,0:T(8,128)S(1)} %broadcast_in_dim.64.row_ref, f32[8,2304]{1,0:T(8,128)S(1)} %maximum_maximum_fusion.cw_ref, ...), custom_call_target="tpu_custom_call" | custom-call | flops 6000000000 | bytes 30000000 | tf_op jit(solution)/shard_map/scan_forward/pallas_call | solution.py:322
  106.1 10.3 %all-gather.3.cloned.1.call-done = bf16[2048,1024]{1,0:T(8,128)(2,1)} async-done(((bf16[256,1024]{1,0:T(8,128)(2,1)}), bf16[2048,1024]{1,0:T(8,128)(2,1)}) %all-gather.3.cloned.1.call-update) | async-done | bytes 4194320 | tf_op jit(solution)/shard_map/all_gather | solution.py:542
  116.5 7.4 %collective-permute-done.8 = bf16[8,256,1024]{2,1,0:T(8,128)(2,1)} collective-permute-done((bf16[8,256,1024]{2,1,0:T(8,128)(2,1)}, bf16[8,256,1024]{2,1,0:T(8,128)(2,1)}, u32[]{:S(2)}, u32[]{:S(2)}) %collective-permute-start.8) | collective-permute-done | bytes 4194336 | tf_op jit(solution)/shard_map/ppermute | solution.py:431
  123.9 3.8 %select_bitcast_fusion.1 = (bf16[8,1,256,1024]{3,2,1,0:T(8,128)(2,1)S(1)}, bf16[8,1,256,1024]{3,2,1,0:T(8,128)(2,1)S(1)}) fusion(bf16[8,256,1024]{2,1,0:T(8,128)(2,1)} %bitcast.163, bf16[8,256,1024]{2,1,0:T(8,128)(2,1)} %collective-permute-done.8, pred[]{:T(512)S(6)} %eq.78), kind=kLoop, calls=%fused_computation.27 | loop fusion | flops 4194304 | bytes 16777216 | tf_op jit(solution)/shard_map/stack | solution.py:437
  131.3 6.7 %convolution_bitcast_fusion.gm_ref = f32[1024,2048]{1,0:T(8,128)} fusion(bf16[2048,1024]{1,0:T(8,128)(2,1)S(1)} %bitcast.160, bf16[1024,1024]{1,0:T(8,128)(2,1)S(1)} %copy-done.15), kind=kOutput, calls=%fused_computation.11 | convolution fusion | flops 4294967296 | bytes 14680064 | tf_op jit(solution)/shard_map/dot_general | solution.py:25
  138.0 7.0 %fusion.16.z_ref = f32[1024,2048]{1,0:T(8,128)} fusion(bf16[1024,1024]{1,0:T(8,128)(2,1)S(1)} %bitcast.175, bf16[1024,1024]{1,0:T(8,128)(2,1)S(1)} %bitcast.173, bf16[1024,1024]{1,0:T(8,128)(2,1)S(1)} %copy-done.5, f32[1024]{0:T(1024)S(1)} %slice_bitcast_fusion.1, f32[1024]{0:T(1024)S(1)} %add_rsqrt_fusion), kind=kOutput, calls=%fused_computation.30 | convolution fusion | flops 4307550208 | bytes 14688256 | tf_op jit(solution)/shard_map/dot_general | solution.py:21
  144.9 18.9 %gate.1 = (bf16[1024,2048]{1,0:T(8,128)(2,1)}, bf16[1024,2048]{1,0:T(8,128)(2,1)}, bf16[1024,2048]{1,0:T(8,128)(2,1)}, f32[8,2048]{1,0:T(8,128)S(1)}) custom-call(f32[1024,2048]{1,0:T(8,128)} %get-tuple-element.31.y_ref, f32[1024,2048]{1,0:T(8,128)} %fusion.16.z_ref, f32[1024,2048]{1,0:T(8,128)} %convolution_bitcast_fusion.gm_ref, ...), custom_call_target="tpu_custom_call" | custom-call | flops 100000000 | bytes 40000000 | tf_op jit(solution)/shard_map/gate/pallas_call | solution.py:392
  163.8 4.3 %fusion.24 = bf16[1024,1024]{1,0:T(8,128)(2,1)S(1)} fusion(bf16[1024,2048]{1,0:T(8,128)(2,1)} %get-tuple-element.34, bf16[1024,1024]{1,0:T(8,128)(2,1)S(1)} %copy-done.5, f32[1024]{0:T(1024)S(1)} %slice_bitcast_fusion.1, f32[1024]{0:T(1024)S(1)} %add_rsqrt_fusion), kind=kOutput, calls=%fused_computation.47 | convolution fusion | flops 2152726528 | bytes 6299648 | tf_op jit(solution)/shard_map/dot_general | solution.py:575
  168.2 4.9 %convolution_convert_fusion.1 = bf16[2048,1024]{1,0:T(8,128)(2,1)S(1)} fusion(bf16[1024,2048]{1,0:T(8,128)(2,1)S(1)} %copy-done.27, bf16[1024,1024]{1,0:T(8,128)(2,1)S(1)} %copy-done.16), kind=kOutput, calls=%fused_computation.28 | convolution fusion | flops 4297064448 | bytes 10485760 | tf_op jit(solution)/shard_map/dot_general | solution.py:575
  193.4 51.9 %scan_backward.1 = (bf16[1024,2432]{1,0:T(8,128)(2,1)}, f32[8,2304]{1,0:T(8,128)S(1)}, f32[8,128]{1,0:T(8,128)S(1)}, f32[8,2048]{1,0:T(8,128)S(1)}) custom-call(f32[1024,2432]{1,0:T(8,128)} %fusion.55.xbc_ref, f32[1024,2304]{1,0:T(8,128)} %get-tuple-element.35.pre_ref, f32[1024,2048]{1,0:T(8,128)} %get-tuple-element.31.y_ref, ...), custom_call_target="tpu_custom_call" | custom-call | flops 20000000000 | bytes 50000000 | tf_op jit(solution)/shard_map/scan_backward/pallas_call | solution.py:353
  246.2 10.3 %convolution_convert_fusion = bf16[1024,2432]{1,0:T(8,128)(2,1)} fusion(bf16[1024,2432]{1,0:T(8,128)(2,1)} %get-tuple-element.39, bf16[1024,1024]{1,0:T(8,128)(2,1)} %param.16, f32[1024]{0:T(1024)S(1)} %slice_bitcast_fusion.1, f32[1024]{0:T(1024)S(1)} %add_rsqrt_fusion), kind=kOutput, calls=%fused_computation.7 | convolution fusion | flops 5106958336 | bytes 12066816 | tf_op jit(solution)/shard_map/dot_general | solution.py:575
  256.5 22.2 %reduce-scatter.2.cloned.1.call-done = bf16[1,256,1024]{2,1,0:T(8,128)(2,1)} async-done(((bf16[8,256,1024]{2,1,0:T(8,128)(2,1)}), bf16[1,256,1024]{2,1,0:T(8,128)(2,1)}) %reduce-scatter.2.cloned.1.call-update) | async-done | bytes 524304 | tf_op jit(solution)/shard_map/reduce_scatter | solution.py:583
  282.2 9.1 %fusion.60 = f32[1024,1024]{1,0:T(8,128)S(1)} fusion(bf16[1024,2432]{1,0:T(8,128)(2,1)} %get-tuple-element.39, bf16[1024,2432]{1,0:T(8,128)(2,1)} %bitcast.157), kind=kOutput, calls=%fused_computation.147 | convolution fusion | flops 5100273664 | bytes 14155776 | tf_op jit(solution)/shard_map/dot_general | solution.py:25
  291.3 7.0 %fusion.11 = (f32[1024]{0:T(1024)S(1)}, f32[1024]{0:T(1024)S(1)}, f32[1024,1024]{1,0:T(8,128)}) fusion(bf16[1024,1024]{1,0:T(8,128)(2,1)S(1)} %copy-done.6, f32[1024]{0:T(1024)S(1)} %add_rsqrt_fusion, f32[1024]{0:T(1024)S(1)} %slice_bitcast_fusion.1, f32[1024,1024]{1,0:T(8,128)S(1)} %fusion.60, bf16[1024,2048]{1,0:T(8,128)(2,1)S(1)} %copy-done.30, ...), kind=kOutput, calls=%fused_computation.18 | convolution fusion | flops 4311742464 | bytes 18890752 | tf_op jit(solution)/shard_map/dot_general | solution.py:25
  304.0 3.7 fusion.4
  309.4 5.7 %fusion.13 = bf16[1024,1024]{1,0:T(8,128)(2,1)} fusion(bf16[1024,1024]{1,0:T(8,128)(2,1)S(1)} %copy-done.6, bf16[1024,2048]{1,0:T(8,128)(2,1)S(1)} %copy-done.28, bf16[2048,1024]{1,0:T(8,128)(2,1)S(1)} %bitcast.161), kind=kOutput, calls=%fused_computation.20 | convolution fusion | flops 4298113024 | bytes 12582912 | tf_op jit(solution)/shard_map/dot_general | solution.py:21
  330.4 4.4 %collective-permute-start.25 = (bf16[64,2432]{1,0:T(8,128)(2,1)S(1)}, bf16[64,2432]{1,0:T(8,128)(2,1)S(1)}, u32[]{:S(2)}, u32[]{:S(2)}) collective-permute-start(bf16[64,2432]{1,0:T(8,128)(2,1)S(1)} %get-tuple-element.73), channel_id=1, source_target_pairs={{0,2},{1,3},{2,4},{3,5},{8,10},{9,11},{10,12},{11,13},{16,18},{17,... | collective-permute-start | bytes 933896 | tf_op jit(solution)/shard_map/ppermute | solution.py:504
  339.5 7.3 %collective-permute-start.26 = (bf16[64,2432]{1,0:T(8,128)(2,1)S(1)}, bf16[64,2432]{1,0:T(8,128)(2,1)S(1)}, u32[]{:S(2)}, u32[]{:S(2)}) collective-permute-start(bf16[64,2432]{1,0:T(8,128)(2,1)S(1)} %get-tuple-element.85), channel_id=1, source_target_pairs={{0,2},{1,3},{2,4},{3,5},{4,6},{5,7},{8,10},{9,11},{10,12},{11,13},... | collective-permute-start | bytes 933896 | tf_op jit(solution)/shard_map/ppermute | solution.py:504
  351.2 4.4 %collective-permute-done.28 = bf16[64,2432]{1,0:T(8,128)(2,1)S(1)} collective-permute-done((bf16[64,2432]{1,0:T(8,128)(2,1)S(1)}, bf16[64,2432]{1,0:T(8,128)(2,1)S(1)}, u32[]{:S(2)}, u32[]{:S(2)}) %collective-permute-start.28) | collective-permute-done | bytes 311328 | tf_op jit(solution)/shard_map/ppermute | solution.py:504
  (247 shorter events, 103.4 us)
Async XLA Ops:
  7.2 109.2 %all-gather.3.cloned.1.call-start = ((), (), s32[]{:S(2)}) async-start(), calls=%async_computation.2 | async-start | bytes 4718592 | tf_op jit(solution)/shard_map/all_gather | solution.py:542
  14.9 34.5 %collective-permute-start.1 = (bf16[64,2432]{1,0:T(8,128)(2,1)}, bf16[64,2432]{1,0:T(8,128)(2,1)}, u32[]{:S(2)}, u32[]{:S(2)}) collective-permute-start(bf16[64,2432]{1,0:T(8,128)(2,1)} %get-tuple-element.78), channel_id=1, source_target_pairs={{0,1},{1,0},{2,3},{3,2},{4,5},{5,4},{6,7},{7,6},{8,9},{9,8},{10,11... | collective-permute-start | bytes 933896 | tf_op jit(solution)/shard_map/ppermute | solution.py:483
  17.9 12.4 %collective-permute-start = (bf16[64,2432]{1,0:T(8,128)(2,1)}, bf16[64,2432]{1,0:T(8,128)(2,1)}, u32[]{:S(2)}, u32[]{:S(2)}) collective-permute-start(bf16[64,2432]{1,0:T(8,128)(2,1)} %get-tuple-element.78), channel_id=1, source_target_pairs={{0,2},{1,3},{2,4},{3,5},{4,6},{5,7},{6,0},{7,1},{8,10},{9,11},{10,... | collective-permute-start | bytes 933896 | tf_op jit(solution)/shard_map/ppermute | solution.py:479
  19.5 15.5 %collective-permute-start.3 = (bf16[64,2432]{1,0:T(8,128)(2,1)}, bf16[64,2432]{1,0:T(8,128)(2,1)}, u32[]{:S(2)}, u32[]{:S(2)}) collective-permute-start(bf16[64,2432]{1,0:T(8,128)(2,1)} %get-tuple-element.78), channel_id=1, source_target_pairs={{0,6},{1,7},{2,0},{3,1},{4,2},{5,3},{6,4},{7,5},{8,14},{9,15},{10,... | collective-permute-start | bytes 933896 | tf_op jit(solution)/shard_map/ppermute | solution.py:479
  21.7 27.2 %collective-permute-start.5 = (bf16[64,2432]{1,0:T(8,128)(2,1)}, bf16[64,2432]{1,0:T(8,128)(2,1)}, u32[]{:S(2)}, u32[]{:S(2)}) collective-permute-start(bf16[64,2432]{1,0:T(8,128)(2,1)} %get-tuple-element.78), channel_id=1, source_target_pairs={{0,4},{1,5},{2,6},{3,7},{4,0},{5,1},{6,2},{7,3},{8,12},{9,13},{10,... | collective-permute-start | bytes 933896 | tf_op jit(solution)/shard_map/ppermute | solution.py:479
  30.3 248.4 %reduce-scatter.2.cloned.1.call-start = ((), (), s32[]{:S(2)}) async-start(), calls=%async_computation.1 | async-start | bytes 4718592 | tf_op jit(solution)/shard_map/reduce_scatter | solution.py:583
  30.4 21.1 %collective-permute-start.2 = (bf16[64,2432]{1,0:T(8,128)(2,1)}, bf16[64,2432]{1,0:T(8,128)(2,1)S(1)}, u32[]{:S(2)}, u32[]{:S(2)}) collective-permute-start(bf16[64,2432]{1,0:T(8,128)(2,1)} %collective-permute-done), channel_id=1, source_target_pairs={{0,1},{1,0},{2,3},{3,2},{4,5},{5,4},{6,7},{7,6},{8,9},{9,8},{10,11... | collective-permute-start | bytes 933896 | tf_op jit(solution)/shard_map/ppermute | solution.py:483
  35.0 17.5 %collective-permute-start.4 = (bf16[64,2432]{1,0:T(8,128)(2,1)}, bf16[64,2432]{1,0:T(8,128)(2,1)S(1)}, u32[]{:S(2)}, u32[]{:S(2)}) collective-permute-start(bf16[64,2432]{1,0:T(8,128)(2,1)} %collective-permute-done.3), channel_id=1, source_target_pairs={{0,1},{1,0},{2,3},{3,2},{4,5},{5,4},{6,7},{7,6},{8,9},{9,8},{10,11... | collective-permute-start | bytes 933896 | tf_op jit(solution)/shard_map/ppermute | solution.py:483
  48.9 15.1 %collective-permute-start.6 = (bf16[64,2432]{1,0:T(8,128)(2,1)}, bf16[64,2432]{1,0:T(8,128)(2,1)S(1)}, u32[]{:S(2)}, u32[]{:S(2)}) collective-permute-start(bf16[64,2432]{1,0:T(8,128)(2,1)} %collective-permute-done.5), channel_id=1, source_target_pairs={{0,1},{1,0},{2,3},{3,2},{4,5},{5,4},{6,7},{7,6},{8,9},{9,8},{10,11... | collective-permute-start | bytes 933896 | tf_op jit(solution)/shard_map/ppermute | solution.py:483
  174.6 12.9 %collective-permute-start.11 = (bf16[8,128,1024]{2,1,0:T(8,128)(2,1)}, bf16[8,128,1024]{2,1,0:T(8,128)(2,1)}, u32[]{:S(2)}, u32[]{:S(2)}) collective-permute-start(bf16[8,128,1024]{2,1,0:T(8,128)(2,1)} %dynamic-slice_bitcast_fusion.1), channel_id=1, source_target_pairs={{0,8},{8,0},{16,24},{24,16},{1,9},{9,1},{17,25},{25,17},{2,10},{10... | collective-permute-start | bytes 6291464 | tf_op jit(solution)/shard_map/ppermute | solution.py:431
  174.9 7.8 %collective-permute-start.9 = (bf16[8,64,1024]{2,1,0:T(8,128)(2,1)S(1)}, bf16[8,64,1024]{2,1,0:T(8,128)(2,1)}, u32[]{:S(2)}, u32[]{:S(2)}) collective-permute-start(bf16[8,64,1024]{2,1,0:T(8,128)(2,1)S(1)} %dynamic-slice_bitcast_fusion.3), channel_id=1, source_target_pairs={{0,8},{8,0},{16,24},{24,16},{1,9},{9,1},{17,25},{25,17},{2,10},{10... | collective-permute-start | bytes 3145736 | tf_op jit(solution)/shard_map/ppermute | solution.py:431
  282.1 21.9 %collective-permute-start.19 = (bf16[8,64,2432]{2,1,0:T(8,128)(2,1)}, bf16[8,64,2432]{2,1,0:T(8,128)(2,1)}, u32[]{:S(2)}, u32[]{:S(2)}) collective-permute-start(bf16[8,64,2432]{2,1,0:T(8,128)(2,1)} %dynamic-slice_bitcast_fusion), channel_id=1, source_target_pairs={{0,8},{8,0},{16,24},{24,16},{1,9},{9,1},{17,25},{25,17},{2,10},{10... | collective-permute-start | bytes 7471112 | tf_op jit(solution)/shard_map/ppermute | solution.py:431
  302.4 12.6 %collective-permute-start.13 = (f32[8,1836]{1,0:T(8,128)S(1)}, f32[8,1836]{1,0:T(8,128)S(1)}, u32[]{:S(2)}, u32[]{:S(2)}) collective-permute-start(f32[8,1836]{1,0:T(8,128)S(1)} %add.264), channel_id=1, source_target_pairs={{0,16},{8,24},{16,0},{24,8},{1,17},{9,25},{17,1},{25,9},{2,18},{10... | collective-permute-start | bytes 176264 | tf_op jit(solution)/shard_map/ppermute | solution.py:462
  307.8 13.9 %collective-permute-start.23 = (bf16[64,2432]{1,0:T(8,128)(2,1)S(1)}, bf16[64,2432]{1,0:T(8,128)(2,1)S(1)}, u32[]{:S(2)}, u32[]{:S(2)}) collective-permute-start(bf16[64,2432]{1,0:T(8,128)(2,1)S(1)} %get-tuple-element.88), channel_id=1, source_target_pairs={{0,1},{1,0},{2,3},{3,2},{4,5},{5,4},{6,7},{7,6},{8,9},{9,8},{10,11... | collective-permute-start | bytes 933896 | tf_op jit(solution)/shard_map/ppermute | solution.py:506
  321.2 7.9 %collective-permute-start.21 = (bf16[64,2432]{1,0:T(8,128)(2,1)S(1)}, bf16[64,2432]{1,0:T(8,128)(2,1)S(1)}, u32[]{:S(2)}, u32[]{:S(2)}) collective-permute-start(bf16[64,2432]{1,0:T(8,128)(2,1)S(1)} %get-tuple-element.90), channel_id=1, source_target_pairs={{0,1},{1,0},{2,3},{3,2},{4,5},{5,4},{6,7},{7,6},{8,9},{9,8},{10,11... | collective-permute-start | bytes 933896 | tf_op jit(solution)/shard_map/ppermute | solution.py:506
  321.8 8.4 %collective-permute-start.24 = (bf16[64,2432]{1,0:T(8,128)(2,1)S(1)}, bf16[64,2432]{1,0:T(8,128)(2,1)S(1)}, u32[]{:S(2)}, u32[]{:S(2)}) collective-permute-start(bf16[64,2432]{1,0:T(8,128)(2,1)S(1)} %fusion.30), channel_id=1, source_target_pairs={{0,2},{1,3},{6,4},{7,5},{8,10},{9,11},{14,12},{15,13},{16,18},{17,... | collective-permute-start | bytes 933896 | tf_op jit(solution)/shard_map/ppermute | solution.py:504
  326.5 9.0 %collective-permute-start.16 = (f32[8,1836]{1,0:T(8,128)S(1)}, f32[8,1836]{1,0:T(8,128)S(1)}, u32[]{:S(2)}, u32[]{:S(2)}) collective-permute-start(f32[8,1836]{1,0:T(8,128)S(1)} %add.267), channel_id=1, source_target_pairs={{0,4},{1,5},{2,6},{3,7},{4,0},{5,1},{6,2},{7,3},{8,12},{9,13},{10,... | collective-permute-start | bytes 176264 | tf_op jit(solution)/shard_map/ppermute | solution.py:462
  326.7 10.0 %collective-permute-start.22 = (bf16[64,2432]{1,0:T(8,128)(2,1)S(1)}, bf16[64,2432]{1,0:T(8,128)(2,1)S(1)}, u32[]{:S(2)}, u32[]{:S(2)}) collective-permute-start(bf16[64,2432]{1,0:T(8,128)(2,1)S(1)} %get-tuple-element.89), channel_id=1, source_target_pairs={{0,1},{1,0},{2,3},{3,2},{4,5},{5,4},{6,7},{7,6},{8,9},{9,8},{10,11... | collective-permute-start | bytes 933896 | tf_op jit(solution)/shard_map/ppermute | solution.py:506
  330.4 8.8 %collective-permute-start.25 = (bf16[64,2432]{1,0:T(8,128)(2,1)S(1)}, bf16[64,2432]{1,0:T(8,128)(2,1)S(1)}, u32[]{:S(2)}, u32[]{:S(2)}) collective-permute-start(bf16[64,2432]{1,0:T(8,128)(2,1)S(1)} %get-tuple-element.73), channel_id=1, source_target_pairs={{0,2},{1,3},{2,4},{3,5},{8,10},{9,11},{10,12},{11,13},{16,18},{17,... | collective-permute-start | bytes 933896 | tf_op jit(solution)/shard_map/ppermute | solution.py:504
  336.1 12.8 %collective-permute-start.20 = (bf16[64,2432]{1,0:T(8,128)(2,1)S(1)}, bf16[64,2432]{1,0:T(8,128)(2,1)S(1)}, u32[]{:S(2)}, u32[]{:S(2)}) collective-permute-start(bf16[64,2432]{1,0:T(8,128)(2,1)S(1)} %get-tuple-element.87), channel_id=1, source_target_pairs={{0,1},{1,0},{2,3},{3,2},{4,5},{5,4},{6,7},{7,6},{8,9},{9,8},{10,11... | collective-permute-start | bytes 933896 | tf_op jit(solution)/shard_map/ppermute | solution.py:506
  339.5 11.7 %collective-permute-start.26 = (bf16[64,2432]{1,0:T(8,128)(2,1)S(1)}, bf16[64,2432]{1,0:T(8,128)(2,1)S(1)}, u32[]{:S(2)}, u32[]{:S(2)}) collective-permute-start(bf16[64,2432]{1,0:T(8,128)(2,1)S(1)} %get-tuple-element.85), channel_id=1, source_target_pairs={{0,2},{1,3},{2,4},{3,5},{4,6},{5,7},{8,10},{9,11},{10,12},{11,13},... | collective-permute-start | bytes 933896 | tf_op jit(solution)/shard_map/ppermute | solution.py:504
  346.8 8.8 %collective-permute-start.28 = (bf16[64,2432]{1,0:T(8,128)(2,1)S(1)}, bf16[64,2432]{1,0:T(8,128)(2,1)S(1)}, u32[]{:S(2)}, u32[]{:S(2)}) collective-permute-start(bf16[64,2432]{1,0:T(8,128)(2,1)S(1)} %get-tuple-element.86), channel_id=1, source_target_pairs={{6,4},{7,5},{4,2},{5,3},{2,0},{3,1},{14,12},{15,13},{12,10},{13,11... | collective-permute-start | bytes 933896 | tf_op jit(solution)/shard_map/ppermute | solution.py:504
  348.7 12.7 %collective-permute-start.17 = (bf16[256,1024]{1,0:T(8,128)(2,1)S(1)}, bf16[256,1024]{1,0:T(8,128)(2,1)S(1)}, u32[]{:S(2)}, u32[]{:S(2)}) collective-permute-start(bf16[256,1024]{1,0:T(8,128)(2,1)S(1)} %bitcast.178), channel_id=1, source_target_pairs={{0,16},{8,24},{16,0},{24,8},{1,17},{9,25},{17,1},{25,9},{2,18},{10... | collective-permute-start | bytes 1572872 | tf_op jit(solution)/shard_map/ppermute | solution.py:453
  355.7 9.0 %collective-permute-start.29 = (bf16[64,2432]{1,0:T(8,128)(2,1)S(1)}, bf16[64,2432]{1,0:T(8,128)(2,1)S(1)}, u32[]{:S(2)}, u32[]{:S(2)}) collective-permute-start(bf16[64,2432]{1,0:T(8,128)(2,1)S(1)} %add_convert_fusion.2), channel_id=1, source_target_pairs={{0,16},{8,24},{16,0},{24,8},{1,17},{9,25},{17,1},{25,9},{2,18},{10... | collective-permute-start | bytes 933896 | tf_op jit(solution)/shard_map/ppermute | solution.py:453
  (40 other events, 339.2 us)
Sparse Core Ops, SparseCore 0:
  30.5 85.8 all-gather.2
  192.5 86.1 reduce-scatter.1

commit v3 on v2

--- a/solution.py
+++ b/solution.py
@@ -255,21 +255,25 @@
     hpg_ref[1:2, :] += jnp.sum(rates * g_rate, axis=0, keepdims=True)
 
 
-def gate_kernel(y_ref, z_ref, gm_ref, gain_ref, out_ref, gy_ref, gz_ref, gg_ref):
+def gate_kernel(y_ref, normed_ref, dy_ref, wz_ref, wo_ref, gain_ref, out_ref, gy_ref, gz_ref, gg_ref, z_ref, gm_ref):
     rows, inner = y_ref.shape
 
     @pl.when(pl.program_id(0) == 0)
     def _():
         gg_ref[...] = jnp.zeros_like(gg_ref)
 
-    pieces = [slice(k, k + LANES) for k in range(0, inner, LANES)]
-    square = jnp.zeros((rows, LANES), F32)
-    cross = jnp.zeros((rows, LANES), F32)
+    pieces = [slice(k, k + 2 * LANES) for k in range(0, inner, 2 * LANES)]
+    square = jnp.zeros((rows, 2 * LANES), F32)
+    cross = jnp.zeros((rows, 2 * LANES), F32)
+    normed, dy = normed_ref[...], dy_ref[...]
     for lanes in pieces:
-        z = z_ref[:, lanes]
+        z = mm(normed, wz_ref[:, lanes])
+        gm = mm_nt(dy, wo_ref[lanes, :])
+        z_ref[:, lanes] = z
+        gm_ref[:, lanes] = gm
         gated = y_ref[:, lanes] * (z * sigmoid(z))
         square = square + gated * gated
-        cross = cross + gated * (gm_ref[:, lanes] * gain_ref[0:1, lanes])
+        cross = cross + gated * (gm * gain_ref[0:1, lanes])
     inv = lax.rsqrt(jnp.sum(square, axis=1, keepdims=True) / inner + EPS)
     pull = inv * inv * inv * (jnp.sum(cross, axis=1, keepdims=True) / inner)
     for lanes in pieces:
@@ -283,7 +287,7 @@
         gg_ref[0:1, lanes] += jnp.sum(gm * unit, axis=0, keepdims=True)
         g_gated = inv * (gm * gain) - gated * pull
         gy_ref[:, lanes] = (g_gated * silu).astype(BF)
-        gz_ref[:, lanes] = (g_gated * y * (sig * (1.0 + z * (1.0 - sig)))).astype(BF)
+        gz_ref[:, lanes] = (g_gated * y * (sig + silu * (1.0 - sig))).astype(BF)
 
 
 def full(shape):
@@ -385,20 +389,55 @@
     )(xbc, pre, y, gy, sin, col, row, cw, hp, skip, spread, collect)
 
 
-def gate(y, z, gm, gain):
+def gate(y, normed, dy, w_z, w_out, gain):
     length, inner = y.shape
-    rows = 128
-    block = lambda: pl.BlockSpec((rows, inner), lambda i: (i, 0))
+    width = normed.shape[1]
+    rows = 256
+    block = lambda columns: pl.BlockSpec((rows, columns), lambda i: (i, 0))
     return pl.pallas_call(
         gate_kernel,
         grid=(length // rows,),
-        in_specs=[block(), block(), block(), full((8, inner))],
-        out_specs=[block(), block(), block(), full((8, inner))],
+        in_specs=[
+            block(inner), block(width), block(width), full((width, inner)), full((inner, width)), full((8, inner)),
+        ],
+        out_specs=[block(inner), block(inner), block(inner), full((8, inner))],
         out_shape=[jax.ShapeDtypeStruct((length, inner), BF)] * 3 + [jax.ShapeDtypeStruct((8, inner), F32)],
+        scratch_shapes=[pltpu.VMEM((rows, inner), F32), pltpu.VMEM((rows, inner), F32)],
         compiler_params=PARAMS,
-        cost_estimate=pl.CostEstimate(flops=10**8, bytes_accessed=4 * 10**7, transcendentals=4 * 10**6),
+        cost_estimate=pl.CostEstimate(flops=9 * 10**9, bytes_accessed=4 * 10**7, transcendentals=4 * 10**6),
         name="gate",
-    )(y, z, gm, gain)
+    )(y, normed, dy, w_z, w_out, gain)
+
+
+def input_kernel(tokens_ref, dy_ref, gz_ref, gp_ref, wz_ref, wx_ref, gain_ref, out_ref, gg_ref):
+    @pl.when(pl.program_id(0) == 0)
+    def _():
+        gg_ref[...] = jnp.zeros_like(gg_ref)
+
+    g_normed = mm_nt(gz_ref[...], wz_ref[...]) + mm_nt(gp_ref[...], wx_ref[...])
+    inputs = tokens_ref[...].astype(F32)
+    inv = lax.rsqrt(jnp.mean(inputs * inputs, axis=1, keepdims=True) + EPS)
+    unit = inputs * inv
+    scaled = g_normed * gain_ref[0:1, :]
+    gg_ref[0:1, :] += jnp.sum(g_normed * unit, axis=0, keepdims=True)
+    pull = jnp.mean(scaled * unit, axis=1, keepdims=True)
+    out_ref[...] = (dy_ref[...].astype(F32) + inv * (scaled - unit * pull)).astype(BF)
+
+
+def input_gradient(tokens, dy, gz, gp, w_z, w_x, gain):
+    length, width = tokens.shape
+    rows = 256
+    block = lambda v: pl.BlockSpec((rows, v.shape[1]), lambda i: (i, 0))
+    return pl.pallas_call(
+        input_kernel,
+        grid=(length // rows,),
+        in_specs=[block(v) for v in (tokens, dy, gz, gp)] + [full(v.shape) for v in (w_z, w_x, gain)],
+        out_specs=[block(tokens), full((8, width))],
+        out_shape=[jax.ShapeDtypeStruct((length, width), BF), jax.ShapeDtypeStruct((8, width), F32)],
+        compiler_params=PARAMS,
+        cost_estimate=pl.CostEstimate(flops=10**7, bytes_accessed=10**5, transcendentals=0),
+        name="input_gradient",
+    )(tokens, dy, gz, gp, w_z, w_x, gain)
 
 
 def document_info(resets):
@@ -450,68 +489,70 @@
 def sum_reps(value, reps):
     flip = 2
     while flip < reps:
-        value = (value.astype(F32) + lax.ppermute(value, "rep", pairs(reps, flip)).astype(F32)).astype(BF)
+        value = add(value, lax.ppermute(value, "rep", pairs(reps, flip)))
         flip *= 2
     return value
 
 
-def sum_all(value, reps, shards):
-    for axis, size in (("rep", reps), ("shard", shards)):
-        flip = 1
-        while flip < size:
-            value = value + lax.ppermute(value, axis, pairs(size, flip))
-            flip *= 2
-    return value
-
-
-def add(*values):
-    return sum(v.astype(F32) for v in values).astype(BF)
-
-
-def gather_shards(value, shards):
+def gather_shards(value, small, shards):
     if shards != 8:
-        return lax.all_gather(value, "shard", axis=0), value
+        return lax.all_gather(value, "shard", axis=0), lax.all_gather(small, "shard", axis=0), value
     member = lax.axis_index("shard")
     z, y = member // 2, member % 2
-    got = [(0, value)]
-    for k in (1, 3, 2):
-        moves = [(i, (i + 2 * k) % 8) for i in range(8)]
-        got.append((k, lax.ppermute(value, "shard", moves)))
-    out = jnp.zeros((4, 2) + value.shape, value.dtype)
-    zero = (0,) * value.ndim
+
+    def from_behind(block, k):
+        return lax.ppermute(block, "shard", [(i, (i + 2 * k) % 8) for i in range(8)])
+
+    got = [(0, value)] + [(k, from_behind(value, k)) for k in (1, 3, 2)]
+    other = lax.ppermute(small, "shard", pairs(8, 1))
+    pair = jnp.stack([jnp.where(y == 0, small, other), jnp.where(y == 0, other, small)])
+    places = jnp.stack([pair] + [from_behind(pair, k) for k in (1, 2, 3)])
+    small_all = jnp.take(places, (z - jnp.arange(4)) % 4, axis=0).reshape((8,) + small.shape)
+    blank, arrived = lax.optimization_barrier((jnp.zeros((), value.dtype), got[1][1]))
+    got[1] = (1, arrived)
+    out = jnp.broadcast_to(blank, (4, 2) + value.shape)
+    start = (0,) * value.ndim
     for k, block in got:
         across = lax.ppermute(block, "shard", pairs(8, 1))
         at = (z - k) % 4
-        out = lax.dynamic_update_slice(out, block[None, None], (at, y) + zero)
-        out = lax.dynamic_update_slice(out, across[None, None], (at, 1 - y) + zero)
-    return out.reshape((8,) + value.shape), got[1][1]
-
-
-ORDER = ((3, 2, 1, 0), (3, 2, 0, 1), (0, 1, 3, 2), (0, 1, 2, 3))
-
-
-def scatter_shards(value, shards):
+        out = lax.dynamic_update_slice(out, block[None, None], (at, y) + start)
+        out = lax.dynamic_update_slice(out, across[None, None], (at, 1 - y) + start)
+        if k == 3:
+            out, small_all = lax.optimization_barrier((out, small_all))
+    return out.reshape((8,) + value.shape), small_all, arrived
+
+
+def along_z(value, z):
+    own = lax.dynamic_index_in_dim(value, z, 0, keepdims=False)
+    got = []
+    for k in (1, 3, 2):
+        entry = lax.dynamic_index_in_dim(value, (z + k) % 4, 0, keepdims=False)
+        got.append(lax.ppermute(entry, "shard", [(i, (i + 2 * k) % 8) for i in range(8)]))
+    return [own] + got
+
+
+def along_y(value, y, axis):
+    mine, theirs = half_of(value, y, axis)
+    return [mine, lax.ppermute(theirs, "shard", pairs(8, 1))]
+
+
+def add(*values):
+    return sum(v.astype(F32) for v in values).astype(values[0].dtype)
+
+
+def scatter_shards(first, second, shards, during):
     if shards != 8:
-        return lax.psum_scatter(value, "shard", scatter_dimension=0)
+        first, second = during(0, (first, second))
+        return during(1, tuple(lax.psum_scatter(v, "shard", scatter_dimension=0) for v in (first, second)))
     member = lax.axis_index("shard")
     z, y = member // 2, member % 2
-    order = lax.dynamic_index_in_dim(jnp.asarray(ORDER, jnp.int32), z, 0, keepdims=False)
-
-    def entry(i, side):
-        return lax.dynamic_index_in_dim(value, 2 * order[i] + side, 0, keepdims=False)
-
-    def move(block, steps):
-        return lax.ppermute(block, "shard", [(2 * a + s, 2 * b + s) for a, b in steps for s in (0, 1)])
-
-    across = [lax.ppermute(entry(i, 1 - y), "shard", pairs(8, 1)) for i in range(4)]
-    line = [add(entry(i, y), across[i]) for i in range(4)]
-    first = move(line[0], ((0, 1), (3, 2)))
-    second = jnp.where((z == 0) | (z == 3), line[1], add(line[0], first))
-    up = move(second, ((0, 1), (1, 2)))
-    down = move(second, ((3, 2), (2, 1)))
-    up = move(add(jnp.where(z == 1, line[1], line[2]), up), ((0, 1), (1, 2), (2, 3)))
-    down = move(add(jnp.where(z == 2, line[1], line[2]), down), ((3, 2), (2, 1), (1, 0)))
-    return add(line[3], up, down)
+    first = along_y(first.reshape((4, 2) + first.shape[1:]), y, 1)
+    second = along_z(second.reshape((4, 2) + second.shape[1:]), z)
+    first, second = during(0, (first, second))
+    first = along_z(add(*first), z)
+    second = along_y(add(*second), y, 0)
+    first, second = during(1, (first, second))
+    return add(*first), add(*second)
 
 
 def on_device(reps, shards, *args):
@@ -524,18 +565,15 @@
     heads = shards * step_bias.shape[0]
     half = rows // 2
     core = lax.axis_index("rep") % 2
-    member = lax.axis_index("shard")
     barrier = lax.optimization_barrier
 
     small_parts = (norm_gain, conv_weight, conv_bias, step_bias, decay_log, skip_gain, gate_gain)
     small = jnp.concatenate([v.reshape(-1) for v in small_parts])
-    spare = LANES - heads
-    small = jnp.pad(small, (0, half * spare - small.shape[0])).reshape(half, spare)
-    small = jnp.pad(small, ((0, 0), (mixed + heads, 0)))
+    small = jnp.pad(small, (0, -small.shape[0] % 1024)).reshape(-1, 1024)
     own_rows = lax.dynamic_slice_in_dim(in_weight, core * half, half, 0)
-    x_all, arrived = gather_shards(jnp.pad(own_rows[:, inner:], ((0, 0), (0, spare))) + small, shards)
+    x_all, small_all, arrived = gather_shards(jnp.pad(own_rows[:, inner:], ((0, 0), (0, LANES - heads))), small, shards)
     w_x = swap_halves(x_all, core, reps, 1).reshape(width, mixed + LANES)
-    small_all = x_all[:, :, mixed + heads :].reshape(shards, -1).astype(F32)
+    small_all = small_all.reshape(shards, -1).astype(F32)
     out_own = lax.dynamic_slice_in_dim(out_weight, core * 2 * half, 2 * half, 0)
     zo_own = jnp.concatenate([own_rows[:, :width], own_rows[:, width:inner], out_own], axis=0)
     zo_own, _ = barrier((zo_own, arrived))
@@ -567,9 +605,7 @@
     zo = swap_halves(zo_all, core, reps, 1)
     w_z = jnp.concatenate([zo[:, :, :half].reshape(width, width), zo[:, :, half : 2 * half].reshape(width, width)], axis=1)
     w_out = zo[:, :, 2 * half :].reshape(inner, width)
-    z = mm(normed, w_z)
-    g_mixed = mm_nt(cotangent, w_out)
-    mixed_out, gy, gz, gg_grad = gate(y, z, g_mixed, gg8)
+    mixed_out, gy, gz, gg_grad = gate(y, normed, cotangent, w_z, w_out, gg8)
 
     def grad_of(left, right):
         return lax.dot_general(left, right, (((0,), (0,)), ((), ())), preferred_element_type=F32).astype(BF)
@@ -582,29 +618,38 @@
     zo_sum, gy = barrier((jnp.concatenate(z_grads + [out_grad], axis=1), gy))
     zo_own = lax.psum_scatter(zo_sum, "shard", scatter_dimension=0)
     gp, cwg, hpg, skg = scan_backward(xbc, pre, y, gy, sin, col, row, cw8, hp8, sk8)
+    cut = (mixed + LANES) // (3 * LANES) * 2 * LANES
     x_grad = grad_of(normed, gp).reshape(shards, 2, half, mixed + LANES)
-    zo_own, x_grad = barrier((zo_own, x_grad))
-    x_own = scatter_shards(sum_cores(x_grad, core, reps), shards)
+    x_mine, x_theirs = half_of(x_grad, core, 1)
+    x_theirs = other_core(x_theirs, reps)
     output = (inputs + mm(mixed_out, w_out)).astype(BF)
-
-    g_normed = mm_nt(gz, w_z) + mm_nt(gp, w_x)
-    scaled = g_normed * gain[None, :]
-    unit = inputs * inv_rms
-    gain_grad = jnp.sum(g_normed * unit, axis=0)
-    back = cotangent.astype(F32) + inv_rms * (scaled - unit * jnp.mean(scaled * unit, axis=-1, keepdims=True))
-    input_grad = back.astype(BF)
+    x_theirs, output = barrier((x_theirs, output))
+    x_sums = [add(x_mine[:, :, s], x_theirs[:, :, s]) for s in (slice(0, cut), slice(cut, mixed + LANES))]
+    x_sums, gp = barrier((x_sums, gp))
+    input_grad, gain_grad = input_gradient(tokens, cotangent, gz, gp, w_z, w_x, rows8(gain))
+
+    def during(stage, value):
+        nonlocal input_grad, gain_grad, zo_own
+        if stage == 0:
+            value, input_grad, gain_grad, zo_own = barrier((value, input_grad, gain_grad, zo_own))
+        return value
+
+    x_parts = scatter_shards(*x_sums, shards, during)
+    gain_grad = gain_grad[0]
 
     grads = (cwg[:4], cwg[4], hpg[0, :heads], hpg[1, :heads], skg[0].reshape(heads, WIDTH).sum(axis=1), gg_grad[0])
     split = lambda v: jnp.moveaxis(v.reshape(v.shape[:-1] + (shards, -1)), -2, 0).reshape(shards, -1)
-    totals = sum_all(jnp.concatenate([split(v) for v in (gain_grad,) + grads], axis=1), reps, shards)
-    own = lax.dynamic_index_in_dim(totals, member, 0, keepdims=False)
+    own = jnp.concatenate([split(v) for v in (gain_grad,) + grads], axis=1)
+    own = own + other_core(own, reps)
+    own, _ = scatter_shards(own, own[:, :LANES], shards, lambda stage, value: value)
+    own = sum_reps(own, reps)
     small_grads, at = [], 0
     for part in small_parts:
         small_grads.append(own[at : at + part.size].reshape(part.shape))
         at += part.size
 
     zo_own = swap_halves(sum_reps(zo_own, reps), core, reps, 0).astype(F32)
-    x_own = swap_halves(sum_reps(x_own, reps), core, reps, 0).astype(F32)
+    x_own = swap_halves(sum_reps(jnp.concatenate(x_parts, axis=1), reps), core, reps, 0).astype(F32)
     out_part = zo_own[:, 2 * half :].reshape(out_weight.shape)
     in_grad = jnp.concatenate(
         [

time: 381 us -> 351 us (0.921)
  matrix products: 66.5 us -> 33.8 us
  Pallas kernels: 95.1 us -> 115 us
  waiting for transfers between devices: 91.9 us -> 75.8 us
  starting transfers between devices: 35.2 us -> 39.5 us
    dot_general x3 -> x0, matrix products: 22.9 us -> none  [mm_nt(): lax.dot_general(a, b, (((1,), (1,)), ((), ())), preferred_element_type=F32)]
    ppermute x19 -> x22, waiting for transfers between devices: 39.7 us -> 62.2 us  [the longest x9 25 us: along_z(): lax.ppermute(entry, 'shard', [(i, (i + 2 * k) % 8) for i in range(8)])]
    reduce_scatter x1, waiting for transfers between devices: 22.2 us -> 0.01 us  [on_device(): zo_own = lax.psum_scatter(zo_sum, 'shard', scatter_dimension=0)]
    pallas_call x1 -> x2, Pallas kernels: 18.9 us -> 39.7 us  [the longest x1 22.1 us: gate(): pl.pallas_call(gate_kernel, grid=(length // rows,), in_specs=[block(inner...]
    ppermute x4, waiting for transfers between devices: 10.5 us -> 0.46 us  [gather_shards(): across = lax.ppermute(block, 'shard', pairs(8, 1))]
    all_gather x1, waiting for transfers between devices: 10.3 us -> 1.16 us  [on_device(): zo_all = lax.all_gather(zo_own, 'shard', axis=0)]
    dot_general x3 -> x2, matrix products: 21.4 us -> 13.9 us  [mm(): return jnp.dot(a, b, preferred_element_type=F32)]
    dynamic_update_slice x7 -> x8, local copies, waits for them, and re-layouts: 4.13 us -> 9.04 us  [the longest x4 5.08 us: gather_shards(): out = lax.dynamic_update_slice(out, across[None, None], (at, 1 - y) + start)]
  transfers between devices with their start and end apart: 33 -> 37, of which waited for: 18 -> 18; matrix products, arithmetic and copies ran while one was open for 21% -> 18% of each run, Pallas kernels for 20% -> 27%
where the time goes in v3:
time: 351 us; the launch traced here: 345 us
  Pallas kernels  115 us (33%)
  waiting for transfers between devices  75.8 us (22%)
  starting transfers between devices  39.5 us (11%)
  local copies, waits for them, and re-layouts  35.8 us (10%)
  matrix products  33.8 us (10%)
  other arithmetic  29.6 us (8%)
  between operations  15.1 us (4%)
    pallas_call x1, Pallas kernels, scan_backward(): pl.pallas_call(partial(bwd_kernel, inner), grid=(blocks,), in_specs=[pl.B...  51.6 us
    ppermute x9, waiting for transfers between devices, along_z(): lax.ppermute(entry, 'shard', [(i, (i + 2 * k) % 8) for i in range(8)])  25 us
    ppermute x6, waiting for transfers between devices, from_behind(): lax.ppermute(block, 'shard', [(i, (i + 2 * k) % 8) for i in range(8)])  24.6 us
    pallas_call x1, Pallas kernels, scan_forward(): pl.pallas_call(partial(fwd_kernel, inner), grid=(blocks,), in_specs=[pl.B...  24.2 us
    pallas_call x1, Pallas kernels, gate(): pl.pallas_call(gate_kernel, grid=(length // rows,), in_specs=[block(inner...  22.1 us
    dot_general x4, matrix products, grad_of(): lax.dot_general(left, right, (((0,), (0,)), ((), ())), preferred_element_...  19.9 us
    pallas_call x1, Pallas kernels, input_gradient(): pl.pallas_call(input_kernel, grid=(length // rows,), in_specs=[block(v) f...  17.5 us
    ppermute x9, starting transfers between devices, along_z(): lax.ppermute(entry, 'shard', [(i, (i + 2 * k) % 8) for i in range(8)])  15.4 us
  transfers between devices with their start and end apart: 37, of which 18 were waited for; matrix products, arithmetic and copies ran while one was open for 18% of the time, Pallas kernels for 27%

profile of v3, /device:TPU:0, one launch (start us, length us, event | category | flops | bytes accessed | tf_op | source)
XLA Modules:
  0.0 345.0 jit_solution(10469227571889620161)
XLA Ops:
  9.7 3.0 collective-permute-start
  19.0 2.9 collective-permute-done.5
  26.7 3.2 collective-permute-start.3
  39.7 22.9 %collective-permute-done.9 = bf16[64,2432]{1,0:T(8,128)(2,1)S(1)} collective-permute-done((bf16[64,2432]{1,0:T(8,128)(2,1)}, bf16[64,2432]{1,0:T(8,128)(2,1)S(1)}, u32[]{:S(2)}, u32[]{:S(2)}) %collective-permute-start.9) | collective-permute-done | bytes 311328 | tf_op jit(solution)/shard_map/ppermute | solution.py:504
  75.2 2.9 select_bitcast_fusion.3
  78.7 8.2 %fusion.47.xbc_ref = f32[1024,2432]{1,0:T(8,128)} fusion(bf16[1024,1024]{1,0:T(8,128)(2,1)S(1)} %fusion.2.normed_ref, bf16[1024,2432]{1,0:T(8,128)(2,1)S(1)} %bitcast.164), kind=kOutput, calls=%fused_computation.160 | convolution fusion | flops 5100273664 | bytes 17039360 | tf_op jit(solution)/shard_map/dot_general | solution.py:21
  86.9 24.2 %scan_forward.1 = (f32[1024,2048]{1,0:T(8,128)}, f32[1024,2304]{1,0:T(8,128)}, bf16[1024,2048]{1,0:T(8,128)(2,1)}) custom-call(f32[1024,2432]{1,0:T(8,128)} %fusion.47.xbc_ref, f32[1024,16]{1,0:T(8,128)S(1)} %copy.57.col_ref, f32[8,1024]{1,0:T(8,128)S(1)} %broadcast_in_dim.82.row_ref, f32[8,2304]{1,0:T(8,128)S(1)} %maximum_maximum_fusion.cw_ref, ...), custom_call_target="tpu_custom_call" | custom-call | flops 6000000000 | bytes 30000000 | tf_op jit(solution)/shard_map/scan_forward/pallas_call | solution.py:326
  112.4 7.4 %collective-permute-done.12 = bf16[8,256,1024]{2,1,0:T(8,128)(2,1)} collective-permute-done((bf16[8,256,1024]{2,1,0:T(8,128)(2,1)}, bf16[8,256,1024]{2,1,0:T(8,128)(2,1)}, u32[]{:S(2)}, u32[]{:S(2)}) %collective-permute-start.12) | collective-permute-done | bytes 4194336 | tf_op jit(solution)/shard_map/ppermute | solution.py:470
  119.8 3.8 %select_bitcast_fusion.1 = (bf16[8,1,256,1024]{3,2,1,0:T(8,128)(2,1)S(1)}, bf16[8,1,256,1024]{3,2,1,0:T(8,128)(2,1)S(1)}) fusion(bf16[8,256,1024]{2,1,0:T(8,128)(2,1)} %bitcast.171, bf16[8,256,1024]{2,1,0:T(8,128)(2,1)} %collective-permute-done.12, pred[]{:T(512)S(6)} %eq.83), kind=kLoop, calls=%fused_computation.16 | loop fusion | flops 4194304 | bytes 16777216 | tf_op jit(solution)/shard_map/stack | solution.py:476
  129.2 22.1 %gate.1 = (bf16[1024,2048]{1,0:T(8,128)(2,1)}, bf16[1024,2048]{1,0:T(8,128)(2,1)}, bf16[1024,2048]{1,0:T(8,128)(2,1)}, f32[8,2048]{1,0:T(8,128)S(1)}) custom-call(f32[1024,2048]{1,0:T(8,128)} %get-tuple-element.54.y_ref, bf16[1024,1024]{1,0:T(8,128)(2,1)} %copy-done.13, bf16[1024,1024]{1,0:T(8,128)(2,1)} %dy_ref.3, ...), custom_call_target="tpu_custom_call" | custom-call | flops 8999999488 | bytes 40000000 | tf_op jit(solution)/shard_map/gate/pallas_call | solution.py:397
  151.4 4.1 %fusion.11 = bf16[1024,1024]{1,0:T(8,128)(2,1)S(1)} fusion(bf16[1024,1024]{1,0:T(8,128)(2,1)S(1)} %copy-done.14, bf16[1024,2048]{1,0:T(8,128)(2,1)} %get-tuple-element.56.gz_ref), kind=kOutput, calls=%fused_computation.35 | convolution fusion | flops 2148532224 | bytes 6291456 | tf_op jit(solution)/shard_map/dot_general | solution.py:611
  155.5 4.8 %convolution_convert_fusion.1 = bf16[2048,1024]{1,0:T(8,128)(2,1)S(1)} fusion(bf16[1024,2048]{1,0:T(8,128)(2,1)S(1)} %copy-done.26, bf16[1024,1024]{1,0:T(8,128)(2,1)S(1)} %copy-done.16), kind=kOutput, calls=%fused_computation.17 | convolution fusion | flops 4297064448 | bytes 10485760 | tf_op jit(solution)/shard_map/dot_general | solution.py:611
  179.6 51.6 %scan_backward.1 = (bf16[1024,2432]{1,0:T(8,128)(2,1)}, f32[8,2304]{1,0:T(8,128)S(1)}, f32[8,128]{1,0:T(8,128)S(1)}, f32[8,2048]{1,0:T(8,128)S(1)}) custom-call(f32[1024,2432]{1,0:T(8,128)} %fusion.47.xbc_ref, f32[1024,2304]{1,0:T(8,128)} %get-tuple-element.51.pre_ref, f32[1024,2048]{1,0:T(8,128)} %get-tuple-element.54.y_ref, ...), custom_call_target="tpu_custom_call" | custom-call | flops 20000000000 | bytes 50000000 | tf_op jit(solution)/shard_map/scan_backward/pallas_call | solution.py:357
  231.1 8.6 %convolution_convert_fusion = bf16[1024,2432]{1,0:T(8,128)(2,1)S(1)} fusion(bf16[1024,1024]{1,0:T(8,128)(2,1)S(1)} %copy-done.15, bf16[1024,2432]{1,0:T(8,128)(2,1)} %get-tuple-element.66.gp_ref), kind=kOutput, calls=%fused_computation.4 | convolution fusion | flops 5102764032 | bytes 12058624 | tf_op jit(solution)/shard_map/dot_general | solution.py:611
  242.6 5.7 %fusion.3 = bf16[1024,1024]{1,0:T(8,128)(2,1)} fusion(bf16[1024,1024]{1,0:T(8,128)(2,1)S(1)} %copy-done.6, bf16[1024,2048]{1,0:T(8,128)(2,1)S(1)} %copy-done.27, bf16[2048,1024]{1,0:T(8,128)(2,1)S(1)} %bitcast.173), kind=kOutput, calls=%fused_computation.9 | convolution fusion | flops 4298113024 | bytes 12582912 | tf_op jit(solution)/shard_map/dot_general | solution.py:21
  251.9 4.3 %collective-permute-start.18 = (bf16[2,64,896]{2,1,0:T(8,128)(2,1)}, bf16[2,64,896]{2,1,0:T(8,128)(2,1)S(1)}, u32[]{:S(2)}, u32[]{:S(2)}) collective-permute-start(bf16[2,64,896]{2,1,0:T(8,128)(2,1)} %get-tuple-element.131), channel_id=1, source_target_pairs={{0,2},{1,3},{2,4},{3,5},{4,6},{5,7},{6,0},{7,1},{8,10},{9,11},{10,... | collective-permute-start | bytes 688136 | tf_op jit(solution)/shard_map/ppermute | solution.py:530
  259.9 17.5 %input_gradient.1 = (bf16[1024,1024]{1,0:T(8,128)(2,1)}, f32[8,1024]{1,0:T(8,128)S(1)}) custom-call(bf16[1024,1024]{1,0:T(8,128)(2,1)} %tokens_ref.1, bf16[1024,1024]{1,0:T(8,128)(2,1)} %dy_ref.3, bf16[1024,2048]{1,0:T(8,128)(2,1)} %get-tuple-element.56.gz_ref, bf16[1024,2432]{1,0:T(8,128)(2,1)} %get-tuple-element.66.gp_ref, ...), custom_call_target="tpu_custom_call" | custom-call | flops 10000000 | bytes 100000 | tf_op jit(solution)/shard_map/input_gradient/pallas_call | solution.py:431
  278.0 12.0 %collective-permute-done.20 = bf16[2,64,896]{2,1,0:T(8,128)(2,1)} collective-permute-done((bf16[2,64,896]{2,1,0:T(8,128)(2,1)}, bf16[2,64,896]{2,1,0:T(8,128)(2,1)}, u32[]{:S(2)}, u32[]{:S(2)}) %collective-permute-start.20) | collective-permute-done | bytes 229408 | tf_op jit(solution)/shard_map/ppermute | solution.py:530
  290.9 3.8 %collective-permute-start.30 = (bf16[64,1536]{1,0:T(8,128)(2,1)S(1)}, bf16[64,1536]{1,0:T(8,128)(2,1)S(1)}, u32[]{:S(2)}, u32[]{:S(2)}) collective-permute-start(bf16[64,1536]{1,0:T(8,128)(2,1)S(1)} %get-tuple-element.135), channel_id=1, source_target_pairs={{0,6},{1,7},{2,0},{3,1},{4,2},{5,3},{6,4},{7,5},{8,14},{9,15},{10,... | collective-permute-start | bytes 589832 | tf_op jit(solution)/shard_map/ppermute | solution.py:530
  298.2 3.6 %collective-permute-done.32 = bf16[64,896]{1,0:T(8,128)(2,1)S(1)} collective-permute-done((bf16[64,896]{1,0:T(8,128)(2,1)S(1)}, bf16[64,896]{1,0:T(8,128)(2,1)S(1)}, u32[]{:S(2)}, u32[]{:S(2)}) %collective-permute-start.32) | collective-permute-done | bytes 114720 | tf_op jit(solution)/shard_map/ppermute | solution.py:536
  303.7 6.1 %collective-permute-done.31 = bf16[64,1536]{1,0:T(8,128)(2,1)} collective-permute-done((bf16[64,1536]{1,0:T(8,128)(2,1)S(1)}, bf16[64,1536]{1,0:T(8,128)(2,1)}, u32[]{:S(2)}, u32[]{:S(2)}) %collective-permute-start.31) | collective-permute-done | bytes 196640 | tf_op jit(solution)/shard_map/ppermute | solution.py:530
  312.9 3.8 %collective-permute-start.24 = (f32[1836]{0:T(1024)S(1)}, f32[1836]{0:T(1024)S(1)}, u32[]{:S(2)}, u32[]{:S(2)}) collective-permute-start(f32[1836]{0:T(1024)S(1)} %get-tuple-element.107), channel_id=1, source_target_pairs={{0,6},{1,7},{2,0},{3,1},{4,2},{5,3},{6,4},{7,5},{8,14},{9,15},{10,... | collective-permute-start | bytes 22040 | tf_op jit(solution)/shard_map/ppermute | solution.py:530
  318.3 2.9 collective-permute-done.25
  328.2 4.2 %collective-permute-done.27 = bf16[256,1024]{1,0:T(8,128)(2,1)S(1)} collective-permute-done((bf16[256,1024]{1,0:T(8,128)(2,1)S(1)}, bf16[256,1024]{1,0:T(8,128)(2,1)S(1)}, u32[]{:S(2)}, u32[]{:S(2)}) %collective-permute-start.27) | collective-permute-done | bytes 524320 | tf_op jit(solution)/shard_map/ppermute | solution.py:492
  (266 shorter events, 96.2 us)
Async XLA Ops:
  7.3 105.0 %all-gather.3.cloned.1.call-start = ((), (), s32[]{:S(2)}) async-start(), calls=%async_computation.2 | async-start | bytes 4718592 | tf_op jit(solution)/shard_map/all_gather | solution.py:580
  9.7 22.7 %collective-permute-start = (bf16[64,2432]{1,0:T(8,128)(2,1)}, bf16[64,2432]{1,0:T(8,128)(2,1)S(1)}, u32[]{:S(2)}, u32[]{:S(2)}) collective-permute-start(bf16[64,2432]{1,0:T(8,128)(2,1)} %pad.35), channel_id=1, source_target_pairs={{0,2},{1,3},{2,4},{3,5},{4,6},{5,7},{6,0},{7,1},{8,10},{9,11},{10,... | collective-permute-start | bytes 933896 | tf_op jit(solution)/shard_map/ppermute | solution.py:504
  12.8 23.8 %collective-permute-start.1 = (bf16[64,2432]{1,0:T(8,128)(2,1)}, bf16[64,2432]{1,0:T(8,128)(2,1)}, u32[]{:S(2)}, u32[]{:S(2)}) collective-permute-start(bf16[64,2432]{1,0:T(8,128)(2,1)} %pad.35), channel_id=1, source_target_pairs={{0,1},{1,0},{2,3},{3,2},{4,5},{5,4},{6,7},{7,6},{8,9},{9,8},{10,11... | collective-permute-start | bytes 933896 | tf_op jit(solution)/shard_map/ppermute | solution.py:516
  14.5 7.4 %collective-permute-start.5 = (bf16[2,1024]{1,0:T(2,128)(2,1)S(1)}, bf16[2,1024]{1,0:T(2,128)(2,1)S(1)}, u32[]{:S(2)}, u32[]{:S(2)}) collective-permute-start(bf16[2,1024]{1,0:T(2,128)(2,1)S(1)} %reshape.319), channel_id=1, source_target_pairs={{0,1},{1,0},{2,3},{3,2},{4,5},{5,4},{6,7},{7,6},{8,9},{9,8},{10,11... | collective-permute-start | bytes 12296 | tf_op jit(solution)/shard_map/ppermute | solution.py:507
  26.7 12.4 %collective-permute-start.3 = (bf16[64,2432]{1,0:T(8,128)(2,1)}, bf16[64,2432]{1,0:T(8,128)(2,1)}, u32[]{:S(2)}, u32[]{:S(2)}) collective-permute-start(bf16[64,2432]{1,0:T(8,128)(2,1)} %pad.35), channel_id=1, source_target_pairs={{0,6},{1,7},{2,0},{3,1},{4,2},{5,3},{6,4},{7,5},{8,14},{9,15},{10,... | collective-permute-start | bytes 933896 | tf_op jit(solution)/shard_map/ppermute | solution.py:504
  29.9 32.6 %collective-permute-start.9 = (bf16[64,2432]{1,0:T(8,128)(2,1)}, bf16[64,2432]{1,0:T(8,128)(2,1)S(1)}, u32[]{:S(2)}, u32[]{:S(2)}) collective-permute-start(bf16[64,2432]{1,0:T(8,128)(2,1)} %pad.35), channel_id=1, source_target_pairs={{0,4},{1,5},{2,6},{3,7},{4,0},{5,1},{6,2},{7,3},{8,12},{9,13},{10,... | collective-permute-start | bytes 933896 | tf_op jit(solution)/shard_map/ppermute | solution.py:504
  32.5 31.6 %collective-permute-start.2 = (bf16[64,2432]{1,0:T(8,128)(2,1)S(1)}, bf16[64,2432]{1,0:T(8,128)(2,1)}, u32[]{:S(2)}, u32[]{:S(2)}) collective-permute-start(bf16[64,2432]{1,0:T(8,128)(2,1)S(1)} %collective-permute-done), channel_id=1, source_target_pairs={{0,1},{1,0},{2,3},{3,2},{4,5},{5,4},{6,7},{7,6},{8,9},{9,8},{10,11... | collective-permute-start | bytes 933896 | tf_op jit(solution)/shard_map/ppermute | solution.py:516
  34.1 255.9 %reduce-scatter.2.cloned.1.call-start = ((), (), s32[]{:S(2)}) async-start(), calls=%async_computation.1 | async-start | bytes 4718592 | tf_op jit(solution)/shard_map/reduce_scatter | solution.py:619
  39.1 28.4 %collective-permute-start.4 = (bf16[64,2432]{1,0:T(8,128)(2,1)}, bf16[64,2432]{1,0:T(8,128)(2,1)S(1)}, u32[]{:S(2)}, u32[]{:S(2)}) collective-permute-start(bf16[64,2432]{1,0:T(8,128)(2,1)} %collective-permute-done.3), channel_id=1, source_target_pairs={{0,1},{1,0},{2,3},{3,2},{4,5},{5,4},{6,7},{7,6},{8,9},{9,8},{10,11... | collective-permute-start | bytes 933896 | tf_op jit(solution)/shard_map/ppermute | solution.py:516
  62.5 6.9 %collective-permute-start.10 = (bf16[64,2432]{1,0:T(8,128)(2,1)S(1)}, bf16[64,2432]{1,0:T(8,128)(2,1)S(1)}, u32[]{:S(2)}, u32[]{:S(2)}) collective-permute-start(bf16[64,2432]{1,0:T(8,128)(2,1)S(1)} %collective-permute-done.9), channel_id=1, source_target_pairs={{0,1},{1,0},{2,3},{3,2},{4,5},{5,4},{6,7},{7,6},{8,9},{9,8},{10,11... | collective-permute-start | bytes 933896 | tf_op jit(solution)/shard_map/ppermute | solution.py:516
  112.3 7.5 %collective-permute-start.12 = (bf16[8,256,1024]{2,1,0:T(8,128)(2,1)}, bf16[8,256,1024]{2,1,0:T(8,128)(2,1)}, u32[]{:S(2)}, u32[]{:S(2)}) collective-permute-start(bf16[8,256,1024]{2,1,0:T(8,128)(2,1)} %bitcast.170), channel_id=1, source_target_pairs={{0,8},{8,0},{16,24},{24,16},{1,9},{9,1},{17,25},{25,17},{2,10},{10... | collective-permute-start | bytes 12582920 | tf_op jit(solution)/shard_map/ppermute | solution.py:470
  162.0 11.8 %collective-permute-start.15 = (bf16[8,128,1024]{2,1,0:T(8,128)(2,1)}, bf16[8,128,1024]{2,1,0:T(8,128)(2,1)}, u32[]{:S(2)}, u32[]{:S(2)}) collective-permute-start(bf16[8,128,1024]{2,1,0:T(8,128)(2,1)} %dynamic-slice_bitcast_fusion.2), channel_id=1, source_target_pairs={{0,8},{8,0},{16,24},{24,16},{1,9},{9,1},{17,25},{25,17},{2,10},{10... | collective-permute-start | bytes 6291464 | tf_op jit(solution)/shard_map/ppermute | solution.py:470
  240.2 8.1 %collective-permute-start.16 = (bf16[8,64,2432]{2,1,0:T(8,128)(2,1)S(1)}, bf16[8,64,2432]{2,1,0:T(8,128)(2,1)S(1)}, u32[]{:S(2)}, u32[]{:S(2)}) collective-permute-start(bf16[8,64,2432]{2,1,0:T(8,128)(2,1)S(1)} %get-tuple-element.118), channel_id=1, source_target_pairs={{0,8},{8,0},{16,24},{24,16},{1,9},{9,1},{17,25},{25,17},{2,10},{10... | collective-permute-start | bytes 7471112 | tf_op jit(solution)/shard_map/ppermute | solution.py:470
  249.9 40.1 %collective-permute-start.17 = (bf16[4,64,1536]{2,1,0:T(8,128)(2,1)}, bf16[4,64,1536]{2,1,0:T(8,128)(2,1)S(1)}, u32[]{:S(2)}, u32[]{:S(2)}) collective-permute-start(bf16[4,64,1536]{2,1,0:T(8,128)(2,1)} %get-tuple-element.121), channel_id=1, source_target_pairs={{0,1},{1,0},{2,3},{3,2},{4,5},{5,4},{6,7},{7,6},{8,9},{9,8},{10,11... | collective-permute-start | bytes 2359304 | tf_op jit(solution)/shard_map/ppermute | solution.py:536
  251.9 25.5 %collective-permute-start.18 = (bf16[2,64,896]{2,1,0:T(8,128)(2,1)}, bf16[2,64,896]{2,1,0:T(8,128)(2,1)S(1)}, u32[]{:S(2)}, u32[]{:S(2)}) collective-permute-start(bf16[2,64,896]{2,1,0:T(8,128)(2,1)} %get-tuple-element.131), channel_id=1, source_target_pairs={{0,2},{1,3},{2,4},{3,5},{4,6},{5,7},{6,0},{7,1},{8,10},{9,11},{10,... | collective-permute-start | bytes 688136 | tf_op jit(solution)/shard_map/ppermute | solution.py:530
  256.1 21.8 %collective-permute-start.19 = (bf16[2,64,896]{2,1,0:T(8,128)(2,1)}, bf16[2,64,896]{2,1,0:T(8,128)(2,1)S(1)}, u32[]{:S(2)}, u32[]{:S(2)}) collective-permute-start(bf16[2,64,896]{2,1,0:T(8,128)(2,1)} %get-tuple-element.130), channel_id=1, source_target_pairs={{0,6},{1,7},{2,0},{3,1},{4,2},{5,3},{6,4},{7,5},{8,14},{9,15},{10,... | collective-permute-start | bytes 688136 | tf_op jit(solution)/shard_map/ppermute | solution.py:530
  259.0 31.0 %collective-permute-start.20 = (bf16[2,64,896]{2,1,0:T(8,128)(2,1)}, bf16[2,64,896]{2,1,0:T(8,128)(2,1)}, u32[]{:S(2)}, u32[]{:S(2)}) collective-permute-start(bf16[2,64,896]{2,1,0:T(8,128)(2,1)} %get-tuple-element.129), channel_id=1, source_target_pairs={{0,4},{1,5},{2,6},{3,7},{4,0},{5,1},{6,2},{7,3},{8,12},{9,13},{10,... | collective-permute-start | bytes 688136 | tf_op jit(solution)/shard_map/ppermute | solution.py:530
  290.9 11.0 %collective-permute-start.29 = (bf16[64,1536]{1,0:T(8,128)(2,1)}, bf16[64,1536]{1,0:T(8,128)(2,1)S(1)}, u32[]{:S(2)}, u32[]{:S(2)}) collective-permute-start(bf16[64,1536]{1,0:T(8,128)(2,1)} %get-tuple-element.133), channel_id=1, source_target_pairs={{0,2},{1,3},{2,4},{3,5},{4,6},{5,7},{6,0},{7,1},{8,10},{9,11},{10,... | collective-permute-start | bytes 589832 | tf_op jit(solution)/shard_map/ppermute | solution.py:530
  290.9 12.8 %collective-permute-start.30 = (bf16[64,1536]{1,0:T(8,128)(2,1)S(1)}, bf16[64,1536]{1,0:T(8,128)(2,1)S(1)}, u32[]{:S(2)}, u32[]{:S(2)}) collective-permute-start(bf16[64,1536]{1,0:T(8,128)(2,1)S(1)} %get-tuple-element.135), channel_id=1, source_target_pairs={{0,6},{1,7},{2,0},{3,1},{4,2},{5,3},{6,4},{7,5},{8,14},{9,15},{10,... | collective-permute-start | bytes 589832 | tf_op jit(solution)/shard_map/ppermute | solution.py:530
  294.7 15.1 %collective-permute-start.31 = (bf16[64,1536]{1,0:T(8,128)(2,1)S(1)}, bf16[64,1536]{1,0:T(8,128)(2,1)}, u32[]{:S(2)}, u32[]{:S(2)}) collective-permute-start(bf16[64,1536]{1,0:T(8,128)(2,1)S(1)} %get-tuple-element.134), channel_id=1, source_target_pairs={{0,4},{1,5},{2,6},{3,7},{4,0},{5,1},{6,2},{7,3},{8,12},{9,13},{10,... | collective-permute-start | bytes 589832 | tf_op jit(solution)/shard_map/ppermute | solution.py:530
  297.4 15.3 %collective-permute-start.22 = (f32[4,1836]{1,0:T(4,128)S(1)}, f32[4,1836]{1,0:T(4,128)S(1)}, u32[]{:S(2)}, u32[]{:S(2)}) collective-permute-start(f32[4,1836]{1,0:T(4,128)S(1)} %bitcast.196), channel_id=1, source_target_pairs={{0,1},{1,0},{2,3},{3,2},{4,5},{5,4},{6,7},{7,6},{8,9},{9,8},{10,11... | collective-permute-start | bytes 88136 | tf_op jit(solution)/shard_map/ppermute | solution.py:536
  310.9 14.1 %collective-permute-start.33 = (bf16[64,2432]{1,0:T(8,128)(2,1)S(1)}, bf16[64,2432]{1,0:T(8,128)(2,1)S(1)}, u32[]{:S(2)}, u32[]{:S(2)}) collective-permute-start(bf16[64,2432]{1,0:T(8,128)(2,1)S(1)} %pad_maximum_fusion.10), channel_id=1, source_target_pairs={{0,16},{8,24},{16,0},{24,8},{1,17},{9,25},{17,1},{25,9},{2,18},{10... | collective-permute-start | bytes 933896 | tf_op jit(solution)/shard_map/ppermute | solution.py:492
  321.5 10.9 %collective-permute-start.27 = (bf16[256,1024]{1,0:T(8,128)(2,1)S(1)}, bf16[256,1024]{1,0:T(8,128)(2,1)S(1)}, u32[]{:S(2)}, u32[]{:S(2)}) collective-permute-start(bf16[256,1024]{1,0:T(8,128)(2,1)S(1)} %bitcast.185), channel_id=1, source_target_pairs={{0,16},{8,24},{16,0},{24,8},{1,17},{9,25},{17,1},{25,9},{2,18},{10... | collective-permute-start | bytes 1572872 | tf_op jit(solution)/shard_map/ppermute | solution.py:492
  325.1 7.6 %collective-permute-start.34 = (bf16[64,2432]{1,0:T(8,128)(2,1)S(1)}, bf16[64,2432]{1,0:T(8,128)(2,1)S(1)}, u32[]{:S(2)}, u32[]{:S(2)}) collective-permute-start(bf16[64,2432]{1,0:T(8,128)(2,1)S(1)} %add_convert_fusion.4), channel_id=1, source_target_pairs={{0,8},{8,0},{16,24},{24,16},{1,9},{9,1},{17,25},{25,17},{2,10},{10... | collective-permute-start | bytes 933896 | tf_op jit(solution)/shard_map/ppermute | solution.py:470
  (41 other events, 334.7 us)
Sparse Core Ops, SparseCore 0:
  34.2 78.0 all-gather.2
  178.7 103.5 reduce-scatter.1

commit v4 on v3

--- a/solution.py
+++ b/solution.py
@@ -255,7 +255,21 @@
     hpg_ref[1:2, :] += jnp.sum(rates * g_rate, axis=0, keepdims=True)
 
 
-def gate_kernel(y_ref, normed_ref, dy_ref, wz_ref, wo_ref, gain_ref, out_ref, gy_ref, gz_ref, gg_ref, z_ref, gm_ref):
+def z_weight(zo_refs, lanes):
+    shards, rows, width = zo_refs[0].shape
+    half, side = rows // 4, lanes.start // width
+    columns = slice(lanes.start - side * width, lanes.stop - side * width)
+    parts = [ref[:, side * half : (side + 1) * half, columns] for ref in zo_refs]
+    return jnp.stack(parts, axis=1).reshape(2 * shards * half, columns.stop - columns.start)
+
+
+def out_weight_rows(zo_refs, lanes):
+    shards, rows, width = zo_refs[0].shape
+    parts = [ref[lanes.start // rows : lanes.stop // rows, rows // 2 :, :] for ref in zo_refs]
+    return jnp.stack(parts, axis=1).reshape(lanes.stop - lanes.start, width)
+
+
+def gate_kernel(y_ref, normed_ref, dy_ref, zo0_ref, zo1_ref, gain_ref, out_ref, gy_ref, gz_ref, gg_ref, z_ref, gm_ref):
     rows, inner = y_ref.shape
 
     @pl.when(pl.program_id(0) == 0)
@@ -267,8 +281,8 @@
     cross = jnp.zeros((rows, 2 * LANES), F32)
     normed, dy = normed_ref[...], dy_ref[...]
     for lanes in pieces:
-        z = mm(normed, wz_ref[:, lanes])
-        gm = mm_nt(dy, wo_ref[lanes, :])
+        z = mm(normed, z_weight((zo0_ref, zo1_ref), lanes))
+        gm = mm_nt(dy, out_weight_rows((zo0_ref, zo1_ref), lanes))
         z_ref[:, lanes] = z
         gm_ref[:, lanes] = gm
         gated = y_ref[:, lanes] * (z * sigmoid(z))
@@ -389,7 +403,7 @@
     )(xbc, pre, y, gy, sin, col, row, cw, hp, skip, spread, collect)
 
 
-def gate(y, normed, dy, w_z, w_out, gain):
+def gate(y, normed, dy, zo, gain):
     length, inner = y.shape
     width = normed.shape[1]
     rows = 256
@@ -398,7 +412,7 @@
         gate_kernel,
         grid=(length // rows,),
         in_specs=[
-            block(inner), block(width), block(width), full((width, inner)), full((inner, width)), full((8, inner)),
+            block(inner), block(width), block(width), full(zo[0].shape), full(zo[1].shape), full((8, inner)),
         ],
         out_specs=[block(inner), block(inner), block(inner), full((8, inner))],
         out_shape=[jax.ShapeDtypeStruct((length, inner), BF)] * 3 + [jax.ShapeDtypeStruct((8, inner), F32)],
@@ -406,38 +420,42 @@
         compiler_params=PARAMS,
         cost_estimate=pl.CostEstimate(flops=9 * 10**9, bytes_accessed=4 * 10**7, transcendentals=4 * 10**6),
         name="gate",
-    )(y, normed, dy, w_z, w_out, gain)
-
-
-def input_kernel(tokens_ref, dy_ref, gz_ref, gp_ref, wz_ref, wx_ref, gain_ref, out_ref, gg_ref):
-    @pl.when(pl.program_id(0) == 0)
-    def _():
-        gg_ref[...] = jnp.zeros_like(gg_ref)
-
-    g_normed = mm_nt(gz_ref[...], wz_ref[...]) + mm_nt(gp_ref[...], wx_ref[...])
+    )(y, normed, dy, *zo, gain)
+
+
+def input_kernel(tokens_ref, dy_ref, gz_ref, gp_ref, mixed_ref, zo0_ref, zo1_ref, wx_ref, gain_ref, grad_ref, out_ref):
+    width, inner = tokens_ref.shape[1], gz_ref.shape[1]
+    g_normed = mm_nt(gp_ref[...], wx_ref[...])
+    for k in range(0, inner, width):
+        lanes = slice(k, k + width)
+        g_normed = g_normed + mm_nt(gz_ref[:, lanes], z_weight((zo0_ref, zo1_ref), lanes))
     inputs = tokens_ref[...].astype(F32)
     inv = lax.rsqrt(jnp.mean(inputs * inputs, axis=1, keepdims=True) + EPS)
     unit = inputs * inv
     scaled = g_normed * gain_ref[0:1, :]
-    gg_ref[0:1, :] += jnp.sum(g_normed * unit, axis=0, keepdims=True)
     pull = jnp.mean(scaled * unit, axis=1, keepdims=True)
-    out_ref[...] = (dy_ref[...].astype(F32) + inv * (scaled - unit * pull)).astype(BF)
-
-
-def input_gradient(tokens, dy, gz, gp, w_z, w_x, gain):
+    grad_ref[...] = (dy_ref[...].astype(F32) + inv * (scaled - unit * pull)).astype(BF)
+    total = inputs
+    for k in range(0, inner, 2 * LANES):
+        lanes = slice(k, k + 2 * LANES)
+        total = total + mm(mixed_ref[:, lanes], out_weight_rows((zo0_ref, zo1_ref), lanes))
+    out_ref[...] = total.astype(BF)
+
+
+def input_gradient(tokens, dy, gz, gp, mixed_out, zo, w_x, gain):
     length, width = tokens.shape
     rows = 256
     block = lambda v: pl.BlockSpec((rows, v.shape[1]), lambda i: (i, 0))
     return pl.pallas_call(
         input_kernel,
         grid=(length // rows,),
-        in_specs=[block(v) for v in (tokens, dy, gz, gp)] + [full(v.shape) for v in (w_z, w_x, gain)],
-        out_specs=[block(tokens), full((8, width))],
-        out_shape=[jax.ShapeDtypeStruct((length, width), BF), jax.ShapeDtypeStruct((8, width), F32)],
+        in_specs=[block(v) for v in (tokens, dy, gz, gp, mixed_out)] + [full(v.shape) for v in (*zo, w_x, gain)],
+        out_specs=[block(tokens)] * 2,
+        out_shape=[jax.ShapeDtypeStruct((length, width), BF)] * 2,
         compiler_params=PARAMS,
         cost_estimate=pl.CostEstimate(flops=10**7, bytes_accessed=10**5, transcendentals=0),
         name="input_gradient",
-    )(tokens, dy, gz, gp, w_z, w_x, gain)
+    )(tokens, dy, gz, gp, mixed_out, *zo, w_x, gain)
 
 
 def document_info(resets):
@@ -486,8 +504,7 @@
     return (mine.astype(F32) + other_core(theirs, reps).astype(F32)).astype(BF)
 
 
-def sum_reps(value, reps):
-    flip = 2
+def sum_reps(value, reps, flip=2):
     while flip < reps:
         value = add(value, lax.ppermute(value, "rep", pairs(reps, flip)))
         flip *= 2
@@ -602,10 +619,9 @@
     xbc = mm(normed, w_x)
     y, pre, sin = scan_forward(xbc, col, row, cw8, hp8, sk8)
     zo_all, y = barrier((zo_all, y))
-    zo = swap_halves(zo_all, core, reps, 1)
-    w_z = jnp.concatenate([zo[:, :, :half].reshape(width, width), zo[:, :, half : 2 * half].reshape(width, width)], axis=1)
-    w_out = zo[:, :, 2 * half :].reshape(inner, width)
-    mixed_out, gy, gz, gg_grad = gate(y, normed, cotangent, w_z, w_out, gg8)
+    zo_other = other_core(zo_all, reps)
+    zo = (jnp.where(core == 0, zo_all, zo_other), jnp.where(core == 0, zo_other, zo_all))
+    mixed_out, gy, gz, gg_grad = gate(y, normed, cotangent, zo, gg8)
 
     def grad_of(left, right):
         return lax.dot_general(left, right, (((0,), (0,)), ((), ())), preferred_element_type=F32).astype(BF)
@@ -622,34 +638,43 @@
     x_grad = grad_of(normed, gp).reshape(shards, 2, half, mixed + LANES)
     x_mine, x_theirs = half_of(x_grad, core, 1)
     x_theirs = other_core(x_theirs, reps)
-    output = (inputs + mm(mixed_out, w_out)).astype(BF)
-    x_theirs, output = barrier((x_theirs, output))
     x_sums = [add(x_mine[:, :, s], x_theirs[:, :, s]) for s in (slice(0, cut), slice(cut, mixed + LANES))]
     x_sums, gp = barrier((x_sums, gp))
-    input_grad, gain_grad = input_gradient(tokens, cotangent, gz, gp, w_z, w_x, rows8(gain))
-
-    def during(stage, value):
-        nonlocal input_grad, gain_grad, zo_own
-        if stage == 0:
-            value, input_grad, gain_grad, zo_own = barrier((value, input_grad, gain_grad, zo_own))
-        return value
-
-    x_parts = scatter_shards(*x_sums, shards, during)
-    gain_grad = gain_grad[0]
+    input_grad, output = input_gradient(tokens, cotangent, gz, gp, mixed_out, zo, w_x, rows8(gain))
 
     grads = (cwg[:4], cwg[4], hpg[0, :heads], hpg[1, :heads], skg[0].reshape(heads, WIDTH).sum(axis=1), gg_grad[0])
     split = lambda v: jnp.moveaxis(v.reshape(v.shape[:-1] + (shards, -1)), -2, 0).reshape(shards, -1)
-    own = jnp.concatenate([split(v) for v in (gain_grad,) + grads], axis=1)
+    own = jnp.concatenate([split(v) for v in grads], axis=1)
     own = own + other_core(own, reps)
-    own, _ = scatter_shards(own, own[:, :LANES], shards, lambda stage, value: value)
+    member = lax.axis_index("shard")
+    z_at, y_at = member // 2, member % 2
+    staged = shards == 8 and reps > 2
+    if staged:
+        own = along_y(own.reshape(4, 2, -1), y_at, 1)
+    else:
+        own = lax.psum_scatter(own, "shard", scatter_dimension=0)
+
+    def during(stage, value):
+        nonlocal input_grad, output, zo_own, own
+        if stage == 0:
+            value, input_grad, output, zo_own, own = barrier((value, input_grad, output, zo_own, own))
+            if staged:
+                zo_own = [zo_own, lax.ppermute(zo_own, "rep", pairs(reps, 2))]
+                own = along_z(add(*own), z_at)
+        elif staged:
+            value, zo_own, own = barrier((value, zo_own, own))
+            zo_own, own = add(*zo_own), add(*own)
+        return value
+
+    x_parts = scatter_shards(*x_sums, shards, during)
+    zo_own = swap_halves(sum_reps(zo_own, reps, 4 if staged else 2), core, reps, 0).astype(F32)
     own = sum_reps(own, reps)
+    x_own = swap_halves(sum_reps(jnp.concatenate(x_parts, axis=1), reps), core, reps, 0).astype(F32)
     small_grads, at = [], 0
-    for part in small_parts:
+    for part in small_parts[1:]:
         small_grads.append(own[at : at + part.size].reshape(part.shape))
         at += part.size
 
-    zo_own = swap_halves(sum_reps(zo_own, reps), core, reps, 0).astype(F32)
-    x_own = swap_halves(sum_reps(jnp.concatenate(x_parts, axis=1), reps), core, reps, 0).astype(F32)
     out_part = zo_own[:, 2 * half :].reshape(out_weight.shape)
     in_grad = jnp.concatenate(
         [
@@ -659,7 +684,8 @@
         ],
         axis=1,
     )
-    return (output, input_grad, small_grads[0], in_grad, *small_grads[1:], out_part)
+    gain_grad = jnp.sum(in_weight.astype(F32) * in_grad, axis=1) / norm_gain.astype(F32)
+    return (output, input_grad, gain_grad, in_grad, *small_grads, out_part)
 
 
 def solution(mesh):

time: 351 us -> 346 us (0.986)
  Pallas kernels: 115 us -> 122 us
  waiting for transfers between devices: 75.8 us -> 70 us
    ppermute x9, waiting for transfers between devices: 25 us -> 15 us  [along_z(): lax.ppermute(entry, 'shard', [(i, (i + 2 * k) % 8) for i in range(8)])]
    another operation x7 -> x5, other arithmetic: 9.89 us -> 3.59 us  [swap_halves(): jnp.stack([jnp.where(first, own, other), jnp.where(first, other, own)], a...]
    pallas_call x1, Pallas kernels: 17.5 us -> 23.8 us  [input_gradient(): pl.pallas_call(input_kernel, grid=(length // rows,), in_specs=[block(v) f...]
    select_n x0 -> x1, other arithmetic: none -> 5.78 us  [on_device(): jnp.where(core == 0, zo_other, zo_all)]
    dot_general x2 -> x1, matrix products: 13.9 us -> 8.48 us  [mm(): return jnp.dot(a, b, preferred_element_type=F32)]
    ppermute x9, waiting for transfers between devices: 11.9 us -> 15.8 us  [other_core(): return lax.ppermute(value, 'rep', pairs(reps, 1))]
    squeeze x6, local copies, waits for them, and re-layouts: 4.19 us -> 7.98 us  [half_of(): pick = lambda k: lax.dynamic_index_in_dim(value, k, axis, keepdims=False)]
    unnamed x64 -> x75, local copies, waits for them, and re-layouts: 9.03 us -> 8.58 us
  transfers between devices with their start and end apart: 37 -> 37, of which waited for: 18 -> 16; matrix products, arithmetic and copies ran while one was open for 18% -> 19% of each run, Pallas kernels for 27% -> 29%
where the time goes in v4:
time: 346 us; the launch traced here: 341 us
  Pallas kernels  122 us (35%)
  waiting for transfers between devices  70 us (20%)
  starting transfers between devices  41.8 us (12%)
  local copies, waits for them, and re-layouts  33.5 us (10%)
  matrix products  30.3 us (9%)
  other arithmetic  28.1 us (8%)
  between operations  15.3 us (4%)
    pallas_call x1, Pallas kernels, scan_backward(): pl.pallas_call(partial(bwd_kernel, inner), grid=(blocks,), in_specs=[pl.B...  51.8 us
    ppermute x6, waiting for transfers between devices, from_behind(): lax.ppermute(block, 'shard', [(i, (i + 2 * k) % 8) for i in range(8)])  25.2 us
    pallas_call x1, Pallas kernels, scan_forward(): pl.pallas_call(partial(fwd_kernel, inner), grid=(blocks,), in_specs=[pl.B...  24.3 us
    pallas_call x1, Pallas kernels, input_gradient(): pl.pallas_call(input_kernel, grid=(length // rows,), in_specs=[block(v) f...  23.8 us
    dot_general x4, matrix products, grad_of(): lax.dot_general(left, right, (((0,), (0,)), ((), ())), preferred_element_...  21.9 us
    pallas_call x1, Pallas kernels, gate(): pl.pallas_call(gate_kernel, grid=(length // rows,), in_specs=[block(inner...  21.7 us
    ppermute x9, starting transfers between devices, along_z(): lax.ppermute(entry, 'shard', [(i, (i + 2 * k) % 8) for i in range(8)])  16.1 us
    ppermute x9, waiting for transfers between devices, other_core(): return lax.ppermute(value, 'rep', pairs(reps, 1))  15.8 us
  transfers between devices with their start and end apart: 37, of which 16 were waited for; matrix products, arithmetic and copies ran while one was open for 19% of the time, Pallas kernels for 29%

profile of v4, /device:TPU:0, one launch (start us, length us, event | category | flops | bytes accessed | tf_op | source)
XLA Modules:
  0.0 340.7 jit_solution(11953083084848064636)
XLA Ops:
  10.0 3.0 collective-permute-start
  18.9 3.2 collective-permute-done.5
  26.9 3.1 collective-permute-start.3
  39.6 23.4 %collective-permute-done.9 = bf16[64,2432]{1,0:T(8,128)(2,1)S(1)} collective-permute-done((bf16[64,2432]{1,0:T(8,128)(2,1)}, bf16[64,2432]{1,0:T(8,128)(2,1)S(1)}, u32[]{:S(2)}, u32[]{:S(2)}) %collective-permute-start.9) | collective-permute-done | bytes 311328 | tf_op jit(solution)/shard_map/ppermute | solution.py:521
  79.2 8.5 %fusion.42.xbc_ref = f32[1024,2432]{1,0:T(8,128)} fusion(bf16[1024,1024]{1,0:T(8,128)(2,1)S(1)} %fusion.2.normed_ref, bf16[1024,2432]{1,0:T(8,128)(2,1)S(1)} %bitcast.156), kind=kOutput, calls=%fused_computation.154 | convolution fusion | flops 5100273664 | bytes 17039360 | tf_op jit(solution)/shard_map/dot_general | solution.py:21
  87.7 24.3 %scan_forward.1 = (f32[1024,2048]{1,0:T(8,128)}, f32[1024,2304]{1,0:T(8,128)}, bf16[1024,2048]{1,0:T(8,128)(2,1)}) custom-call(f32[1024,2432]{1,0:T(8,128)} %fusion.42.xbc_ref, f32[1024,16]{1,0:T(8,128)S(1)} %copy.62.col_ref, f32[8,1024]{1,0:T(8,128)S(1)} %broadcast_in_dim.82.row_ref, f32[8,2304]{1,0:T(8,128)S(1)} %maximum_maximum_fusion.cw_ref, ...), custom_call_target="tpu_custom_call" | custom-call | flops 6000000000 | bytes 30000000 | tf_op jit(solution)/shard_map/scan_forward/pallas_call | solution.py:340
  112.2 7.2 %collective-permute-done.12 = bf16[8,256,1024]{2,1,0:T(8,128)(2,1)} collective-permute-done((bf16[8,256,1024]{2,1,0:T(8,128)(2,1)}, bf16[8,256,1024]{2,1,0:T(8,128)(2,1)}, u32[]{:S(2)}, u32[]{:S(2)}) %collective-permute-start.12) | collective-permute-done | bytes 4194336 | tf_op jit(solution)/shard_map/ppermute | solution.py:488
  119.4 5.8 %broadcast_select_fusion = (bf16[8,256,1024]{2,1,0:T(8,128)(2,1)}, bf16[8,256,1024]{2,1,0:T(8,128)(2,1)}) fusion(bf16[8,256,1024]{2,1,0:T(8,128)(2,1)} %collective-permute-done.12, bf16[8,256,1024]{2,1,0:T(8,128)(2,1)} %bitcast.161, pred[]{:T(512)S(6)} %eq.84), kind=kLoop, calls=%fused_computation.11 | loop fusion | flops 4194304 | bytes 16777216 | tf_op jit(solution)/shard_map/jit(_where)/select_n | solution.py:623
  125.2 21.7 %gate.1 = (bf16[1024,2048]{1,0:T(8,128)(2,1)}, bf16[1024,2048]{1,0:T(8,128)(2,1)}, bf16[1024,2048]{1,0:T(8,128)(2,1)}, f32[8,2048]{1,0:T(8,128)S(1)}) custom-call(f32[1024,2048]{1,0:T(8,128)} %get-tuple-element.66.y_ref, bf16[1024,1024]{1,0:T(8,128)(2,1)} %copy-done.14, bf16[1024,1024]{1,0:T(8,128)(2,1)} %dy_ref.3, ...), custom_call_target="tpu_custom_call" | custom-call | flops 8999999488 | bytes 40000000 | tf_op jit(solution)/shard_map/gate/pallas_call | solution.py:411
  147.0 7.3 %convolution_convert_fusion.1 = bf16[2048,1024]{1,0:T(8,128)(2,1)S(1)} fusion(bf16[1024,2048]{1,0:T(8,128)(2,1)} %get-tuple-element.69.mixed_ref, bf16[1024,1024]{1,0:T(8,128)(2,1)S(1)} %copy-done.12), kind=kOutput, calls=%fused_computation.13 | convolution fusion | flops 4297064448 | bytes 10485760 | tf_op jit(solution)/shard_map/dot_general | solution.py:627
  162.5 3.7 %fusion.10 = bf16[1024,1024]{1,0:T(8,128)(2,1)} fusion(bf16[1024,1024]{1,0:T(8,128)(2,1)S(1)} %copy-done.15, bf16[1024,2048]{1,0:T(8,128)(2,1)S(1)} %copy-done.10), kind=kOutput, calls=%fused_computation.30 | convolution fusion | flops 2148532224 | bytes 6291456 | tf_op jit(solution)/shard_map/dot_general | solution.py:627
  177.8 51.8 %scan_backward.1 = (bf16[1024,2432]{1,0:T(8,128)(2,1)}, f32[8,2304]{1,0:T(8,128)S(1)}, f32[8,128]{1,0:T(8,128)S(1)}, f32[8,2048]{1,0:T(8,128)S(1)}) custom-call(f32[1024,2432]{1,0:T(8,128)} %fusion.42.xbc_ref, f32[1024,2304]{1,0:T(8,128)} %get-tuple-element.63.pre_ref, f32[1024,2048]{1,0:T(8,128)} %get-tuple-element.66.y_ref, ...), custom_call_target="tpu_custom_call" | custom-call | flops 20000000000 | bytes 50000000 | tf_op jit(solution)/shard_map/scan_backward/pallas_call | solution.py:371
  229.6 8.4 %convolution_convert_fusion = bf16[1024,2432]{1,0:T(8,128)(2,1)S(1)} fusion(bf16[1024,1024]{1,0:T(8,128)(2,1)S(1)} %copy-done.16, bf16[1024,2432]{1,0:T(8,128)(2,1)} %get-tuple-element.76.gp_ref), kind=kOutput, calls=%fused_computation.1 | convolution fusion | flops 5102764032 | bytes 12058624 | tf_op jit(solution)/shard_map/dot_general | solution.py:627
  240.5 4.5 %collective-permute-done.16 = bf16[8,64,2432]{2,1,0:T(8,128)(2,1)} collective-permute-done((bf16[8,64,2432]{2,1,0:T(8,128)(2,1)}, bf16[8,64,2432]{2,1,0:T(8,128)(2,1)}, u32[]{:S(2)}, u32[]{:S(2)}) %collective-permute-start.16) | collective-permute-done | bytes 2490400 | tf_op jit(solution)/shard_map/ppermute | solution.py:488
  255.4 3.4 %collective-permute-start.19 = (bf16[2,64,896]{2,1,0:T(8,128)(2,1)S(1)}, bf16[2,64,896]{2,1,0:T(8,128)(2,1)S(1)}, u32[]{:S(2)}, u32[]{:S(2)}) collective-permute-start(bf16[2,64,896]{2,1,0:T(8,128)(2,1)S(1)} %get-tuple-element.154), channel_id=1, source_target_pairs={{0,6},{1,7},{2,0},{3,1},{4,2},{5,3},{6,4},{7,5},{8,14},{9,15},{10,... | collective-permute-start | bytes 688136 | tf_op jit(solution)/shard_map/ppermute | solution.py:547
  259.8 23.8 %input_gradient.1 = (bf16[1024,1024]{1,0:T(8,128)(2,1)}, bf16[1024,1024]{1,0:T(8,128)(2,1)}) custom-call(bf16[1024,1024]{1,0:T(8,128)(2,1)} %tokens_ref.1, bf16[1024,1024]{1,0:T(8,128)(2,1)} %dy_ref.3, bf16[1024,2048]{1,0:T(8,128)(2,1)} %get-tuple-element.68.gz_ref, bf16[1024,2432]{1,0:T(8,128)(2,1)} %get-tuple-element.76.gp_ref, ...), custom_call_target="tpu_custom_call" | custom-call | flops 10000000 | bytes 100000 | tf_op jit(solution)/shard_map/input_gradient/pallas_call | solution.py:449
  283.6 3.8 %collective-permute-done.20 = bf16[2,64,896]{2,1,0:T(8,128)(2,1)S(1)} collective-permute-done((bf16[2,64,896]{2,1,0:T(8,128)(2,1)S(1)}, bf16[2,64,896]{2,1,0:T(8,128)(2,1)S(1)}, u32[]{:S(2)}, u32[]{:S(2)}) %collective-permute-start.20) | collective-permute-done | bytes 229408 | tf_op jit(solution)/shard_map/ppermute | solution.py:547
  289.3 3.8 %collective-permute-start.24 = (bf16[64,1536]{1,0:T(8,128)(2,1)S(1)}, bf16[64,1536]{1,0:T(8,128)(2,1)S(1)}, u32[]{:S(2)}, u32[]{:S(2)}) collective-permute-start(bf16[64,1536]{1,0:T(8,128)(2,1)S(1)} %get-tuple-element.158), channel_id=1, source_target_pairs={{0,6},{1,7},{2,0},{3,1},{4,2},{5,3},{6,4},{7,5},{8,14},{9,15},{10,... | collective-permute-start | bytes 589832 | tf_op jit(solution)/shard_map/ppermute | solution.py:547
  293.3 3.8 %collective-permute-start.29 = (f32[1708]{0:T(1024)S(1)}, f32[1708]{0:T(1024)S(1)}, u32[]{:S(2)}, u32[]{:S(2)}) collective-permute-start(f32[1708]{0:T(1024)S(1)} %get-tuple-element.130), channel_id=1, source_target_pairs={{0,6},{1,7},{2,0},{3,1},{4,2},{5,3},{6,4},{7,5},{8,14},{9,15},{10,... | collective-permute-start | bytes 20504 | tf_op jit(solution)/shard_map/ppermute | solution.py:547
  297.2 4.9 %collective-permute-done.28 = f32[1708]{0:T(1024)S(1)} collective-permute-done((f32[1708]{0:T(1024)S(1)}, f32[1708]{0:T(1024)S(1)}, u32[]{:S(2)}, u32[]{:S(2)}) %collective-permute-start.28) | collective-permute-done | bytes 6864 | tf_op jit(solution)/shard_map/ppermute | solution.py:547
  302.1 2.9 collective-permute-start.30
  305.1 6.3 %collective-permute-done.30 = f32[1708]{0:T(1024)S(1)} collective-permute-done((f32[1708]{0:T(1024)S(1)}, f32[1708]{0:T(1024)S(1)}, u32[]{:S(2)}, u32[]{:S(2)}) %collective-permute-start.30) | collective-permute-done | bytes 6864 | tf_op jit(solution)/shard_map/ppermute | solution.py:547
  312.4 4.0 %collective-permute-done.26 = bf16[64,896]{1,0:T(8,128)(2,1)S(1)} collective-permute-done((bf16[64,896]{1,0:T(8,128)(2,1)S(1)}, bf16[64,896]{1,0:T(8,128)(2,1)S(1)}, u32[]{:S(2)}, u32[]{:S(2)}) %collective-permute-start.26) | collective-permute-done | bytes 114720 | tf_op jit(solution)/shard_map/ppermute | solution.py:553
  319.0 6.3 %collective-permute-done.34 = f32[1708]{0:T(1024)S(1)} collective-permute-done((f32[1708]{0:T(1024)S(1)}, f32[1708]{0:T(1024)S(1)}, u32[]{:S(2)}, u32[]{:S(2)}) %collective-permute-start.34) | collective-permute-done | bytes 6864 | tf_op jit(solution)/shard_map/ppermute | solution.py:509
  (271 shorter events, 86.4 us)
Async XLA Ops:
  7.3 104.7 %all-gather.3.cloned.1.call-start = ((), (), s32[]{:S(2)}) async-start(), calls=%async_computation.2 | async-start | bytes 4718592 | tf_op jit(solution)/shard_map/all_gather | solution.py:597
  10.0 21.7 %collective-permute-start = (bf16[64,2432]{1,0:T(8,128)(2,1)}, bf16[64,2432]{1,0:T(8,128)(2,1)S(1)}, u32[]{:S(2)}, u32[]{:S(2)}) collective-permute-start(bf16[64,2432]{1,0:T(8,128)(2,1)} %pad.35), channel_id=1, source_target_pairs={{0,2},{1,3},{2,4},{3,5},{4,6},{5,7},{6,0},{7,1},{8,10},{9,11},{10,... | collective-permute-start | bytes 933896 | tf_op jit(solution)/shard_map/ppermute | solution.py:521
  13.0 22.7 %collective-permute-start.1 = (bf16[64,2432]{1,0:T(8,128)(2,1)}, bf16[64,2432]{1,0:T(8,128)(2,1)S(1)}, u32[]{:S(2)}, u32[]{:S(2)}) collective-permute-start(bf16[64,2432]{1,0:T(8,128)(2,1)} %pad.35), channel_id=1, source_target_pairs={{0,1},{1,0},{2,3},{3,2},{4,5},{5,4},{6,7},{7,6},{8,9},{9,8},{10,11... | collective-permute-start | bytes 933896 | tf_op jit(solution)/shard_map/ppermute | solution.py:533
  26.9 11.2 %collective-permute-start.3 = (bf16[64,2432]{1,0:T(8,128)(2,1)}, bf16[64,2432]{1,0:T(8,128)(2,1)}, u32[]{:S(2)}, u32[]{:S(2)}) collective-permute-start(bf16[64,2432]{1,0:T(8,128)(2,1)} %pad.35), channel_id=1, source_target_pairs={{0,6},{1,7},{2,0},{3,1},{4,2},{5,3},{6,4},{7,5},{8,14},{9,15},{10,... | collective-permute-start | bytes 933896 | tf_op jit(solution)/shard_map/ppermute | solution.py:521
  30.0 33.0 %collective-permute-start.9 = (bf16[64,2432]{1,0:T(8,128)(2,1)}, bf16[64,2432]{1,0:T(8,128)(2,1)S(1)}, u32[]{:S(2)}, u32[]{:S(2)}) collective-permute-start(bf16[64,2432]{1,0:T(8,128)(2,1)} %pad.35), channel_id=1, source_target_pairs={{0,4},{1,5},{2,6},{3,7},{4,0},{5,1},{6,2},{7,3},{8,12},{9,13},{10,... | collective-permute-start | bytes 933896 | tf_op jit(solution)/shard_map/ppermute | solution.py:521
  31.7 33.0 %collective-permute-start.2 = (bf16[64,2432]{1,0:T(8,128)(2,1)S(1)}, bf16[64,2432]{1,0:T(8,128)(2,1)}, u32[]{:S(2)}, u32[]{:S(2)}) collective-permute-start(bf16[64,2432]{1,0:T(8,128)(2,1)S(1)} %collective-permute-done), channel_id=1, source_target_pairs={{0,1},{1,0},{2,3},{3,2},{4,5},{5,4},{6,7},{7,6},{8,9},{9,8},{10,11... | collective-permute-start | bytes 933896 | tf_op jit(solution)/shard_map/ppermute | solution.py:533
  33.3 254.1 %reduce-scatter.2.cloned.1.call-start = ((), (), s32[]{:S(2)}) async-start(), calls=%async_computation.1 | async-start | bytes 4718592 | tf_op jit(solution)/shard_map/reduce_scatter | solution.py:635
  38.1 30.0 %collective-permute-start.4 = (bf16[64,2432]{1,0:T(8,128)(2,1)}, bf16[64,2432]{1,0:T(8,128)(2,1)S(1)}, u32[]{:S(2)}, u32[]{:S(2)}) collective-permute-start(bf16[64,2432]{1,0:T(8,128)(2,1)} %collective-permute-done.3), channel_id=1, source_target_pairs={{0,1},{1,0},{2,3},{3,2},{4,5},{5,4},{6,7},{7,6},{8,9},{9,8},{10,11... | collective-permute-start | bytes 933896 | tf_op jit(solution)/shard_map/ppermute | solution.py:533
  155.9 17.6 %collective-permute-start.15 = (bf16[8,128,1024]{2,1,0:T(8,128)(2,1)}, bf16[8,128,1024]{2,1,0:T(8,128)(2,1)S(1)}, u32[]{:S(2)}, u32[]{:S(2)}) collective-permute-start(bf16[8,128,1024]{2,1,0:T(8,128)(2,1)} %dynamic-slice_bitcast_fusion.2), channel_id=1, source_target_pairs={{0,8},{8,0},{16,24},{24,16},{1,9},{9,1},{17,25},{25,17},{2,10},{10... | collective-permute-start | bytes 6291464 | tf_op jit(solution)/shard_map/ppermute | solution.py:488
  250.2 37.3 %collective-permute-start.17 = (bf16[4,64,1536]{2,1,0:T(8,128)(2,1)}, bf16[4,64,1536]{2,1,0:T(8,128)(2,1)S(1)}, u32[]{:S(2)}, u32[]{:S(2)}) collective-permute-start(bf16[4,64,1536]{2,1,0:T(8,128)(2,1)} %get-tuple-element.145), channel_id=1, source_target_pairs={{0,1},{1,0},{2,3},{3,2},{4,5},{5,4},{6,7},{7,6},{8,9},{9,8},{10,11... | collective-permute-start | bytes 2359304 | tf_op jit(solution)/shard_map/ppermute | solution.py:553
  254.0 29.6 %collective-permute-start.18 = (bf16[2,64,896]{2,1,0:T(8,128)(2,1)S(1)}, bf16[2,64,896]{2,1,0:T(8,128)(2,1)S(1)}, u32[]{:S(2)}, u32[]{:S(2)}) collective-permute-start(bf16[2,64,896]{2,1,0:T(8,128)(2,1)S(1)} %get-tuple-element.155), channel_id=1, source_target_pairs={{0,2},{1,3},{2,4},{3,5},{4,6},{5,7},{6,0},{7,1},{8,10},{9,11},{10,... | collective-permute-start | bytes 688136 | tf_op jit(solution)/shard_map/ppermute | solution.py:547
  255.4 28.2 %collective-permute-start.19 = (bf16[2,64,896]{2,1,0:T(8,128)(2,1)S(1)}, bf16[2,64,896]{2,1,0:T(8,128)(2,1)S(1)}, u32[]{:S(2)}, u32[]{:S(2)}) collective-permute-start(bf16[2,64,896]{2,1,0:T(8,128)(2,1)S(1)} %get-tuple-element.154), channel_id=1, source_target_pairs={{0,6},{1,7},{2,0},{3,1},{4,2},{5,3},{6,4},{7,5},{8,14},{9,15},{10,... | collective-permute-start | bytes 688136 | tf_op jit(solution)/shard_map/ppermute | solution.py:547
  258.9 28.6 %collective-permute-start.20 = (bf16[2,64,896]{2,1,0:T(8,128)(2,1)S(1)}, bf16[2,64,896]{2,1,0:T(8,128)(2,1)S(1)}, u32[]{:S(2)}, u32[]{:S(2)}) collective-permute-start(bf16[2,64,896]{2,1,0:T(8,128)(2,1)S(1)} %get-tuple-element.153), channel_id=1, source_target_pairs={{0,4},{1,5},{2,6},{3,7},{4,0},{5,1},{6,2},{7,3},{8,12},{9,13},{10,... | collective-permute-start | bytes 688136 | tf_op jit(solution)/shard_map/ppermute | solution.py:547
  259.4 24.2 %collective-permute-start.22 = (f32[4,1708]{1,0:T(4,128)S(1)}, f32[4,1708]{1,0:T(4,128)S(1)}, u32[]{:S(2)}, u32[]{:S(2)}) collective-permute-start(f32[4,1708]{1,0:T(4,128)S(1)} %bitcast.184), channel_id=1, source_target_pairs={{0,1},{1,0},{2,3},{3,2},{4,5},{5,4},{6,7},{7,6},{8,9},{9,8},{10,11... | collective-permute-start | bytes 81992 | tf_op jit(solution)/shard_map/ppermute | solution.py:553
  287.5 29.0 %collective-permute-start.27 = (bf16[256,1024]{1,0:T(8,128)(2,1)}, bf16[256,1024]{1,0:T(8,128)(2,1)S(1)}, u32[]{:S(2)}, u32[]{:S(2)}) collective-permute-start(bf16[256,1024]{1,0:T(8,128)(2,1)} %bitcast.171), channel_id=1, source_target_pairs={{0,16},{8,24},{16,0},{24,8},{1,17},{9,25},{17,1},{25,9},{2,18},{10... | collective-permute-start | bytes 1572872 | tf_op jit(solution)/shard_map/ppermute | solution.py:662
  289.2 27.2 %collective-permute-start.23 = (bf16[64,1536]{1,0:T(8,128)(2,1)S(1)}, bf16[64,1536]{1,0:T(8,128)(2,1)S(1)}, u32[]{:S(2)}, u32[]{:S(2)}) collective-permute-start(bf16[64,1536]{1,0:T(8,128)(2,1)S(1)} %get-tuple-element.159), channel_id=1, source_target_pairs={{0,2},{1,3},{2,4},{3,5},{4,6},{5,7},{6,0},{7,1},{8,10},{9,11},{10,... | collective-permute-start | bytes 589832 | tf_op jit(solution)/shard_map/ppermute | solution.py:547
  289.3 27.1 %collective-permute-start.24 = (bf16[64,1536]{1,0:T(8,128)(2,1)S(1)}, bf16[64,1536]{1,0:T(8,128)(2,1)S(1)}, u32[]{:S(2)}, u32[]{:S(2)}) collective-permute-start(bf16[64,1536]{1,0:T(8,128)(2,1)S(1)} %get-tuple-element.158), channel_id=1, source_target_pairs={{0,6},{1,7},{2,0},{3,1},{4,2},{5,3},{6,4},{7,5},{8,14},{9,15},{10,... | collective-permute-start | bytes 589832 | tf_op jit(solution)/shard_map/ppermute | solution.py:547
  293.2 8.9 %collective-permute-start.28 = (f32[1708]{0:T(1024)S(1)}, f32[1708]{0:T(1024)S(1)}, u32[]{:S(2)}, u32[]{:S(2)}) collective-permute-start(f32[1708]{0:T(1024)S(1)} %get-tuple-element.131), channel_id=1, source_target_pairs={{0,2},{1,3},{2,4},{3,5},{4,6},{5,7},{6,0},{7,1},{8,10},{9,11},{10,... | collective-permute-start | bytes 20504 | tf_op jit(solution)/shard_map/ppermute | solution.py:547
  293.3 8.9 %collective-permute-start.29 = (f32[1708]{0:T(1024)S(1)}, f32[1708]{0:T(1024)S(1)}, u32[]{:S(2)}, u32[]{:S(2)}) collective-permute-start(f32[1708]{0:T(1024)S(1)} %get-tuple-element.130), channel_id=1, source_target_pairs={{0,6},{1,7},{2,0},{3,1},{4,2},{5,3},{6,4},{7,5},{8,14},{9,15},{10,... | collective-permute-start | bytes 20504 | tf_op jit(solution)/shard_map/ppermute | solution.py:547
  302.1 14.3 %collective-permute-start.25 = (bf16[64,1536]{1,0:T(8,128)(2,1)S(1)}, bf16[64,1536]{1,0:T(8,128)(2,1)S(1)}, u32[]{:S(2)}, u32[]{:S(2)}) collective-permute-start(bf16[64,1536]{1,0:T(8,128)(2,1)S(1)} %get-tuple-element.157), channel_id=1, source_target_pairs={{0,4},{1,5},{2,6},{3,7},{4,0},{5,1},{6,2},{7,3},{8,12},{9,13},{10,... | collective-permute-start | bytes 589832 | tf_op jit(solution)/shard_map/ppermute | solution.py:547
  302.1 9.2 %collective-permute-start.30 = (f32[1708]{0:T(1024)S(1)}, f32[1708]{0:T(1024)S(1)}, u32[]{:S(2)}, u32[]{:S(2)}) collective-permute-start(f32[1708]{0:T(1024)S(1)} %get-tuple-element.129), channel_id=1, source_target_pairs={{0,4},{1,5},{2,6},{3,7},{4,0},{5,1},{6,2},{7,3},{8,12},{9,13},{10,... | collective-permute-start | bytes 20504 | tf_op jit(solution)/shard_map/ppermute | solution.py:547
  316.6 11.2 %collective-permute-start.32 = (bf16[64,2432]{1,0:T(8,128)(2,1)S(1)}, bf16[64,2432]{1,0:T(8,128)(2,1)S(1)}, u32[]{:S(2)}, u32[]{:S(2)}) collective-permute-start(bf16[64,2432]{1,0:T(8,128)(2,1)S(1)} %pad_maximum_fusion.6), channel_id=1, source_target_pairs={{0,16},{8,24},{16,0},{24,8},{1,17},{9,25},{17,1},{25,9},{2,18},{10... | collective-permute-start | bytes 933896 | tf_op jit(solution)/shard_map/ppermute | solution.py:509
  317.3 8.0 %collective-permute-start.34 = (f32[1708]{0:T(1024)S(1)}, f32[1708]{0:T(1024)S(1)}, u32[]{:S(2)}, u32[]{:S(2)}) collective-permute-start(f32[1708]{0:T(1024)S(1)} %add_add_fusion), channel_id=1, source_target_pairs={{0,16},{8,24},{16,0},{24,8},{1,17},{9,25},{17,1},{25,9},{2,18},{10... | collective-permute-start | bytes 20504 | tf_op jit(solution)/shard_map/ppermute | solution.py:509
  318.9 9.0 %collective-permute-start.31 = (bf16[256,1024]{1,0:T(8,128)(2,1)S(1)}, bf16[256,1024]{1,0:T(8,128)(2,1)S(1)}, u32[]{:S(2)}, u32[]{:S(2)}) collective-permute-start(bf16[256,1024]{1,0:T(8,128)(2,1)S(1)} %add_convert_fusion.3), channel_id=1, source_target_pairs={{0,8},{8,0},{16,24},{24,16},{1,9},{9,1},{17,25},{25,17},{2,10},{10... | collective-permute-start | bytes 1572872 | tf_op jit(solution)/shard_map/ppermute | solution.py:488
  (47 other events, 560.9 us)
Sparse Core Ops, SparseCore 0:
  33.4 78.3 all-gather.2
  176.9 100.9 reduce-scatter.1

commit v5 on v4

--- a/solution.py
+++ b/solution.py
@@ -269,20 +269,36 @@
     return jnp.stack(parts, axis=1).reshape(lanes.stop - lanes.start, width)
 
 
-def gate_kernel(y_ref, normed_ref, dy_ref, zo0_ref, zo1_ref, gain_ref, out_ref, gy_ref, gz_ref, gg_ref, z_ref, gm_ref):
-    rows, inner = y_ref.shape
-
+def in_core_order(core_ref, mine_ref, other_ref, body):
+    @pl.when(core_ref[0] == 0)
+    def _():
+        body((mine_ref, other_ref))
+
+    @pl.when(core_ref[0] != 0)
+    def _():
+        body((other_ref, mine_ref))
+
+
+def gate_kernel(core_ref, y_ref, normed_ref, dy_ref, mine_ref, other_ref, *refs):
     @pl.when(pl.program_id(0) == 0)
     def _():
-        gg_ref[...] = jnp.zeros_like(gg_ref)
+        refs[4][...] = jnp.zeros_like(refs[4])
+
+    in_core_order(
+        core_ref, mine_ref, other_ref, lambda zo: gate_body(y_ref, normed_ref, dy_ref, zo, *refs)
+    )
+
+
+def gate_body(y_ref, normed_ref, dy_ref, zo, gain_ref, out_ref, gy_ref, gz_ref, gg_ref, z_ref, gm_ref):
+    rows, inner = y_ref.shape
 
     pieces = [slice(k, k + 2 * LANES) for k in range(0, inner, 2 * LANES)]
     square = jnp.zeros((rows, 2 * LANES), F32)
     cross = jnp.zeros((rows, 2 * LANES), F32)
     normed, dy = normed_ref[...], dy_ref[...]
     for lanes in pieces:
-        z = mm(normed, z_weight((zo0_ref, zo1_ref), lanes))
-        gm = mm_nt(dy, out_weight_rows((zo0_ref, zo1_ref), lanes))
+        z = mm(normed, z_weight(zo, lanes))
+        gm = mm_nt(dy, out_weight_rows(zo, lanes))
         z_ref[:, lanes] = z
         gm_ref[:, lanes] = gm
         gated = y_ref[:, lanes] * (z * sigmoid(z))
@@ -403,7 +419,7 @@
     )(xbc, pre, y, gy, sin, col, row, cw, hp, skip, spread, collect)
 
 
-def gate(y, normed, dy, zo, gain):
+def gate(core, y, normed, dy, zo, gain):
     length, inner = y.shape
     width = normed.shape[1]
     rows = 256
@@ -412,6 +428,7 @@
         gate_kernel,
         grid=(length // rows,),
         in_specs=[
+            pl.BlockSpec(memory_space=pltpu.SMEM),
             block(inner), block(width), block(width), full(zo[0].shape), full(zo[1].shape), full((8, inner)),
         ],
         out_specs=[block(inner), block(inner), block(inner), full((8, inner))],
@@ -420,15 +437,24 @@
         compiler_params=PARAMS,
         cost_estimate=pl.CostEstimate(flops=9 * 10**9, bytes_accessed=4 * 10**7, transcendentals=4 * 10**6),
         name="gate",
-    )(y, normed, dy, *zo, gain)
-
-
-def input_kernel(tokens_ref, dy_ref, gz_ref, gp_ref, mixed_ref, zo0_ref, zo1_ref, wx_ref, gain_ref, grad_ref, out_ref):
+    )(core, y, normed, dy, *zo, gain)
+
+
+def input_kernel(core_ref, tokens_ref, dy_ref, gz_ref, gp_ref, mixed_ref, mine_ref, other_ref, *refs):
+    in_core_order(
+        core_ref,
+        mine_ref,
+        other_ref,
+        lambda zo: input_body(tokens_ref, dy_ref, gz_ref, gp_ref, mixed_ref, zo, *refs),
+    )
+
+
+def input_body(tokens_ref, dy_ref, gz_ref, gp_ref, mixed_ref, zo, wx_ref, gain_ref, grad_ref, out_ref):
     width, inner = tokens_ref.shape[1], gz_ref.shape[1]
     g_normed = mm_nt(gp_ref[...], wx_ref[...])
     for k in range(0, inner, width):
         lanes = slice(k, k + width)
-        g_normed = g_normed + mm_nt(gz_ref[:, lanes], z_weight((zo0_ref, zo1_ref), lanes))
+        g_normed = g_normed + mm_nt(gz_ref[:, lanes], z_weight(zo, lanes))
     inputs = tokens_ref[...].astype(F32)
     inv = lax.rsqrt(jnp.mean(inputs * inputs, axis=1, keepdims=True) + EPS)
     unit = inputs * inv
@@ -438,24 +464,25 @@
     total = inputs
     for k in range(0, inner, 2 * LANES):
         lanes = slice(k, k + 2 * LANES)
-        total = total + mm(mixed_ref[:, lanes], out_weight_rows((zo0_ref, zo1_ref), lanes))
+        total = total + mm(mixed_ref[:, lanes], out_weight_rows(zo, lanes))
     out_ref[...] = total.astype(BF)
 
 
-def input_gradient(tokens, dy, gz, gp, mixed_out, zo, w_x, gain):
+def input_gradient(core, tokens, dy, gz, gp, mixed_out, zo, w_x, gain):
     length, width = tokens.shape
     rows = 256
     block = lambda v: pl.BlockSpec((rows, v.shape[1]), lambda i: (i, 0))
     return pl.pallas_call(
         input_kernel,
         grid=(length // rows,),
-        in_specs=[block(v) for v in (tokens, dy, gz, gp, mixed_out)] + [full(v.shape) for v in (*zo, w_x, gain)],
+        in_specs=[pl.BlockSpec(memory_space=pltpu.SMEM)]
+        + [block(v) for v in (tokens, dy, gz, gp, mixed_out)] + [full(v.shape) for v in (*zo, w_x, gain)],
         out_specs=[block(tokens)] * 2,
         out_shape=[jax.ShapeDtypeStruct((length, width), BF)] * 2,
         compiler_params=PARAMS,
         cost_estimate=pl.CostEstimate(flops=10**7, bytes_accessed=10**5, transcendentals=0),
         name="input_gradient",
-    )(tokens, dy, gz, gp, mixed_out, *zo, w_x, gain)
+    )(core, tokens, dy, gz, gp, mixed_out, *zo, w_x, gain)
 
 
 def document_info(resets):
@@ -619,19 +646,17 @@
     xbc = mm(normed, w_x)
     y, pre, sin = scan_forward(xbc, col, row, cw8, hp8, sk8)
     zo_all, y = barrier((zo_all, y))
-    zo_other = other_core(zo_all, reps)
-    zo = (jnp.where(core == 0, zo_all, zo_other), jnp.where(core == 0, zo_other, zo_all))
-    mixed_out, gy, gz, gg_grad = gate(y, normed, cotangent, zo, gg8)
+    zo = (zo_all, other_core(zo_all, reps))
+    core_at = jnp.reshape(core, (1,))
+    mixed_out, gy, gz, gg_grad = gate(core_at, y, normed, cotangent, zo, gg8)
 
     def grad_of(left, right):
         return lax.dot_general(left, right, (((0,), (0,)), ((), ())), preferred_element_type=F32).astype(BF)
 
     out_grad = sum_cores(grad_of(mixed_out, cotangent).reshape(shards, 2, 2 * half, width), core, reps)
-    z_grads = [
-        sum_cores(grad_of(normed, gz[:, k : k + width]).reshape(shards, 2, half, width), core, reps)
-        for k in (0, width)
-    ]
-    zo_sum, gy = barrier((jnp.concatenate(z_grads + [out_grad], axis=1), gy))
+    z_grad = sum_cores(grad_of(normed, gz).reshape(shards, 2, half, inner), core, reps)
+    zo_sum = jnp.concatenate([z_grad[:, :, :width], z_grad[:, :, width:], out_grad], axis=1)
+    zo_sum, gy = barrier((zo_sum, gy))
     zo_own = lax.psum_scatter(zo_sum, "shard", scatter_dimension=0)
     gp, cwg, hpg, skg = scan_backward(xbc, pre, y, gy, sin, col, row, cw8, hp8, sk8)
     cut = (mixed + LANES) // (3 * LANES) * 2 * LANES
@@ -640,7 +665,7 @@
     x_theirs = other_core(x_theirs, reps)
     x_sums = [add(x_mine[:, :, s], x_theirs[:, :, s]) for s in (slice(0, cut), slice(cut, mixed + LANES))]
     x_sums, gp = barrier((x_sums, gp))
-    input_grad, output = input_gradient(tokens, cotangent, gz, gp, mixed_out, zo, w_x, rows8(gain))
+    input_grad, output = input_gradient(core_at, tokens, cotangent, gz, gp, mixed_out, zo, w_x, rows8(gain))
 
     grads = (cwg[:4], cwg[4], hpg[0, :heads], hpg[1, :heads], skg[0].reshape(heads, WIDTH).sum(axis=1), gg_grad[0])
     split = lambda v: jnp.moveaxis(v.reshape(v.shape[:-1] + (shards, -1)), -2, 0).reshape(shards, -1)

time: 346 us -> 338 us (0.977)
  other arithmetic: 28.1 us -> 21.7 us
    select_n x1 -> x0, other arithmetic: 5.78 us -> none  [on_device(): jnp.where(core == 0, zo_other, zo_all)]
    squeeze x6 -> x5, local copies, waits for them, and re-layouts: 7.98 us -> 4.44 us  [half_of(): pick = lambda k: lax.dynamic_index_in_dim(value, k, axis, keepdims=False)]
    unnamed x75 -> x91, local copies, waits for them, and re-layouts: 8.58 us -> 11.4 us
    dot_general x4 -> x3, matrix products: 21.9 us -> 20.6 us  [grad_of(): lax.dot_general(left, right, (((0,), (0,)), ((), ())), preferred_element_...]
    ppermute x9 -> x8, waiting for transfers between devices: 15.8 us -> 16.6 us  [other_core(): return lax.ppermute(value, 'rep', pairs(reps, 1))]
  transfers between devices with their start and end apart: 37 -> 36, of which waited for: 16 -> 17; matrix products, arithmetic and copies ran while one was open for 19% -> 17% of each run, Pallas kernels for 29% -> 30%
where the time goes in v5:
time: 338 us; the launch traced here: 332 us
  Pallas kernels  121 us (36%)
  waiting for transfers between devices  72.1 us (21%)
  starting transfers between devices  39.8 us (12%)
  local copies, waits for them, and re-layouts  33.3 us (10%)
  matrix products  28.8 us (9%)
  other arithmetic  21.7 us (6%)
  between operations  15.2 us (4%)
    pallas_call x1, Pallas kernels, scan_backward(): pl.pallas_call(partial(bwd_kernel, inner), grid=(blocks,), in_specs=[pl.B...  52 us
    ppermute x6, waiting for transfers between devices, from_behind(): lax.ppermute(block, 'shard', [(i, (i + 2 * k) % 8) for i in range(8)])  24.8 us
    pallas_call x1, Pallas kernels, scan_forward(): pl.pallas_call(partial(fwd_kernel, inner), grid=(blocks,), in_specs=[pl.B...  24.3 us
    pallas_call x1, Pallas kernels, input_gradient(): pl.pallas_call(input_kernel, grid=(length // rows,), in_specs=[pl.BlockSp...  23.9 us
    pallas_call x1, Pallas kernels, gate(): pl.pallas_call(gate_kernel, grid=(length // rows,), in_specs=[pl.BlockSpe...  21.2 us
    dot_general x3, matrix products, grad_of(): lax.dot_general(left, right, (((0,), (0,)), ((), ())), preferred_element_...  20.6 us
    ppermute x9, waiting for transfers between devices, along_z(): lax.ppermute(entry, 'shard', [(i, (i + 2 * k) % 8) for i in range(8)])  18.2 us
    ppermute x8, waiting for transfers between devices, other_core(): return lax.ppermute(value, 'rep', pairs(reps, 1))  16.6 us
  transfers between devices with their start and end apart: 36, of which 17 were waited for; matrix products, arithmetic and copies ran while one was open for 17% of the time, Pallas kernels for 30%

profile of v5, /device:TPU:0, one launch (start us, length us, event | category | flops | bytes accessed | tf_op | source)
XLA Modules:
  0.0 332.4 jit_solution(10553248422540636428)
XLA Ops:
  10.0 3.0 collective-permute-start
  22.2 2.7 collective-permute-start.7
  26.9 3.2 collective-permute-start.3
  39.7 23.1 %collective-permute-done.9 = bf16[64,2432]{1,0:T(8,128)(2,1)S(1)} collective-permute-done((bf16[64,2432]{1,0:T(8,128)(2,1)}, bf16[64,2432]{1,0:T(8,128)(2,1)S(1)}, u32[]{:S(2)}, u32[]{:S(2)}) %collective-permute-start.9) | collective-permute-done | bytes 311328 | tf_op jit(solution)/shard_map/ppermute | solution.py:548
  75.5 2.9 select_bitcast_fusion.1
  78.9 8.1 %fusion.32.xbc_ref = f32[1024,2432]{1,0:T(8,128)} fusion(bf16[1024,1024]{1,0:T(8,128)(2,1)S(1)} %fusion.2.normed_ref, bf16[1024,2432]{1,0:T(8,128)(2,1)S(1)} %bitcast.149), kind=kOutput, calls=%fused_computation.145 | convolution fusion | flops 5100273664 | bytes 17039360 | tf_op jit(solution)/shard_map/dot_general | solution.py:21
  87.1 24.3 %scan_forward.1 = (f32[1024,2048]{1,0:T(8,128)}, f32[1024,2304]{1,0:T(8,128)}, bf16[1024,2048]{1,0:T(8,128)(2,1)}) custom-call(f32[1024,2432]{1,0:T(8,128)} %fusion.32.xbc_ref, f32[1024,16]{1,0:T(8,128)S(1)} %copy.61.col_ref, f32[8,1024]{1,0:T(8,128)S(1)} %broadcast_in_dim.82.row_ref, f32[8,2304]{1,0:T(8,128)S(1)} %maximum_maximum_fusion.cw_ref, ...), custom_call_target="tpu_custom_call" | custom-call | flops 6000000000 | bytes 30000000 | tf_op jit(solution)/shard_map/scan_forward/pallas_call | solution.py:356
  112.6 7.4 %collective-permute-done.12.other_ref = bf16[8,256,1024]{2,1,0:T(8,128)(2,1)} collective-permute-done((bf16[8,256,1024]{2,1,0:T(8,128)(2,1)}, bf16[8,256,1024]{2,1,0:T(8,128)(2,1)}, u32[]{:S(2)}, u32[]{:S(2)}) %collective-permute-start.12) | collective-permute-done | bytes 4194336 | tf_op jit(solution)/shard_map/ppermute | solution.py:515
  120.0 21.2 %gate.1 = (bf16[1024,2048]{1,0:T(8,128)(2,1)}, bf16[1024,2048]{1,0:T(8,128)(2,1)}, bf16[1024,2048]{1,0:T(8,128)(2,1)}, f32[8,2048]{1,0:T(8,128)S(1)}) custom-call(s32[1]{0:T(128)} %bitcast.36.core_ref, f32[1024,2048]{1,0:T(8,128)} %get-tuple-element.66.y_ref, bf16[1024,1024]{1,0:T(8,128)(2,1)} %copy-done.13, bf16[1024,1024]{1,0:T(8,128)(2,1)} %dy_ref.3, ...), custom_call_target="tpu_custom_call" | custom-call | flops 8999999488 | bytes 40000000 | tf_op jit(solution)/shard_map/gate/pallas_call | solution.py:427
  141.3 7.3 %convolution_convert_fusion.2 = bf16[1024,2048]{1,0:T(8,128)(2,1)S(1)} fusion(bf16[1024,1024]{1,0:T(8,128)(2,1)S(1)} %copy-done.14, bf16[1024,2048]{1,0:T(8,128)(2,1)} %get-tuple-element.68.gz_ref), kind=kOutput, calls=%fused_computation.14 | convolution fusion | flops 4297064448 | bytes 10485760 | tf_op jit(solution)/shard_map/dot_general | solution.py:654
  153.0 4.9 %convolution_convert_fusion.1 = bf16[2048,1024]{1,0:T(8,128)(2,1)S(1)} fusion(bf16[1024,2048]{1,0:T(8,128)(2,1)S(1)} %copy-done.8, bf16[1024,1024]{1,0:T(8,128)(2,1)S(1)} %copy-done.12), kind=kOutput, calls=%fused_computation.13 | convolution fusion | flops 4297064448 | bytes 10485760 | tf_op jit(solution)/shard_map/dot_general | solution.py:654
  161.7 3.0 fusion.4
  172.8 52.0 %scan_backward.1 = (bf16[1024,2432]{1,0:T(8,128)(2,1)}, f32[8,2304]{1,0:T(8,128)S(1)}, f32[8,128]{1,0:T(8,128)S(1)}, f32[8,2048]{1,0:T(8,128)S(1)}) custom-call(f32[1024,2432]{1,0:T(8,128)} %fusion.32.xbc_ref, f32[1024,2304]{1,0:T(8,128)} %get-tuple-element.63.pre_ref, f32[1024,2048]{1,0:T(8,128)} %get-tuple-element.66.y_ref, ...), custom_call_target="tpu_custom_call" | custom-call | flops 20000000000 | bytes 50000000 | tf_op jit(solution)/shard_map/scan_backward/pallas_call | solution.py:387
  224.8 8.4 %convolution_convert_fusion = bf16[1024,2432]{1,0:T(8,128)(2,1)S(1)} fusion(bf16[1024,1024]{1,0:T(8,128)(2,1)S(1)} %copy-done.15, bf16[1024,2432]{1,0:T(8,128)(2,1)} %get-tuple-element.76.gp_ref), kind=kOutput, calls=%fused_computation.1 | convolution fusion | flops 5102764032 | bytes 12058624 | tf_op jit(solution)/shard_map/dot_general | solution.py:654
  234.1 4.3 %collective-permute-done.15 = bf16[8,64,2432]{2,1,0:T(8,128)(2,1)S(1)} collective-permute-done((bf16[8,64,2432]{2,1,0:T(8,128)(2,1)S(1)}, bf16[8,64,2432]{2,1,0:T(8,128)(2,1)S(1)}, u32[]{:S(2)}, u32[]{:S(2)}) %collective-permute-start.15) | collective-permute-done | bytes 2490400 | tf_op jit(solution)/shard_map/ppermute | solution.py:515
  243.0 4.0 %collective-permute-start.17 = (bf16[2,64,896]{2,1,0:T(8,128)(2,1)S(1)}, bf16[2,64,896]{2,1,0:T(8,128)(2,1)S(1)}, u32[]{:S(2)}, u32[]{:S(2)}) collective-permute-start(bf16[2,64,896]{2,1,0:T(8,128)(2,1)S(1)} %get-tuple-element.155), channel_id=1, source_target_pairs={{0,2},{1,3},{2,4},{3,5},{4,6},{5,7},{6,0},{7,1},{8,10},{9,11},{10,... | collective-permute-start | bytes 688136 | tf_op jit(solution)/shard_map/ppermute | solution.py:574
  246.9 2.8 collective-permute-start.18
  251.0 23.9 %input_gradient.1 = (bf16[1024,1024]{1,0:T(8,128)(2,1)}, bf16[1024,1024]{1,0:T(8,128)(2,1)}) custom-call(s32[1]{0:T(128)} %bitcast.36.core_ref, bf16[1024,1024]{1,0:T(8,128)(2,1)} %tokens_ref.1, bf16[1024,1024]{1,0:T(8,128)(2,1)} %dy_ref.3, bf16[1024,2048]{1,0:T(8,128)(2,1)} %get-tuple-element.68.gz_ref, bf16[1024,2432]{1,0:T(8,128)(2,1)} %get-tuple-element.76.gp_ref, ...), custom_call_target="tpu_custom_call" | custom-call | flops 10000000 | bytes 100000 | tf_op jit(solution)/shard_map/input_gradient/pallas_call | solution.py:475
  275.0 7.9 %collective-permute-done.19 = bf16[2,64,896]{2,1,0:T(8,128)(2,1)S(1)} collective-permute-done((bf16[2,64,896]{2,1,0:T(8,128)(2,1)S(1)}, bf16[2,64,896]{2,1,0:T(8,128)(2,1)S(1)}, u32[]{:S(2)}, u32[]{:S(2)}) %collective-permute-start.19) | collective-permute-done | bytes 229408 | tf_op jit(solution)/shard_map/ppermute | solution.py:574
  283.0 3.8 %collective-permute-start.28 = (f32[1708]{0:T(1024)S(1)}, f32[1708]{0:T(1024)S(1)}, u32[]{:S(2)}, u32[]{:S(2)}) collective-permute-start(f32[1708]{0:T(1024)S(1)} %get-tuple-element.130), channel_id=1, source_target_pairs={{0,6},{1,7},{2,0},{3,1},{4,2},{5,3},{6,4},{7,5},{8,14},{9,15},{10,... | collective-permute-start | bytes 20504 | tf_op jit(solution)/shard_map/ppermute | solution.py:574
  290.4 3.3 collective-permute-start.23
  296.5 3.3 collective-permute-done.25
  301.3 8.9 %collective-permute-done.24 = bf16[64,1536]{1,0:T(8,128)(2,1)S(1)} collective-permute-done((bf16[64,1536]{1,0:T(8,128)(2,1)S(1)}, bf16[64,1536]{1,0:T(8,128)(2,1)S(1)}, u32[]{:S(2)}, u32[]{:S(2)}) %collective-permute-start.24) | collective-permute-done | bytes 196640 | tf_op jit(solution)/shard_map/ppermute | solution.py:574
  316.4 3.3 collective-permute-done.31
  (282 shorter events, 80.2 us)
Async XLA Ops:
  7.3 105.3 %all-gather.3.cloned.1.call-start = ((), (), s32[]{:S(2)}) async-start(), calls=%async_computation.2 | async-start | bytes 4718592 | tf_op jit(solution)/shard_map/all_gather | solution.py:624
  10.0 23.3 %collective-permute-start = (bf16[64,2432]{1,0:T(8,128)(2,1)}, bf16[64,2432]{1,0:T(8,128)(2,1)S(1)}, u32[]{:S(2)}, u32[]{:S(2)}) collective-permute-start(bf16[64,2432]{1,0:T(8,128)(2,1)} %pad.35), channel_id=1, source_target_pairs={{0,2},{1,3},{2,4},{3,5},{4,6},{5,7},{6,0},{7,1},{8,10},{9,11},{10,... | collective-permute-start | bytes 933896 | tf_op jit(solution)/shard_map/ppermute | solution.py:548
  13.0 24.4 %collective-permute-start.1 = (bf16[64,2432]{1,0:T(8,128)(2,1)}, bf16[64,2432]{1,0:T(8,128)(2,1)S(1)}, u32[]{:S(2)}, u32[]{:S(2)}) collective-permute-start(bf16[64,2432]{1,0:T(8,128)(2,1)} %pad.35), channel_id=1, source_target_pairs={{0,1},{1,0},{2,3},{3,2},{4,5},{5,4},{6,7},{7,6},{8,9},{9,8},{10,11... | collective-permute-start | bytes 933896 | tf_op jit(solution)/shard_map/ppermute | solution.py:560
  14.8 7.3 %collective-permute-start.5 = (bf16[2,1024]{1,0:T(2,128)(2,1)S(1)}, bf16[2,1024]{1,0:T(2,128)(2,1)S(1)}, u32[]{:S(2)}, u32[]{:S(2)}) collective-permute-start(bf16[2,1024]{1,0:T(2,128)(2,1)S(1)} %reshape.304), channel_id=1, source_target_pairs={{0,1},{1,0},{2,3},{3,2},{4,5},{5,4},{6,7},{7,6},{8,9},{9,8},{10,11... | collective-permute-start | bytes 12296 | tf_op jit(solution)/shard_map/ppermute | solution.py:551
  26.9 12.1 %collective-permute-start.3 = (bf16[64,2432]{1,0:T(8,128)(2,1)}, bf16[64,2432]{1,0:T(8,128)(2,1)S(1)}, u32[]{:S(2)}, u32[]{:S(2)}) collective-permute-start(bf16[64,2432]{1,0:T(8,128)(2,1)} %pad.35), channel_id=1, source_target_pairs={{0,6},{1,7},{2,0},{3,1},{4,2},{5,3},{6,4},{7,5},{8,14},{9,15},{10,... | collective-permute-start | bytes 933896 | tf_op jit(solution)/shard_map/ppermute | solution.py:548
  30.1 32.7 %collective-permute-start.9 = (bf16[64,2432]{1,0:T(8,128)(2,1)}, bf16[64,2432]{1,0:T(8,128)(2,1)S(1)}, u32[]{:S(2)}, u32[]{:S(2)}) collective-permute-start(bf16[64,2432]{1,0:T(8,128)(2,1)} %pad.35), channel_id=1, source_target_pairs={{0,4},{1,5},{2,6},{3,7},{4,0},{5,1},{6,2},{7,3},{8,12},{9,13},{10,... | collective-permute-start | bytes 933896 | tf_op jit(solution)/shard_map/ppermute | solution.py:548
  33.2 30.4 %collective-permute-start.2 = (bf16[64,2432]{1,0:T(8,128)(2,1)S(1)}, bf16[64,2432]{1,0:T(8,128)(2,1)}, u32[]{:S(2)}, u32[]{:S(2)}) collective-permute-start(bf16[64,2432]{1,0:T(8,128)(2,1)S(1)} %collective-permute-done), channel_id=1, source_target_pairs={{0,1},{1,0},{2,3},{3,2},{4,5},{5,4},{6,7},{7,6},{8,9},{9,8},{10,11... | collective-permute-start | bytes 933896 | tf_op jit(solution)/shard_map/ppermute | solution.py:560
  34.8 248.0 %reduce-scatter.2.cloned.1.call-start = ((), (), s32[]{:S(2)}) async-start(), calls=%async_computation.1 | async-start | bytes 4718592 | tf_op jit(solution)/shard_map/reduce_scatter | solution.py:660
  39.0 27.2 %collective-permute-start.4 = (bf16[64,2432]{1,0:T(8,128)(2,1)S(1)}, bf16[64,2432]{1,0:T(8,128)(2,1)S(1)}, u32[]{:S(2)}, u32[]{:S(2)}) collective-permute-start(bf16[64,2432]{1,0:T(8,128)(2,1)S(1)} %collective-permute-done.3), channel_id=1, source_target_pairs={{0,1},{1,0},{2,3},{3,2},{4,5},{5,4},{6,7},{7,6},{8,9},{9,8},{10,11... | collective-permute-start | bytes 933896 | tf_op jit(solution)/shard_map/ppermute | solution.py:560
  112.5 7.5 %collective-permute-start.12 = (bf16[8,256,1024]{2,1,0:T(8,128)(2,1)}, bf16[8,256,1024]{2,1,0:T(8,128)(2,1)}, u32[]{:S(2)}, u32[]{:S(2)}) collective-permute-start(bf16[8,256,1024]{2,1,0:T(8,128)(2,1)} %bitcast.153), channel_id=1, source_target_pairs={{0,8},{8,0},{16,24},{24,16},{1,9},{9,1},{17,25},{25,17},{2,10},{10... | collective-permute-start | bytes 12582920 | tf_op jit(solution)/shard_map/ppermute | solution.py:515
  150.1 11.6 %collective-permute-start.13 = (bf16[8,64,2048]{2,1,0:T(8,128)(2,1)}, bf16[8,64,2048]{2,1,0:T(8,128)(2,1)}, u32[]{:S(2)}, u32[]{:S(2)}) collective-permute-start(bf16[8,64,2048]{2,1,0:T(8,128)(2,1)} %dynamic-slice_bitcast_fusion.3), channel_id=1, source_target_pairs={{0,8},{8,0},{16,24},{24,16},{1,9},{9,1},{17,25},{25,17},{2,10},{10... | collective-permute-start | bytes 6291464 | tf_op jit(solution)/shard_map/ppermute | solution.py:515
  240.0 42.8 %collective-permute-start.16 = (bf16[4,64,1536]{2,1,0:T(8,128)(2,1)}, bf16[4,64,1536]{2,1,0:T(8,128)(2,1)}, u32[]{:S(2)}, u32[]{:S(2)}) collective-permute-start(bf16[4,64,1536]{2,1,0:T(8,128)(2,1)} %get-tuple-element.145), channel_id=1, source_target_pairs={{0,1},{1,0},{2,3},{3,2},{4,5},{5,4},{6,7},{7,6},{8,9},{9,8},{10,11... | collective-permute-start | bytes 2359304 | tf_op jit(solution)/shard_map/ppermute | solution.py:580
  243.0 32.0 %collective-permute-start.17 = (bf16[2,64,896]{2,1,0:T(8,128)(2,1)S(1)}, bf16[2,64,896]{2,1,0:T(8,128)(2,1)S(1)}, u32[]{:S(2)}, u32[]{:S(2)}) collective-permute-start(bf16[2,64,896]{2,1,0:T(8,128)(2,1)S(1)} %get-tuple-element.155), channel_id=1, source_target_pairs={{0,2},{1,3},{2,4},{3,5},{4,6},{5,7},{6,0},{7,1},{8,10},{9,11},{10,... | collective-permute-start | bytes 688136 | tf_op jit(solution)/shard_map/ppermute | solution.py:574
  246.9 28.0 %collective-permute-start.18 = (bf16[2,64,896]{2,1,0:T(8,128)(2,1)S(1)}, bf16[2,64,896]{2,1,0:T(8,128)(2,1)S(1)}, u32[]{:S(2)}, u32[]{:S(2)}) collective-permute-start(bf16[2,64,896]{2,1,0:T(8,128)(2,1)S(1)} %get-tuple-element.154), channel_id=1, source_target_pairs={{0,6},{1,7},{2,0},{3,1},{4,2},{5,3},{6,4},{7,5},{8,14},{9,15},{10,... | collective-permute-start | bytes 688136 | tf_op jit(solution)/shard_map/ppermute | solution.py:574
  249.7 33.1 %collective-permute-start.19 = (bf16[2,64,896]{2,1,0:T(8,128)(2,1)S(1)}, bf16[2,64,896]{2,1,0:T(8,128)(2,1)S(1)}, u32[]{:S(2)}, u32[]{:S(2)}) collective-permute-start(bf16[2,64,896]{2,1,0:T(8,128)(2,1)S(1)} %get-tuple-element.153), channel_id=1, source_target_pairs={{0,4},{1,5},{2,6},{3,7},{4,0},{5,1},{6,2},{7,3},{8,12},{9,13},{10,... | collective-permute-start | bytes 688136 | tf_op jit(solution)/shard_map/ppermute | solution.py:574
  250.3 24.7 %collective-permute-start.21 = (f32[4,1708]{1,0:T(4,128)S(1)}, f32[4,1708]{1,0:T(4,128)S(1)}, u32[]{:S(2)}, u32[]{:S(2)}) collective-permute-start(f32[4,1708]{1,0:T(4,128)S(1)} %bitcast.178), channel_id=1, source_target_pairs={{0,1},{1,0},{2,3},{3,2},{4,5},{5,4},{6,7},{7,6},{8,9},{9,8},{10,11... | collective-permute-start | bytes 81992 | tf_op jit(solution)/shard_map/ppermute | solution.py:580
  282.9 7.5 %collective-permute-start.27 = (f32[1708]{0:T(1024)S(1)}, f32[1708]{0:T(1024)S(1)}, u32[]{:S(2)}, u32[]{:S(2)}) collective-permute-start(f32[1708]{0:T(1024)S(1)} %get-tuple-element.131), channel_id=1, source_target_pairs={{0,2},{1,3},{2,4},{3,5},{4,6},{5,7},{6,0},{7,1},{8,10},{9,11},{10,... | collective-permute-start | bytes 20504 | tf_op jit(solution)/shard_map/ppermute | solution.py:574
  283.0 10.8 %collective-permute-start.28 = (f32[1708]{0:T(1024)S(1)}, f32[1708]{0:T(1024)S(1)}, u32[]{:S(2)}, u32[]{:S(2)}) collective-permute-start(f32[1708]{0:T(1024)S(1)} %get-tuple-element.130), channel_id=1, source_target_pairs={{0,6},{1,7},{2,0},{3,1},{4,2},{5,3},{6,4},{7,5},{8,14},{9,15},{10,... | collective-permute-start | bytes 20504 | tf_op jit(solution)/shard_map/ppermute | solution.py:574
  286.8 8.1 %collective-permute-start.29 = (f32[1708]{0:T(1024)S(1)}, f32[1708]{0:T(1024)S(1)}, u32[]{:S(2)}, u32[]{:S(2)}) collective-permute-start(f32[1708]{0:T(1024)S(1)} %get-tuple-element.129), channel_id=1, source_target_pairs={{0,4},{1,5},{2,6},{3,7},{4,0},{5,1},{6,2},{7,3},{8,12},{9,13},{10,... | collective-permute-start | bytes 20504 | tf_op jit(solution)/shard_map/ppermute | solution.py:574
  286.8 23.3 %collective-permute-start.26 = (bf16[256,1024]{1,0:T(8,128)(2,1)}, bf16[256,1024]{1,0:T(8,128)(2,1)S(1)}, u32[]{:S(2)}, u32[]{:S(2)}) collective-permute-start(bf16[256,1024]{1,0:T(8,128)(2,1)} %bitcast.165), channel_id=1, source_target_pairs={{0,16},{8,24},{16,0},{24,8},{1,17},{9,25},{17,1},{25,9},{2,18},{10... | collective-permute-start | bytes 1572872 | tf_op jit(solution)/shard_map/ppermute | solution.py:687
  289.7 10.1 %collective-permute-start.22 = (bf16[64,1536]{1,0:T(8,128)(2,1)S(1)}, bf16[64,1536]{1,0:T(8,128)(2,1)S(1)}, u32[]{:S(2)}, u32[]{:S(2)}) collective-permute-start(bf16[64,1536]{1,0:T(8,128)(2,1)S(1)} %get-tuple-element.159), channel_id=1, source_target_pairs={{0,2},{1,3},{2,4},{3,5},{4,6},{5,7},{6,0},{7,1},{8,10},{9,11},{10,... | collective-permute-start | bytes 589832 | tf_op jit(solution)/shard_map/ppermute | solution.py:574
  290.4 10.8 %collective-permute-start.23 = (bf16[64,1536]{1,0:T(8,128)(2,1)S(1)}, bf16[64,1536]{1,0:T(8,128)(2,1)S(1)}, u32[]{:S(2)}, u32[]{:S(2)}) collective-permute-start(bf16[64,1536]{1,0:T(8,128)(2,1)S(1)} %get-tuple-element.158), channel_id=1, source_target_pairs={{0,6},{1,7},{2,0},{3,1},{4,2},{5,3},{6,4},{7,5},{8,14},{9,15},{10,... | collective-permute-start | bytes 589832 | tf_op jit(solution)/shard_map/ppermute | solution.py:574
  293.8 16.4 %collective-permute-start.24 = (bf16[64,1536]{1,0:T(8,128)(2,1)S(1)}, bf16[64,1536]{1,0:T(8,128)(2,1)S(1)}, u32[]{:S(2)}, u32[]{:S(2)}) collective-permute-start(bf16[64,1536]{1,0:T(8,128)(2,1)S(1)} %get-tuple-element.157), channel_id=1, source_target_pairs={{0,4},{1,5},{2,6},{3,7},{4,0},{5,1},{6,2},{7,3},{8,12},{9,13},{10,... | collective-permute-start | bytes 589832 | tf_op jit(solution)/shard_map/ppermute | solution.py:574
  310.9 8.7 %collective-permute-start.31 = (bf16[64,2432]{1,0:T(8,128)(2,1)S(1)}, bf16[64,2432]{1,0:T(8,128)(2,1)S(1)}, u32[]{:S(2)}, u32[]{:S(2)}) collective-permute-start(bf16[64,2432]{1,0:T(8,128)(2,1)S(1)} %pad_maximum_fusion.6), channel_id=1, source_target_pairs={{0,16},{8,24},{16,0},{24,8},{1,17},{9,25},{17,1},{25,9},{2,18},{10... | collective-permute-start | bytes 933896 | tf_op jit(solution)/shard_map/ppermute | solution.py:536
  (54 other events, 734.0 us)
Sparse Core Ops, SparseCore 0:
  34.9 77.5 all-gather.2
  171.9 108.1 reduce-scatter.1

commit v6 on v5

--- a/solution.py
+++ b/solution.py
@@ -659,7 +659,7 @@
     zo_sum, gy = barrier((zo_sum, gy))
     zo_own = lax.psum_scatter(zo_sum, "shard", scatter_dimension=0)
     gp, cwg, hpg, skg = scan_backward(xbc, pre, y, gy, sin, col, row, cw8, hp8, sk8)
-    cut = (mixed + LANES) // (3 * LANES) * 2 * LANES
+    cut = (mixed + 2 * LANES) // (2 * LANES) * LANES
     x_grad = grad_of(normed, gp).reshape(shards, 2, half, mixed + LANES)
     x_mine, x_theirs = half_of(x_grad, core, 1)
     x_theirs = other_core(x_theirs, reps)

time: 338 us -> 339 us (level)
  waiting for transfers between devices: 72.1 us -> 68 us
  other arithmetic: 21.7 us -> 25.4 us
    convert_element_type x8, other arithmetic: 2.44 us -> 6.22 us  [add(): return sum((v.astype(F32) for v in values)).astype(values[0].dtype)]
    ppermute x9, waiting for transfers between devices: 18.2 us -> 14.6 us  [along_z(): lax.ppermute(entry, 'shard', [(i, (i + 2 * k) % 8) for i in range(8)])]
    unnamed x91 -> x93, local copies, waits for them, and re-layouts: 11.4 us -> 11.4 us
  transfers between devices with their start and end apart: 36 -> 36, of which waited for: 17 -> 15; matrix products, arithmetic and copies ran while one was open for 17% -> 19% of each run, Pallas kernels for 30% -> 30%
where the time goes in v6:
time: 339 us; the launch traced here: 334 us
  Pallas kernels  122 us (36%)
  waiting for transfers between devices  68 us (20%)
  starting transfers between devices  39.5 us (12%)
  local copies, waits for them, and re-layouts  35.3 us (10%)
  matrix products  28.9 us (9%)
  other arithmetic  25.4 us (7%)
  between operations  15.2 us (4%)
    pallas_call x1, Pallas kernels, scan_backward(): pl.pallas_call(partial(bwd_kernel, inner), grid=(blocks,), in_specs=[pl.B...  52.3 us
    ppermute x6, waiting for transfers between devices, from_behind(): lax.ppermute(block, 'shard', [(i, (i + 2 * k) % 8) for i in range(8)])  24.9 us
    pallas_call x1, Pallas kernels, scan_forward(): pl.pallas_call(partial(fwd_kernel, inner), grid=(blocks,), in_specs=[pl.B...  24.4 us
    pallas_call x1, Pallas kernels, input_gradient(): pl.pallas_call(input_kernel, grid=(length // rows,), in_specs=[pl.BlockSp...  23.9 us
    pallas_call x1, Pallas kernels, gate(): pl.pallas_call(gate_kernel, grid=(length // rows,), in_specs=[pl.BlockSpe...  21.2 us
    dot_general x3, matrix products, grad_of(): lax.dot_general(left, right, (((0,), (0,)), ((), ())), preferred_element_...  20.6 us
    ppermute x9, starting transfers between devices, along_z(): lax.ppermute(entry, 'shard', [(i, (i + 2 * k) % 8) for i in range(8)])  16.6 us
    ppermute x8, waiting for transfers between devices, other_core(): return lax.ppermute(value, 'rep', pairs(reps, 1))  15.1 us
  transfers between devices with their start and end apart: 36, of which 15 were waited for; matrix products, arithmetic and copies ran while one was open for 19% of the time, Pallas kernels for 30%

profile of v6, /device:TPU:0, one launch (start us, length us, event | category | flops | bytes accessed | tf_op | source)
XLA Modules:
  0.0 334.2 jit_solution(1654993061958789654)
XLA Ops:
  10.0 3.0 collective-permute-start
  22.2 2.7 collective-permute-start.7
  26.9 3.2 collective-permute-start.3
  39.7 23.1 %collective-permute-done.9 = bf16[64,2432]{1,0:T(8,128)(2,1)S(1)} collective-permute-done((bf16[64,2432]{1,0:T(8,128)(2,1)}, bf16[64,2432]{1,0:T(8,128)(2,1)S(1)}, u32[]{:S(2)}, u32[]{:S(2)}) %collective-permute-start.9) | collective-permute-done | bytes 311328 | tf_op jit(solution)/shard_map/ppermute | solution.py:548
  75.5 2.9 select_bitcast_fusion.1
  79.0 8.2 %fusion.32.xbc_ref = f32[1024,2432]{1,0:T(8,128)} fusion(bf16[1024,1024]{1,0:T(8,128)(2,1)S(1)} %fusion.2.normed_ref, bf16[1024,2432]{1,0:T(8,128)(2,1)S(1)} %bitcast.149), kind=kOutput, calls=%fused_computation.145 | convolution fusion | flops 5100273664 | bytes 17039360 | tf_op jit(solution)/shard_map/dot_general | solution.py:21
  87.2 24.4 %scan_forward.1 = (f32[1024,2048]{1,0:T(8,128)}, f32[1024,2304]{1,0:T(8,128)}, bf16[1024,2048]{1,0:T(8,128)(2,1)}) custom-call(f32[1024,2432]{1,0:T(8,128)} %fusion.32.xbc_ref, f32[1024,16]{1,0:T(8,128)S(1)} %copy.61.col_ref, f32[8,1024]{1,0:T(8,128)S(1)} %broadcast_in_dim.82.row_ref, f32[8,2304]{1,0:T(8,128)S(1)} %maximum_maximum_fusion.cw_ref, ...), custom_call_target="tpu_custom_call" | custom-call | flops 6000000000 | bytes 30000000 | tf_op jit(solution)/shard_map/scan_forward/pallas_call | solution.py:356
  112.7 7.4 %collective-permute-done.12.other_ref = bf16[8,256,1024]{2,1,0:T(8,128)(2,1)} collective-permute-done((bf16[8,256,1024]{2,1,0:T(8,128)(2,1)}, bf16[8,256,1024]{2,1,0:T(8,128)(2,1)}, u32[]{:S(2)}, u32[]{:S(2)}) %collective-permute-start.12) | collective-permute-done | bytes 4194336 | tf_op jit(solution)/shard_map/ppermute | solution.py:515
  120.1 21.2 %gate.1 = (bf16[1024,2048]{1,0:T(8,128)(2,1)}, bf16[1024,2048]{1,0:T(8,128)(2,1)}, bf16[1024,2048]{1,0:T(8,128)(2,1)}, f32[8,2048]{1,0:T(8,128)S(1)}) custom-call(s32[1]{0:T(128)} %bitcast.36.core_ref, f32[1024,2048]{1,0:T(8,128)} %get-tuple-element.66.y_ref, bf16[1024,1024]{1,0:T(8,128)(2,1)} %copy-done.14, bf16[1024,1024]{1,0:T(8,128)(2,1)} %dy_ref.3, ...), custom_call_target="tpu_custom_call" | custom-call | flops 8999999488 | bytes 40000000 | tf_op jit(solution)/shard_map/gate/pallas_call | solution.py:427
  141.3 7.3 %convolution_convert_fusion.2 = bf16[1024,2048]{1,0:T(8,128)(2,1)S(1)} fusion(bf16[1024,1024]{1,0:T(8,128)(2,1)S(1)} %copy-done.15, bf16[1024,2048]{1,0:T(8,128)(2,1)} %get-tuple-element.68.gz_ref), kind=kOutput, calls=%fused_computation.14 | convolution fusion | flops 4297064448 | bytes 10485760 | tf_op jit(solution)/shard_map/dot_general | solution.py:654
  153.1 4.9 %convolution_convert_fusion.1 = bf16[2048,1024]{1,0:T(8,128)(2,1)S(1)} fusion(bf16[1024,2048]{1,0:T(8,128)(2,1)S(1)} %copy-done.9, bf16[1024,1024]{1,0:T(8,128)(2,1)S(1)} %copy-done.13), kind=kOutput, calls=%fused_computation.13 | convolution fusion | flops 4297064448 | bytes 10485760 | tf_op jit(solution)/shard_map/dot_general | solution.py:654
  161.7 3.0 fusion.4
  172.7 52.3 %scan_backward.1 = (bf16[1024,2432]{1,0:T(8,128)(2,1)}, f32[8,2304]{1,0:T(8,128)S(1)}, f32[8,128]{1,0:T(8,128)S(1)}, f32[8,2048]{1,0:T(8,128)S(1)}) custom-call(f32[1024,2432]{1,0:T(8,128)} %fusion.32.xbc_ref, f32[1024,2304]{1,0:T(8,128)} %get-tuple-element.63.pre_ref, f32[1024,2048]{1,0:T(8,128)} %get-tuple-element.66.y_ref, ...), custom_call_target="tpu_custom_call" | custom-call | flops 20000000000 | bytes 50000000 | tf_op jit(solution)/shard_map/scan_backward/pallas_call | solution.py:387
  225.0 8.4 %convolution_convert_fusion = bf16[1024,2432]{1,0:T(8,128)(2,1)S(1)} fusion(bf16[1024,1024]{1,0:T(8,128)(2,1)S(1)} %copy-done.16, bf16[1024,2432]{1,0:T(8,128)(2,1)} %get-tuple-element.76.gp_ref), kind=kOutput, calls=%fused_computation.1 | convolution fusion | flops 5102764032 | bytes 12058624 | tf_op jit(solution)/shard_map/dot_general | solution.py:654
  236.3 4.0 %collective-permute-done.15 = bf16[8,64,2432]{2,1,0:T(8,128)(2,1)} collective-permute-done((bf16[8,64,2432]{2,1,0:T(8,128)(2,1)}, bf16[8,64,2432]{2,1,0:T(8,128)(2,1)}, u32[]{:S(2)}, u32[]{:S(2)}) %collective-permute-start.15) | collective-permute-done | bytes 2490400 | tf_op jit(solution)/shard_map/ppermute | solution.py:515
  247.4 4.0 %collective-permute-start.17 = (bf16[2,64,1152]{2,1,0:T(8,128)(2,1)}, bf16[2,64,1152]{2,1,0:T(8,128)(2,1)S(1)}, u32[]{:S(2)}, u32[]{:S(2)}) collective-permute-start(bf16[2,64,1152]{2,1,0:T(8,128)(2,1)} %get-tuple-element.149), channel_id=1, source_target_pairs={{0,2},{1,3},{2,4},{3,5},{4,6},{5,7},{6,0},{7,1},{8,10},{9,11},{10,... | collective-permute-start | bytes 884744 | tf_op jit(solution)/shard_map/ppermute | solution.py:574
  251.4 3.0 collective-permute-start.18
  255.9 23.9 %input_gradient.1 = (bf16[1024,1024]{1,0:T(8,128)(2,1)}, bf16[1024,1024]{1,0:T(8,128)(2,1)}) custom-call(s32[1]{0:T(128)} %bitcast.36.core_ref, bf16[1024,1024]{1,0:T(8,128)(2,1)} %tokens_ref.1, bf16[1024,1024]{1,0:T(8,128)(2,1)} %dy_ref.3, bf16[1024,2048]{1,0:T(8,128)(2,1)} %get-tuple-element.68.gz_ref, bf16[1024,2432]{1,0:T(8,128)(2,1)} %get-tuple-element.76.gp_ref, ...), custom_call_target="tpu_custom_call" | custom-call | flops 10000000 | bytes 100000 | tf_op jit(solution)/shard_map/input_gradient/pallas_call | solution.py:475
  279.8 9.5 %collective-permute-done.19 = bf16[2,64,1152]{2,1,0:T(8,128)(2,1)} collective-permute-done((bf16[2,64,1152]{2,1,0:T(8,128)(2,1)S(1)}, bf16[2,64,1152]{2,1,0:T(8,128)(2,1)}, u32[]{:S(2)}, u32[]{:S(2)}) %collective-permute-start.19) | collective-permute-done | bytes 294944 | tf_op jit(solution)/shard_map/ppermute | solution.py:574
  289.5 3.8 %collective-permute-start.28 = (f32[1708]{0:T(1024)S(1)}, f32[1708]{0:T(1024)S(1)}, u32[]{:S(2)}, u32[]{:S(2)}) collective-permute-start(f32[1708]{0:T(1024)S(1)} %get-tuple-element.130), channel_id=1, source_target_pairs={{0,6},{1,7},{2,0},{3,1},{4,2},{5,3},{6,4},{7,5},{8,14},{9,15},{10,... | collective-permute-start | bytes 20504 | tf_op jit(solution)/shard_map/ppermute | solution.py:574
  296.8 3.3 collective-permute-start.23
  302.3 4.2 %collective-permute-done.25 = bf16[64,1152]{1,0:T(8,128)(2,1)S(1)} collective-permute-done((bf16[64,1152]{1,0:T(8,128)(2,1)S(1)}, bf16[64,1152]{1,0:T(8,128)(2,1)S(1)}, u32[]{:S(2)}, u32[]{:S(2)}) %collective-permute-start.25) | collective-permute-done | bytes 147488 | tf_op jit(solution)/shard_map/ppermute | solution.py:580
  306.5 5.1 %collective-permute-done.24 = bf16[64,1280]{1,0:T(8,128)(2,1)S(1)} collective-permute-done((bf16[64,1280]{1,0:T(8,128)(2,1)S(1)}, bf16[64,1280]{1,0:T(8,128)(2,1)S(1)}, u32[]{:S(2)}, u32[]{:S(2)}) %collective-permute-start.24) | collective-permute-done | bytes 163872 | tf_op jit(solution)/shard_map/ppermute | solution.py:574
  317.9 3.5 %collective-permute-done.31 = bf16[64,2432]{1,0:T(8,128)(2,1)S(1)} collective-permute-done((bf16[64,2432]{1,0:T(8,128)(2,1)S(1)}, bf16[64,2432]{1,0:T(8,128)(2,1)S(1)}, u32[]{:S(2)}, u32[]{:S(2)}) %collective-permute-start.31) | collective-permute-done | bytes 311328 | tf_op jit(solution)/shard_map/ppermute | solution.py:536
  (284 shorter events, 82.3 us)
Async XLA Ops:
  7.3 105.3 %all-gather.3.cloned.1.call-start = ((), (), s32[]{:S(2)}) async-start(), calls=%async_computation.2 | async-start | bytes 4718592 | tf_op jit(solution)/shard_map/all_gather | solution.py:624
  10.0 23.3 %collective-permute-start = (bf16[64,2432]{1,0:T(8,128)(2,1)}, bf16[64,2432]{1,0:T(8,128)(2,1)S(1)}, u32[]{:S(2)}, u32[]{:S(2)}) collective-permute-start(bf16[64,2432]{1,0:T(8,128)(2,1)} %pad.35), channel_id=1, source_target_pairs={{0,2},{1,3},{2,4},{3,5},{4,6},{5,7},{6,0},{7,1},{8,10},{9,11},{10,... | collective-permute-start | bytes 933896 | tf_op jit(solution)/shard_map/ppermute | solution.py:548
  13.0 24.4 %collective-permute-start.1 = (bf16[64,2432]{1,0:T(8,128)(2,1)}, bf16[64,2432]{1,0:T(8,128)(2,1)S(1)}, u32[]{:S(2)}, u32[]{:S(2)}) collective-permute-start(bf16[64,2432]{1,0:T(8,128)(2,1)} %pad.35), channel_id=1, source_target_pairs={{0,1},{1,0},{2,3},{3,2},{4,5},{5,4},{6,7},{7,6},{8,9},{9,8},{10,11... | collective-permute-start | bytes 933896 | tf_op jit(solution)/shard_map/ppermute | solution.py:560
  26.9 12.0 %collective-permute-start.3 = (bf16[64,2432]{1,0:T(8,128)(2,1)}, bf16[64,2432]{1,0:T(8,128)(2,1)S(1)}, u32[]{:S(2)}, u32[]{:S(2)}) collective-permute-start(bf16[64,2432]{1,0:T(8,128)(2,1)} %pad.35), channel_id=1, source_target_pairs={{0,6},{1,7},{2,0},{3,1},{4,2},{5,3},{6,4},{7,5},{8,14},{9,15},{10,... | collective-permute-start | bytes 933896 | tf_op jit(solution)/shard_map/ppermute | solution.py:548
  30.1 32.7 %collective-permute-start.9 = (bf16[64,2432]{1,0:T(8,128)(2,1)}, bf16[64,2432]{1,0:T(8,128)(2,1)S(1)}, u32[]{:S(2)}, u32[]{:S(2)}) collective-permute-start(bf16[64,2432]{1,0:T(8,128)(2,1)} %pad.35), channel_id=1, source_target_pairs={{0,4},{1,5},{2,6},{3,7},{4,0},{5,1},{6,2},{7,3},{8,12},{9,13},{10,... | collective-permute-start | bytes 933896 | tf_op jit(solution)/shard_map/ppermute | solution.py:548
  33.3 30.4 %collective-permute-start.2 = (bf16[64,2432]{1,0:T(8,128)(2,1)S(1)}, bf16[64,2432]{1,0:T(8,128)(2,1)}, u32[]{:S(2)}, u32[]{:S(2)}) collective-permute-start(bf16[64,2432]{1,0:T(8,128)(2,1)S(1)} %collective-permute-done), channel_id=1, source_target_pairs={{0,1},{1,0},{2,3},{3,2},{4,5},{5,4},{6,7},{7,6},{8,9},{9,8},{10,11... | collective-permute-start | bytes 933896 | tf_op jit(solution)/shard_map/ppermute | solution.py:560
  34.8 254.5 %reduce-scatter.2.cloned.1.call-start = ((), (), s32[]{:S(2)}) async-start(), calls=%async_computation.1 | async-start | bytes 4718592 | tf_op jit(solution)/shard_map/reduce_scatter | solution.py:660
  38.9 27.3 %collective-permute-start.4 = (bf16[64,2432]{1,0:T(8,128)(2,1)S(1)}, bf16[64,2432]{1,0:T(8,128)(2,1)S(1)}, u32[]{:S(2)}, u32[]{:S(2)}) collective-permute-start(bf16[64,2432]{1,0:T(8,128)(2,1)S(1)} %collective-permute-done.3), channel_id=1, source_target_pairs={{0,1},{1,0},{2,3},{3,2},{4,5},{5,4},{6,7},{7,6},{8,9},{9,8},{10,11... | collective-permute-start | bytes 933896 | tf_op jit(solution)/shard_map/ppermute | solution.py:560
  112.6 7.5 %collective-permute-start.12 = (bf16[8,256,1024]{2,1,0:T(8,128)(2,1)}, bf16[8,256,1024]{2,1,0:T(8,128)(2,1)}, u32[]{:S(2)}, u32[]{:S(2)}) collective-permute-start(bf16[8,256,1024]{2,1,0:T(8,128)(2,1)} %bitcast.154), channel_id=1, source_target_pairs={{0,8},{8,0},{16,24},{24,16},{1,9},{9,1},{17,25},{25,17},{2,10},{10... | collective-permute-start | bytes 12582920 | tf_op jit(solution)/shard_map/ppermute | solution.py:515
  150.2 11.5 %collective-permute-start.13 = (bf16[8,64,2048]{2,1,0:T(8,128)(2,1)}, bf16[8,64,2048]{2,1,0:T(8,128)(2,1)}, u32[]{:S(2)}, u32[]{:S(2)}) collective-permute-start(bf16[8,64,2048]{2,1,0:T(8,128)(2,1)} %dynamic-slice_bitcast_fusion.3), channel_id=1, source_target_pairs={{0,8},{8,0},{16,24},{24,16},{1,9},{9,1},{17,25},{25,17},{2,10},{10... | collective-permute-start | bytes 6291464 | tf_op jit(solution)/shard_map/ppermute | solution.py:515
  245.7 43.6 %collective-permute-start.16 = (bf16[4,64,1280]{2,1,0:T(8,128)(2,1)}, bf16[4,64,1280]{2,1,0:T(8,128)(2,1)S(1)}, u32[]{:S(2)}, u32[]{:S(2)}) collective-permute-start(bf16[4,64,1280]{2,1,0:T(8,128)(2,1)} %get-tuple-element.145), channel_id=1, source_target_pairs={{0,1},{1,0},{2,3},{3,2},{4,5},{5,4},{6,7},{7,6},{8,9},{9,8},{10,11... | collective-permute-start | bytes 1966088 | tf_op jit(solution)/shard_map/ppermute | solution.py:580
  246.4 8.7 %collective-permute-start.20 = (f32[8,1708]{1,0:T(8,128)S(1)}, f32[8,1708]{1,0:T(8,128)S(1)}, u32[]{:S(2)}, u32[]{:S(2)}) collective-permute-start(f32[8,1708]{1,0:T(8,128)S(1)} %concatenate.45), channel_id=1, source_target_pairs={{0,8},{8,0},{16,24},{24,16},{1,9},{9,1},{17,25},{25,17},{2,10},{10... | collective-permute-start | bytes 163976 | tf_op jit(solution)/shard_map/ppermute | solution.py:515
  247.4 32.4 %collective-permute-start.17 = (bf16[2,64,1152]{2,1,0:T(8,128)(2,1)}, bf16[2,64,1152]{2,1,0:T(8,128)(2,1)S(1)}, u32[]{:S(2)}, u32[]{:S(2)}) collective-permute-start(bf16[2,64,1152]{2,1,0:T(8,128)(2,1)} %get-tuple-element.149), channel_id=1, source_target_pairs={{0,2},{1,3},{2,4},{3,5},{4,6},{5,7},{6,0},{7,1},{8,10},{9,11},{10,... | collective-permute-start | bytes 884744 | tf_op jit(solution)/shard_map/ppermute | solution.py:574
  251.4 28.4 %collective-permute-start.18 = (bf16[2,64,1152]{2,1,0:T(8,128)(2,1)}, bf16[2,64,1152]{2,1,0:T(8,128)(2,1)}, u32[]{:S(2)}, u32[]{:S(2)}) collective-permute-start(bf16[2,64,1152]{2,1,0:T(8,128)(2,1)} %get-tuple-element.148), channel_id=1, source_target_pairs={{0,6},{1,7},{2,0},{3,1},{4,2},{5,3},{6,4},{7,5},{8,14},{9,15},{10,... | collective-permute-start | bytes 884744 | tf_op jit(solution)/shard_map/ppermute | solution.py:574
  254.5 34.8 %collective-permute-start.19 = (bf16[2,64,1152]{2,1,0:T(8,128)(2,1)S(1)}, bf16[2,64,1152]{2,1,0:T(8,128)(2,1)}, u32[]{:S(2)}, u32[]{:S(2)}) collective-permute-start(bf16[2,64,1152]{2,1,0:T(8,128)(2,1)S(1)} %get-tuple-element.147), channel_id=1, source_target_pairs={{0,4},{1,5},{2,6},{3,7},{4,0},{5,1},{6,2},{7,3},{8,12},{9,13},{10,... | collective-permute-start | bytes 884744 | tf_op jit(solution)/shard_map/ppermute | solution.py:574
  255.2 24.6 %collective-permute-start.21 = (f32[4,1708]{1,0:T(4,128)S(1)}, f32[4,1708]{1,0:T(4,128)S(1)}, u32[]{:S(2)}, u32[]{:S(2)}) collective-permute-start(f32[4,1708]{1,0:T(4,128)S(1)} %bitcast.178), channel_id=1, source_target_pairs={{0,1},{1,0},{2,3},{3,2},{4,5},{5,4},{6,7},{7,6},{8,9},{9,8},{10,11... | collective-permute-start | bytes 81992 | tf_op jit(solution)/shard_map/ppermute | solution.py:580
  289.4 7.4 %collective-permute-start.27 = (f32[1708]{0:T(1024)S(1)}, f32[1708]{0:T(1024)S(1)}, u32[]{:S(2)}, u32[]{:S(2)}) collective-permute-start(f32[1708]{0:T(1024)S(1)} %get-tuple-element.131), channel_id=1, source_target_pairs={{0,2},{1,3},{2,4},{3,5},{4,6},{5,7},{6,0},{7,1},{8,10},{9,11},{10,... | collective-permute-start | bytes 20504 | tf_op jit(solution)/shard_map/ppermute | solution.py:574
  289.5 10.7 %collective-permute-start.28 = (f32[1708]{0:T(1024)S(1)}, f32[1708]{0:T(1024)S(1)}, u32[]{:S(2)}, u32[]{:S(2)}) collective-permute-start(f32[1708]{0:T(1024)S(1)} %get-tuple-element.130), channel_id=1, source_target_pairs={{0,6},{1,7},{2,0},{3,1},{4,2},{5,3},{6,4},{7,5},{8,14},{9,15},{10,... | collective-permute-start | bytes 20504 | tf_op jit(solution)/shard_map/ppermute | solution.py:574
  293.3 8.0 %collective-permute-start.29 = (f32[1708]{0:T(1024)S(1)}, f32[1708]{0:T(1024)S(1)}, u32[]{:S(2)}, u32[]{:S(2)}) collective-permute-start(f32[1708]{0:T(1024)S(1)} %get-tuple-element.129), channel_id=1, source_target_pairs={{0,4},{1,5},{2,6},{3,7},{4,0},{5,1},{6,2},{7,3},{8,12},{9,13},{10,... | collective-permute-start | bytes 20504 | tf_op jit(solution)/shard_map/ppermute | solution.py:574
  293.5 13.0 %collective-permute-start.22 = (bf16[64,1280]{1,0:T(8,128)(2,1)S(1)}, bf16[64,1280]{1,0:T(8,128)(2,1)S(1)}, u32[]{:S(2)}, u32[]{:S(2)}) collective-permute-start(bf16[64,1280]{1,0:T(8,128)(2,1)S(1)} %get-tuple-element.159), channel_id=1, source_target_pairs={{0,2},{1,3},{2,4},{3,5},{4,6},{5,7},{6,0},{7,1},{8,10},{9,11},{10,... | collective-permute-start | bytes 491528 | tf_op jit(solution)/shard_map/ppermute | solution.py:574
  294.2 17.5 %collective-permute-start.26 = (bf16[256,1024]{1,0:T(8,128)(2,1)S(1)}, bf16[256,1024]{1,0:T(8,128)(2,1)S(1)}, u32[]{:S(2)}, u32[]{:S(2)}) collective-permute-start(bf16[256,1024]{1,0:T(8,128)(2,1)S(1)} %bitcast.165), channel_id=1, source_target_pairs={{0,16},{8,24},{16,0},{24,8},{1,17},{9,25},{17,1},{25,9},{2,18},{10... | collective-permute-start | bytes 1572872 | tf_op jit(solution)/shard_map/ppermute | solution.py:687
  296.8 9.7 %collective-permute-start.23 = (bf16[64,1280]{1,0:T(8,128)(2,1)S(1)}, bf16[64,1280]{1,0:T(8,128)(2,1)S(1)}, u32[]{:S(2)}, u32[]{:S(2)}) collective-permute-start(bf16[64,1280]{1,0:T(8,128)(2,1)S(1)} %get-tuple-element.158), channel_id=1, source_target_pairs={{0,6},{1,7},{2,0},{3,1},{4,2},{5,3},{6,4},{7,5},{8,14},{9,15},{10,... | collective-permute-start | bytes 491528 | tf_op jit(solution)/shard_map/ppermute | solution.py:574
  300.2 11.5 %collective-permute-start.24 = (bf16[64,1280]{1,0:T(8,128)(2,1)S(1)}, bf16[64,1280]{1,0:T(8,128)(2,1)S(1)}, u32[]{:S(2)}, u32[]{:S(2)}) collective-permute-start(bf16[64,1280]{1,0:T(8,128)(2,1)S(1)} %get-tuple-element.157), channel_id=1, source_target_pairs={{0,4},{1,5},{2,6},{3,7},{4,0},{5,1},{6,2},{7,3},{8,12},{9,13},{10,... | collective-permute-start | bytes 491528 | tf_op jit(solution)/shard_map/ppermute | solution.py:574
  313.4 8.1 %collective-permute-start.31 = (bf16[64,2432]{1,0:T(8,128)(2,1)S(1)}, bf16[64,2432]{1,0:T(8,128)(2,1)S(1)}, u32[]{:S(2)}, u32[]{:S(2)}) collective-permute-start(bf16[64,2432]{1,0:T(8,128)(2,1)S(1)} %pad_maximum_fusion.6), channel_id=1, source_target_pairs={{0,16},{8,24},{16,0},{24,8},{1,17},{9,25},{17,1},{25,9},{2,18},{10... | collective-permute-start | bytes 933896 | tf_op jit(solution)/shard_map/ppermute | solution.py:536
  (55 other events, 726.1 us)
Sparse Core Ops, SparseCore 0:
  34.9 77.6 all-gather.2
  171.8 103.7 reduce-scatter.1
